TPU v7x, 1024 devices: a whole 4x4x32 slice. The times are simulated.
1024 devices in a mesh: node: 64 (over z, core), local: 16 (over x, y).
Axes of the slice: x: 4, y: 4, z: 32, core: 2. Of those that a mesh axis runs over, the one named last changes fastest.
Arguments:
- out_grad: bfloat16 [8192, 4, 1792], P('node', None, 'local'), may hold values from -4 to 4
- combine: float32 [8192, 8], P('node'), may hold values from 0.1 to 1
- expert_ids: int32 [8192, 8], P('node'), may hold values from 0 to 255, as said below
- slot_ids: int32 [8192, 8], P('node'), may hold values from 0 to 3, as said below
- kept_mask: int32 [8192, 8], P('node'), may hold values from 0 to 1, as said below
- saved_inputs: bfloat16 [64, 4, 114688], P(None, None, 'node'), may hold values from -6 to 6
- gate_weight: bfloat16 [114688, 2048], P('node', 'local'), may hold values from -0.0625 to 0.0625
- up_weight: bfloat16 [114688, 2048], P('node', 'local'), may hold values from -0.0625 to 0.0625
- down_weight_t: bfloat16 [114688, 2048], P('node', 'local'), may hold values from -0.125 to 0.125
Outputs:
- token_grad: bfloat16 [8192, 4, 1792], P('node', None, 'local')
- grad_gate: bfloat16 [114688, 2048], P('node', 'local')
- grad_up: bfloat16 [114688, 2048], P('node', 'local')
- grad_down_t: bfloat16 [114688, 2048], P('node', 'local')
Inputs may be any that keep to these rules, and one draw needn't show every extreme that they name: `expert_ids`: each token names 8 distinct experts, all in at most 4 of the 8 groups of consecutive experts. `slot_ids`: for one node's tokens and one slab expert the kept choices take the slots 0, 1, 2, ... in token order, each once; 0 where kept_mask is 0. `kept_mask`: 1 exactly where the expert is below 16 and fewer than 4 earlier tokens of the same node chose it.
All inputs are finite; a program needn't handle non-finite values.
Results may differ from a plain program's by a relative error of at most 0.025.
Values may be sent and summed in bfloat16 or wider, within the bound.
No kernel may reach another device: no remote copies, remote signals or barrier semaphores. Data moves between devices by JAX's collectives and lax.ppermute only.
A program may use at most 32 MiB of HBM per device.

v0:
```python
import jax
import jax.numpy as jnp
from jax import lax
from jax.sharding import PartitionSpec as P


def swapped(block, axis, bit):
    count = lax.axis_size(axis)
    route = []
    for low in range(count):
        high = low | 1 << bit
        if high != low and high < count:
            route += [(low, high), (high, low)]
    return lax.ppermute(block, axis, route)


def activation_step(pre_gate, pre_up, grad_act):
    gate_sig = jax.nn.sigmoid(pre_gate)
    silu_gate = pre_gate * gate_sig
    activated = (silu_gate * pre_up).astype(jnp.bfloat16)
    grad_pre_gate = (grad_act * pre_up * gate_sig * (1.0 + pre_gate * (1.0 - gate_sig))).astype(
        jnp.bfloat16
    )
    grad_pre_up = (grad_act * silu_gate).astype(jnp.bfloat16)
    return (activated, grad_pre_gate, grad_pre_up)


def per_device(
    out_grad,
    combine,
    expert_ids,
    slot_ids,
    kept_mask,
    saved_inputs,
    gate_weight,
    up_weight,
    down_weight_t,
):
    node_count = lax.axis_size("node")
    slab_count = node_count // 4
    capacity = saved_inputs.shape[1]
    quarter = saved_inputs.shape[2]
    token_count = out_grad.shape[0]
    column_piece = out_grad.shape[2]
    hidden = gate_weight.shape[1]
    row_count = node_count * capacity
    targets = jnp.arange(slab_count * capacity, dtype=jnp.int32)
    route_code = expert_ids * capacity + slot_ids
    matched = (route_code[:, :, None] == targets[None, None, :]) & (kept_mask[:, :, None] == 1)
    placed = jnp.sum(jnp.where(matched, 1.0, 0.0), axis=1).astype(jnp.bfloat16)
    slot_weight = jnp.sum(jnp.sum(jnp.where(matched, combine[:, :, None], 0.0), axis=1), axis=0)
    grad_rows = out_grad.reshape(token_count, 4 * column_piece)
    contract_rows = (((0,), (0,)), ((), ()))
    selected = lax.dot_general(placed, grad_rows, contract_rows, preferred_element_type=jnp.float32)
    outgoing = selected * slot_weight[:, None]
    outgoing = outgoing.reshape(slab_count, capacity, 4, column_piece).transpose(0, 2, 1, 3)
    outgoing = outgoing.reshape(node_count, capacity, column_piece).astype(jnp.bfloat16)
    inputs = saved_inputs.reshape(row_count, quarter)
    arrived = lax.all_to_all(outgoing, "node", split_axis=0, concat_axis=0, tiled=True)
    grads_in = lax.all_gather(arrived, "local", axis=2, tiled=True).reshape(row_count, quarter)
    down_part = jnp.dot(grads_in, down_weight_t, preferred_element_type=jnp.float32)
    joined = jnp.concatenate(
        [
            jnp.dot(inputs, gate_weight, preferred_element_type=jnp.float32),
            jnp.dot(inputs, up_weight, preferred_element_type=jnp.float32),
            down_part,
        ],
        axis=1,
    )
    for swap_bit in range(2):
        joined = joined + swapped(joined.astype(jnp.bfloat16), "node", swap_bit).astype(
            joined.dtype
        )
    activated, grad_pre_gate, grad_pre_up = activation_step(
        joined[:, :hidden], joined[:, hidden : 2 * hidden], joined[:, 2 * hidden :]
    )
    both_grads = jnp.concatenate([grad_pre_gate, grad_pre_up], axis=1)
    weight_in = lax.dot_general(
        inputs, both_grads, contract_rows, preferred_element_type=jnp.float32
    )
    grad_gate = weight_in[:, :hidden].astype(jnp.bfloat16)
    grad_up = weight_in[:, hidden:].astype(jnp.bfloat16)
    grad_down_t = lax.dot_general(
        grads_in, activated, contract_rows, preferred_element_type=jnp.float32
    ).astype(jnp.bfloat16)
    stacked_weight = jnp.concatenate([gate_weight, up_weight], axis=1)
    partial_value = lax.dot_general(
        both_grads, stacked_weight, (((1,), (1,)), ((), ())), preferred_element_type=jnp.float32
    )
    partial_value = lax.optimization_barrier(partial_value.astype(jnp.bfloat16))
    summed = lax.psum_scatter(
        partial_value.astype(jnp.float32)
        .reshape(node_count, capacity, quarter)
        .astype(jnp.bfloat16),
        "local",
        scatter_dimension=2,
        tiled=True,
    )
    returned = lax.all_to_all(summed, "node", split_axis=0, concat_axis=0, tiled=True)
    returned_rows = returned.reshape(slab_count, 4, capacity, column_piece).transpose(0, 2, 1, 3)
    returned_rows = returned_rows.reshape(slab_count * capacity, 4 * column_piece)
    token_grad = jnp.dot(placed, returned_rows, preferred_element_type=jnp.float32)
    token_grad = token_grad.reshape(token_count, 4, column_piece).astype(jnp.bfloat16)
    return (token_grad, grad_gate, grad_up, grad_down_t)


def solution(mesh):
    placed = (
        P("node", None, "local"),
        P("node", None),
        P("node", None),
        P("node", None),
        P("node", None),
        P(None, None, "node"),
        P("node", "local"),
        P("node", "local"),
        P("node", "local"),
    )
    return jax.shard_map(
        per_device,
        mesh=mesh,
        in_specs=placed,
        out_specs=(
            P("node", None, "local"),
            P("node", "local"),
            P("node", "local"),
            P("node", "local"),
        ),
        check_vma=False,
    )
```

profile of v0, /device:TPU:2, one launch (start us, length us, event | category | flops | bytes accessed | tf_op | source)
XLA Modules:
  0.0 267.7 jit_solution(4068648582158449782)
XLA Ops:
  7.2 0.0 copy-start
  7.2 0.0 copy-start.4
  7.2 0.8 broadcast_compare_fusion
  8.0 0.7 multiply_add_fusion
  8.7 0.9 select_reduce_fusion.1
  9.5 1.1 fusion.1
  10.6 0.1 convert_element_type.54
  10.8 0.0 copy-start.6
  10.8 0.7 copy.50
  11.5 29.4 %all-to-all-start = ((bf16[64,4,112]{2,1,0:T(4,128)(2,1)}), bf16[64,4,112]{2,1,0:T(4,128)(2,1)S(1)}, u32[]{:S(2)}, u32[]{:S(2)}) async-start(bf16[64,4,112]{2,1,0:T(4,128)(2,1)} %copy.50), calls=%async_computation | async-start | bytes 131072 | tf_op jit(solution)/shard_map/all_to_all | solution.py:59
  40.8 0.0 reduce-scatter.4.cloned.1.call-start
  40.9 1.7 reshape.36
  42.5 0.0 copy-done.4
  42.5 0.5 fusion.19
  43.0 0.0 copy-done.6
  43.0 0.5 fusion.18
  43.5 23.7 %all-to-all-done = bf16[64,4,112]{2,1,0:T(4,128)(2,1)S(1)} async-done(((bf16[64,4,112]{2,1,0:T(4,128)(2,1)}), bf16[64,4,112]{2,1,0:T(4,128)(2,1)S(1)}, u32[]{:S(2)}, u32[]{:S(2)}) %all-to-all-start) | async-done | bytes 57376 | tf_op jit(solution)/shard_map/all_to_all | solution.py:59
  67.2 0.8 copy.51
  67.9 26.1 %all_gather.3 = bf16[64,4,1792]{0,1,2:T(4,128)(2,1)S(1)} all-gather(bf16[64,4,112]{0,1,2:T(4,128)(2,1)} %copy.51), channel_id=1, replica_groups=mesh['node'=64,'local'=16] {'local'}, dimensions={2}, use_global_device_ids=true | all-gather | bytes 974848 | tf_op jit(solution)/shard_map/all_gather | solution.py:60
  94.0 3.2 %copy.52 = bf16[64,4,1792]{2,1,0:T(4,128)(2,1)} copy(bf16[64,4,1792]{0,1,2:T(4,128)(2,1)S(1)} %all_gather.3) | data formatting | bytes 1835008 | tf_op jit(solution)/shard_map/all_gather | solution.py:60
  97.2 1.6 reshape.38
  98.9 0.0 copy-done
  98.9 0.0 copy-start.1
  98.9 0.5 fusion.20
  99.3 0.0 copy-start.5
  99.4 0.0 copy-start.7
  99.4 2.1 collective-permute-start
  101.5 1.4 collective-permute-done
  102.9 2.9 %collective-permute-start.1 = (bf16[256,384]{0,1:T(8,128)(2,1)S(1)}, bf16[256,384]{0,1:T(8,128)(2,1)S(1)}, u32[]{:S(2)}, u32[]{:S(2)}) collective-permute-start(bf16[256,384]{0,1:T(8,128)(2,1)S(1)} %fusion.7), channel_id=1, source_target_pairs={{0,32},{32,0},{16,48},{48,16},{64,96},{96,64},{80,112},{112,80},{1... | collective-permute-start | bytes 589832 | tf_op jit(solution)/shard_map/ppermute | solution.py:14
  105.8 5.9 %collective-permute-done.1 = bf16[256,384]{0,1:T(8,128)(2,1)S(1)} collective-permute-done((bf16[256,384]{0,1:T(8,128)(2,1)S(1)}, bf16[256,384]{0,1:T(8,128)(2,1)S(1)}, u32[]{:S(2)}, u32[]{:S(2)}) %collective-permute-start.1) | collective-permute-done | bytes 196640 | tf_op jit(solution)/shard_map/ppermute | solution.py:14
  111.8 0.1 convert_add_fusion
  111.8 0.0 copy-done.1
  111.8 0.0 copy-start.3
  111.8 0.1 multiply_convert_fusion.2
  111.9 0.0 copy-done.5
  111.9 0.0 copy-done.7
  111.9 0.5 convolution_convert_fusion.1
  112.4 0.2 copy-done.3
  112.6 1.2 convert_element_type.64
  113.8 3.7 %copy.60 = bf16[64,4,1792]{0,1,2:T(4,128)(2,1)S(1)} copy(bf16[64,4,1792]{2,1,0:T(4,128)(2,1)} %convert_element_type.64) | data formatting | bytes 1835008
  117.5 1.9 reshape.42
  119.5 0.0 reduce-scatter.4.cloned.1.call-update
  119.5 0.4 fusion
  119.9 88.4 %reduce-scatter.4.cloned.1.call-done = bf16[112,256]{1,0:T(8,128)(2,1)} async-done(((bf16[1792,256]{1,0:T(8,128)(2,1)}), bf16[112,256]{1,0:T(8,128)(2,1)}) %reduce-scatter.4.cloned.1.call-update) | async-done | bytes 57360
  208.4 0.9 reshape.43
  209.3 0.7 copy.54
  210.0 23.3 %all-to-all-start.1 = ((bf16[64,4,112]{2,1,0:T(4,128)(2,1)}), bf16[64,4,112]{2,1,0:T(4,128)(2,1)S(1)}, u32[]{:S(2)}, u32[]{:S(2)}) async-start(bf16[64,4,112]{2,1,0:T(4,128)(2,1)} %copy.54), calls=%async_computation.1 | async-start | bytes 131072 | tf_op jit(solution)/shard_map/all_to_all | solution.py:99
  233.3 0.0 copy-start.2
  233.3 0.1 fusion.17
  233.4 1.0 copy.59
  234.4 1.0 copy.58
  235.4 0.0 copy-done.2
  235.4 2.2 convolution_convert_fusion.2
  237.5 22.1 %all-to-all-done.1 = bf16[64,4,112]{2,1,0:T(4,128)(2,1)S(1)} async-done(((bf16[64,4,112]{2,1,0:T(4,128)(2,1)}), bf16[64,4,112]{2,1,0:T(4,128)(2,1)S(1)}, u32[]{:S(2)}, u32[]{:S(2)}) %all-to-all-start.1) | async-done | bytes 57376 | tf_op jit(solution)/shard_map/all_to_all | solution.py:99
  259.7 0.1 reshape.40
  259.8 0.1 dot_general.36
  259.9 0.9 convolution_convert_fusion.3
  (5 shorter events, 0.1 us)
Async XLA Ops:
  7.2 91.7 %copy-start = (bf16[1792,128]{1,0:T(8,128)(2,1)S(1)}, bf16[1792,128]{1,0:T(8,128)(2,1)}, u32[]{:S(2)}) copy-start(bf16[1792,128]{1,0:T(8,128)(2,1)} %param.17) | copy-start | bytes 1376260
  7.2 35.3 %copy-start.4 = (bf16[1792,128]{1,0:T(8,128)(2,1)S(1)}, bf16[1792,128]{1,0:T(8,128)(2,1)}, u32[]{:S(2)}) copy-start(bf16[1792,128]{1,0:T(8,128)(2,1)} %param.16) | copy-start | bytes 1376260
  10.8 32.2 %copy-start.6 = (bf16[1792,128]{1,0:T(8,128)(2,1)S(1)}, bf16[1792,128]{1,0:T(8,128)(2,1)}, u32[]{:S(2)}) copy-start(bf16[1792,128]{1,0:T(8,128)(2,1)} %param.15) | copy-start | bytes 1376260
  11.5 55.7 %all-to-all-start = ((bf16[64,4,112]{2,1,0:T(4,128)(2,1)}), bf16[64,4,112]{2,1,0:T(4,128)(2,1)S(1)}, u32[]{:S(2)}, u32[]{:S(2)}) async-start(bf16[64,4,112]{2,1,0:T(4,128)(2,1)} %copy.50), calls=%async_computation | async-start | bytes 131072 | tf_op jit(solution)/shard_map/all_to_all | solution.py:59
  40.8 167.5 %reduce-scatter.4.cloned.1.call-start = ((), (), s32[]{:S(2)}) async-start(), calls=%async_computation.3 | async-start | bytes 974848
  98.9 12.9 %copy-start.1 = (bf16[256,1792]{1,0:T(8,128)(2,1)}, bf16[256,1792]{1,0:T(8,128)(2,1)S(1)}, u32[]{:S(2)}) copy-start(bf16[256,1792]{1,0:T(8,128)(2,1)S(1)} %reshape.38) | copy-start | bytes 2752516
  99.3 12.6 %copy-start.5 = (bf16[1792,128]{1,0:T(8,128)(2,1)S(1)}, bf16[1792,128]{1,0:T(8,128)(2,1)}, u32[]{:S(2)}) copy-start(bf16[1792,128]{1,0:T(8,128)(2,1)} %param.16) | copy-start | bytes 1376260
  99.4 12.6 %copy-start.7 = (bf16[1792,128]{1,0:T(8,128)(2,1)S(1)}, bf16[1792,128]{1,0:T(8,128)(2,1)}, u32[]{:S(2)}) copy-start(bf16[1792,128]{1,0:T(8,128)(2,1)} %param.15) | copy-start | bytes 1376260
  99.4 3.5 %collective-permute-start = (bf16[256,384]{0,1:T(8,128)(2,1)S(1)}, bf16[256,384]{0,1:T(8,128)(2,1)S(1)}, u32[]{:S(2)}, u32[]{:S(2)}) collective-permute-start(bf16[256,384]{0,1:T(8,128)(2,1)S(1)} %fusion.5), channel_id=1, source_target_pairs={{0,16},{16,0},{32,48},{48,32},{64,80},{80,64},{96,112},{112,96},{1... | collective-permute-start | bytes 589832 | tf_op jit(solution)/shard_map/ppermute | solution.py:14
  102.9 8.8 %collective-permute-start.1 = (bf16[256,384]{0,1:T(8,128)(2,1)S(1)}, bf16[256,384]{0,1:T(8,128)(2,1)S(1)}, u32[]{:S(2)}, u32[]{:S(2)}) collective-permute-start(bf16[256,384]{0,1:T(8,128)(2,1)S(1)} %fusion.7), channel_id=1, source_target_pairs={{0,32},{32,0},{16,48},{48,16},{64,96},{96,64},{80,112},{112,80},{1... | collective-permute-start | bytes 589832 | tf_op jit(solution)/shard_map/ppermute | solution.py:14
  111.8 0.8 copy-start.3
  210.0 49.6 %all-to-all-start.1 = ((bf16[64,4,112]{2,1,0:T(4,128)(2,1)}), bf16[64,4,112]{2,1,0:T(4,128)(2,1)S(1)}, u32[]{:S(2)}, u32[]{:S(2)}) async-start(bf16[64,4,112]{2,1,0:T(4,128)(2,1)} %copy.54), calls=%async_computation.1 | async-start | bytes 131072 | tf_op jit(solution)/shard_map/all_to_all | solution.py:99
  233.3 2.0 copy-start.2
Sparse Core Ops, SparseCore 0:
  119.6 88.6 reduce-scatter.3
where the time goes:
time: 268 us
  waiting for transfers between devices  142 us (53%)
  starting transfers between devices  57.6 us (21%)
  blocking collectives  26.1 us (10%)
  local copies, waits for them, and re-layouts  19.1 us (7%)
  between operations  14.3 us (5%)
  matrix products  6.41 us (2%)
    unnamed x2, waiting for transfers between devices  88.4 us
    all_to_all x1, starting transfers between devices, per_device(): lax.all_to_all(outgoing, 'node', split_axis=0, concat_axis=0, tiled=True)  29.4 us
    all_gather x1, blocking collectives, per_device(): lax.all_gather(arrived, 'local', axis=2, tiled=True)  26.1 us
    all_to_all x1, waiting for transfers between devices, per_device(): lax.all_to_all(outgoing, 'node', split_axis=0, concat_axis=0, tiled=True)  23.7 us
    all_to_all x1, starting transfers between devices, per_device(): lax.all_to_all(summed, 'node', split_axis=0, concat_axis=0, tiled=True)  23.3 us
    all_to_all x1, waiting for transfers between devices, per_device(): lax.all_to_all(summed, 'node', split_axis=0, concat_axis=0, tiled=True)  22.1 us
    unnamed x21, local copies, waits for them, and re-layouts  8.83 us
    ppermute x2, waiting for transfers between devices, swapped(): return lax.ppermute(block, axis, route)  7.34 us
  transfers between devices with their start and end apart: 5, of which 5 were waited for; matrix products, arithmetic and copies ran while one was open for 3% of the time, Pallas kernels for 0%

commit v1 on v0

v1 whole, which is shorter than its diff:
```python
import jax
import jax.numpy as jnp
from jax import lax
from jax.sharding import PartitionSpec as P


def swapped(block, axis, bit):
    count = lax.axis_size(axis)
    route = []
    for low in range(count):
        high = low | 1 << bit
        if high != low and high < count:
            route += [(low, high), (high, low)]
    return lax.ppermute(block, axis, route)


def quarter_sum(part):
    for swap_bit in range(2):
        part = part + swapped(part.astype(jnp.bfloat16), "node", swap_bit).astype(jnp.float32)
    return part


def dot(lhs, rhs, lhs_dim, rhs_dim):
    return lax.dot_general(
        lhs, rhs, (((lhs_dim,), (rhs_dim,)), ((), ())), preferred_element_type=jnp.float32
    )


def per_device(
    out_grad,
    combine,
    expert_ids,
    slot_ids,
    kept_mask,
    saved_inputs,
    gate_weight,
    up_weight,
    down_weight_t,
):
    node_count = lax.axis_size("node")
    local_count = lax.axis_size("local")
    slab_count = node_count // 4
    capacity = saved_inputs.shape[1]
    quarter = saved_inputs.shape[2]
    token_count = out_grad.shape[0]
    piece = out_grad.shape[2]
    hidden = gate_weight.shape[1]
    row_count = node_count * capacity

    targets = jnp.arange(slab_count * capacity, dtype=jnp.int32)
    route_code = expert_ids * capacity + slot_ids
    matched = (route_code[:, :, None] == targets[None, None, :]) & (kept_mask[:, :, None] == 1)
    placed = jnp.sum(jnp.where(matched, 1.0, 0.0), axis=1).astype(jnp.bfloat16)
    slot_weight = jnp.sum(jnp.sum(jnp.where(matched, combine[:, :, None], 0.0), axis=1), axis=0)
    grad_rows = out_grad.reshape(token_count, 4 * piece)
    selected = dot(placed, grad_rows, 0, 0)
    outgoing = selected * slot_weight[:, None]
    outgoing = outgoing.reshape(slab_count, capacity, 4, piece).transpose(0, 2, 1, 3)
    outgoing = outgoing.reshape(node_count, capacity, piece).astype(jnp.bfloat16)
    arrived = lax.all_to_all(outgoing, "node", split_axis=0, concat_axis=0, tiled=True)

    inputs = saved_inputs.reshape(row_count, quarter)
    pre_gate_up = quarter_sum(
        jnp.concatenate([dot(inputs, gate_weight, 1, 0), dot(inputs, up_weight, 1, 0)], axis=1)
    )

    arrived, pre_gate_up = lax.optimization_barrier((arrived, pre_gate_up))
    turned = arrived.reshape(row_count, piece).T
    copies = lax.optimization_barrier(
        jnp.broadcast_to(turned[None], (local_count, piece, row_count))
    )
    grads_in = lax.all_to_all(copies, "local", split_axis=0, concat_axis=0, tiled=True)
    grads_in = grads_in.reshape(quarter, row_count)
    grad_act = quarter_sum(dot(grads_in, down_weight_t, 0, 0))

    pre_gate = pre_gate_up[:, :hidden]
    pre_up = pre_gate_up[:, hidden:]
    gate_sig = jax.nn.sigmoid(pre_gate)
    silu_gate = pre_gate * gate_sig
    activated = (silu_gate * pre_up).astype(jnp.bfloat16)
    gate_slope = pre_up * gate_sig * (1.0 + pre_gate * (1.0 - gate_sig))
    grad_pre_gate = (grad_act * gate_slope).astype(jnp.bfloat16)
    grad_pre_up = (grad_act * silu_gate).astype(jnp.bfloat16)

    partial_value = dot(gate_weight, grad_pre_gate, 1, 1) + dot(up_weight, grad_pre_up, 1, 1)
    partial_value = partial_value.astype(jnp.bfloat16).reshape(local_count, piece, row_count)
    pieces = lax.all_to_all(partial_value, "local", split_axis=0, concat_axis=0, tiled=True)
    summed = jnp.sum(pieces.astype(jnp.float32), axis=0).astype(jnp.bfloat16)
    summed = summed.T.reshape(node_count, capacity, piece)
    returned = lax.all_to_all(summed, "node", split_axis=0, concat_axis=0, tiled=True)

    grad_gate = dot(inputs, grad_pre_gate, 0, 0).astype(jnp.bfloat16)
    grad_up = dot(inputs, grad_pre_up, 0, 0).astype(jnp.bfloat16)
    grad_down_t = dot(grads_in, activated, 1, 0).astype(jnp.bfloat16)

    returned_rows = returned.reshape(slab_count, 4, capacity, piece).transpose(0, 2, 1, 3)
    returned_rows = returned_rows.reshape(slab_count * capacity, 4 * piece)
    token_grad = dot(placed, returned_rows, 1, 0)
    token_grad = token_grad.reshape(token_count, 4, piece).astype(jnp.bfloat16)
    return (token_grad, grad_gate, grad_up, grad_down_t)


def solution(mesh):
    placed = (
        P("node", None, "local"),
        P("node", None),
        P("node", None),
        P("node", None),
        P("node", None),
        P(None, None, "node"),
        P("node", "local"),
        P("node", "local"),
        P("node", "local"),
    )
    return jax.shard_map(
        per_device,
        mesh=mesh,
        in_specs=placed,
        out_specs=(
            P("node", None, "local"),
            P("node", "local"),
            P("node", "local"),
            P("node", "local"),
        ),
        check_vma=False,
    )
```

time: 268 us -> 150 us (0.56)
  the two profiles are of different devices: /device:TPU:2 before, /device:TPU:1 now
where the time goes in v1:
time: 150 us
  waiting for transfers between devices  59.4 us (40%)
  starting transfers between devices  56.5 us (38%)
  blocking collectives  19.5 us (13%)
  local copies, waits for them, and re-layouts  7.15 us (5%)
  matrix products  5.81 us (4%)
    ppermute x4, starting transfers between devices, swapped(): return lax.ppermute(block, axis, route)  27.1 us
    all_to_all x1, waiting for transfers between devices, per_device(): lax.all_to_all(summed, 'node', split_axis=0, concat_axis=0, tiled=True)  21.6 us
    all_to_all x1, blocking collectives, per_device(): lax.all_to_all(copies, 'local', split_axis=0, concat_axis=0, tiled=True)  19.5 us
    all_to_all x1, starting transfers between devices, per_device(): lax.all_to_all(outgoing, 'node', split_axis=0, concat_axis=0, tiled=True)  16.4 us
    all_to_all x1, waiting for transfers between devices, per_device(): lax.all_to_all(outgoing, 'node', split_axis=0, concat_axis=0, tiled=True)  16.3 us
    all_to_all x1, waiting for transfers between devices, per_device(): lax.all_to_all(partial_value, 'local', split_axis=0, concat_axis=0, tiled...  12.7 us
    all_to_all x1, starting transfers between devices, per_device(): lax.all_to_all(summed, 'node', split_axis=0, concat_axis=0, tiled=True)  9.46 us
    ppermute x4, waiting for transfers between devices, swapped(): return lax.ppermute(block, axis, route)  8.86 us
  transfers between devices with their start and end apart: 7, of which 6 were waited for; matrix products, arithmetic and copies ran while one was open for 4% of the time, Pallas kernels for 0%

profile of v1, /device:TPU:1, one launch (start us, length us, event | category | flops | bytes accessed | tf_op | source)
XLA Modules:
  0.0 149.9 jit_solution(6287347728838818975)
XLA Ops:
  0.6 0.0 copy-start
  0.6 0.0 copy-start.1
  0.7 1.7 %reshape.45 = bf16[256,1792]{1,0:T(8,128)(2,1)S(1)} reshape(bf16[64,4,1792]{2,1,0:T(4,128)(2,1)} %param.14) | data formatting | bytes 1835008 | tf_op jit(solution)/shard_map/reshape | solution.py:62
  2.4 0.0 copy-done
  2.4 0.0 copy-start.9
  2.4 0.0 copy-start.6
  2.4 0.0 copy-start.7
  2.4 0.0 copy-start.8
  2.5 0.0 copy-start.5
  2.5 0.5 fusion.18
  2.9 0.0 copy-done.1
  2.9 0.5 fusion.17
  3.4 16.1 %collective-permute-start = (bf16[256,256]{0,1:T(8,128)(2,1)S(1)}, bf16[256,256]{0,1:T(8,128)(2,1)S(1)}, u32[]{:S(2)}, u32[]{:S(2)}) collective-permute-start(bf16[256,256]{0,1:T(8,128)(2,1)S(1)} %fusion.6), channel_id=1, source_target_pairs={{0,16},{16,0},{32,48},{48,32},{64,80},{80,64},{96,112},{112,96},{1... | collective-permute-start | bytes 393224 | tf_op jit(solution)/shard_map/ppermute | solution.py:14
  19.5 0.0 copy-done.9
  19.5 0.0 copy-done.6
  19.5 0.0 copy-done.7
  19.5 0.0 copy-done.8
  19.6 0.2 select_reduce_fusion.1
  19.7 0.0 copy-done.5
  19.7 0.2 fusion.4
  19.9 0.1 convert_element_type.76
  20.1 0.7 copy.61
  20.7 16.4 %all-to-all-start = ((bf16[64,4,112]{2,1,0:T(4,128)(2,1)}), bf16[64,4,112]{2,1,0:T(4,128)(2,1)S(1)}, u32[]{:S(2)}, u32[]{:S(2)}) async-start(bf16[64,4,112]{2,1,0:T(4,128)(2,1)} %copy.61), calls=%async_computation | async-start | bytes 131072 | tf_op jit(solution)/shard_map/all_to_all | solution.py:60
  37.1 0.0 collective-permute-done
  37.2 0.0 copy-start.4
  37.2 3.4 %collective-permute-start.1 = (bf16[256,256]{0,1:T(8,128)(2,1)S(1)}, bf16[256,256]{0,1:T(8,128)(2,1)S(1)}, u32[]{:S(2)}, u32[]{:S(2)}) collective-permute-start(bf16[256,256]{0,1:T(8,128)(2,1)S(1)} %fusion.7), channel_id=1, source_target_pairs={{0,32},{32,0},{16,48},{48,16},{64,96},{96,64},{80,112},{112,80},{1... | collective-permute-start | bytes 393224 | tf_op jit(solution)/shard_map/ppermute | solution.py:14
  40.6 5.1 %collective-permute-done.1 = bf16[256,256]{0,1:T(8,128)(2,1)S(1)} collective-permute-done((bf16[256,256]{0,1:T(8,128)(2,1)S(1)}, bf16[256,256]{0,1:T(8,128)(2,1)S(1)}, u32[]{:S(2)}, u32[]{:S(2)}) %collective-permute-start.1) | collective-permute-done | bytes 131104 | tf_op jit(solution)/shard_map/ppermute | solution.py:14
  45.7 16.3 %all-to-all-done = bf16[64,4,112]{2,1,0:T(4,128)(2,1)S(1)} async-done(((bf16[64,4,112]{2,1,0:T(4,128)(2,1)}), bf16[64,4,112]{2,1,0:T(4,128)(2,1)S(1)}, u32[]{:S(2)}, u32[]{:S(2)}) %all-to-all-start) | async-done | bytes 57376 | tf_op jit(solution)/shard_map/all_to_all | solution.py:60
  62.1 0.1 copy.62
  62.2 0.1 broadcast_in_dim.32
  62.2 19.5 %all_to_all.20 = bf16[16,112,256]{2,1,0:T(8,128)(2,1)S(1)} all-to-all(bf16[16,112,256]{2,1,0:T(8,128)(2,1)S(1)} %broadcast_in_dim.32), channel_id=1, replica_groups=mesh['node'=64,'local'=16] {'local'}, dimensions={0} | all-to-all | bytes 1835008 | tf_op jit(solution)/shard_map/all_to_all | solution.py:72
  81.8 0.0 copy-done.4
  81.8 0.3 fusion.16
  82.1 0.0 copy-start.2
  82.1 5.5 %collective-permute-start.2 = (bf16[256,128]{0,1:T(8,128)(2,1)S(1)}, bf16[256,128]{0,1:T(8,128)(2,1)S(1)}, u32[]{:S(2)}, u32[]{:S(2)}) collective-permute-start(bf16[256,128]{0,1:T(8,128)(2,1)S(1)} %get-tuple-element.32), channel_id=1, source_target_pairs={{0,16},{16,0},{32,48},{48,32},{64,80},{80,64},{96,112},{112,96},{1... | collective-permute-start | bytes 196616 | tf_op jit(solution)/shard_map/ppermute | solution.py:14
  87.6 0.9 collective-permute-done.2
  88.5 2.1 %collective-permute-start.3 = (bf16[256,128]{0,1:T(8,128)(2,1)S(1)}, bf16[256,128]{0,1:T(8,128)(2,1)S(1)}, u32[]{:S(2)}, u32[]{:S(2)}) collective-permute-start(bf16[256,128]{0,1:T(8,128)(2,1)S(1)} %fusion.9), channel_id=1, source_target_pairs={{0,32},{32,0},{16,48},{48,16},{64,96},{96,64},{80,112},{112,80},{1... | collective-permute-start | bytes 196616 | tf_op jit(solution)/shard_map/ppermute | solution.py:14
  90.6 2.9 %collective-permute-done.3 = bf16[256,128]{0,1:T(8,128)(2,1)S(1)} collective-permute-done((bf16[256,128]{0,1:T(8,128)(2,1)S(1)}, bf16[256,128]{0,1:T(8,128)(2,1)S(1)}, u32[]{:S(2)}, u32[]{:S(2)}) %collective-permute-start.3) | collective-permute-done | bytes 65568 | tf_op jit(solution)/shard_map/ppermute | solution.py:14
  93.5 0.1 multiply_convert_fusion.2
  93.6 0.0 copy-start.3
  93.6 0.4 fusion.19
  94.0 0.2 copy-done.3
  94.2 0.0 copy-done.2
  94.2 0.4 fusion.1
  94.7 1.3 copy.65
  96.0 3.6 %all-to-all-start.2 = ((bf16[16,112,256]{2,1,0:T(8,128)(2,1)}), bf16[16,112,256]{2,1,0:T(8,128)(2,1)S(1)}, u32[]{:S(2)}, u32[]{:S(2)}) async-start(bf16[16,112,256]{2,1,0:T(8,128)(2,1)} %bitcast.8), calls=%async_computation.2 | async-start | bytes 1835008 | tf_op jit(solution)/shard_map/all_to_all | solution.py:87
  99.6 1.2 convolution_convert_fusion
  100.8 12.7 %all-to-all-done.2 = bf16[16,112,256]{2,1,0:T(8,128)(2,1)S(1)} async-done(((bf16[16,112,256]{2,1,0:T(8,128)(2,1)}), bf16[16,112,256]{2,1,0:T(8,128)(2,1)S(1)}, u32[]{:S(2)}, u32[]{:S(2)}) %all-to-all-start.2) | async-done | bytes 917536 | tf_op jit(solution)/shard_map/all_to_all | solution.py:87
  113.5 0.1 reduce_sum.36
  113.6 0.7 copy.66
  114.4 9.5 %all-to-all-start.3 = ((bf16[64,4,112]{2,1,0:T(4,128)(2,1)}), bf16[64,4,112]{2,1,0:T(4,128)(2,1)S(1)}, u32[]{:S(2)}, u32[]{:S(2)}) async-start(bf16[64,4,112]{2,1,0:T(4,128)(2,1)} %bitcast.10), calls=%async_computation.3 | async-start | bytes 131072 | tf_op jit(solution)/shard_map/all_to_all | solution.py:90
  123.8 1.1 fusion.3
  125.0 1.0 copy.70
  125.9 0.3 fusion.2
  126.2 1.0 copy.69
  127.2 21.6 %all-to-all-done.3 = bf16[64,4,112]{2,1,0:T(4,128)(2,1)S(1)} async-done(((bf16[64,4,112]{2,1,0:T(4,128)(2,1)}), bf16[64,4,112]{2,1,0:T(4,128)(2,1)S(1)}, u32[]{:S(2)}, u32[]{:S(2)}) %all-to-all-start.3) | async-done | bytes 57376 | tf_op jit(solution)/shard_map/all_to_all | solution.py:90
  148.8 0.1 reshape.51
  148.9 0.1 dot_general.41
  149.0 0.9 convolution_convert_fusion.3
  (8 shorter events, 0.2 us)
Async XLA Ops:
  0.6 1.8 %copy-start = (bf16[1792,128]{1,0:T(8,128)(2,1)S(1)}, bf16[1792,128]{1,0:T(8,128)(2,1)}, u32[]{:S(2)}) copy-start(bf16[1792,128]{1,0:T(8,128)(2,1)} %param.16) | copy-start | bytes 1376260
  0.6 2.3 %copy-start.1 = (bf16[1792,128]{1,0:T(8,128)(2,1)S(1)}, bf16[1792,128]{1,0:T(8,128)(2,1)}, u32[]{:S(2)}) copy-start(bf16[1792,128]{1,0:T(8,128)(2,1)} %param.15) | copy-start | bytes 1376260
  2.4 17.1 %copy-start.9 = (s32[128,8]{0,1:T(8,128)S(1)}, s32[128,8]{0,1:T(8,128)}, u32[]{:S(2)}) copy-start(s32[128,8]{0,1:T(8,128)} %param.13) | copy-start | bytes 12292
  2.4 17.1 %copy-start.6 = (s32[128,8]{0,1:T(8,128)S(1)}, s32[128,8]{0,1:T(8,128)}, u32[]{:S(2)}) copy-start(s32[128,8]{0,1:T(8,128)} %param.12) | copy-start | bytes 12292
  2.4 17.1 %copy-start.7 = (s32[128,8]{0,1:T(8,128)S(1)}, s32[128,8]{0,1:T(8,128)}, u32[]{:S(2)}) copy-start(s32[128,8]{0,1:T(8,128)} %param.11) | copy-start | bytes 12292
  2.4 17.1 %copy-start.8 = (f32[128,8]{0,1:T(8,128)S(1)}, f32[128,8]{0,1:T(8,128)}, u32[]{:S(2)}) copy-start(f32[128,8]{0,1:T(8,128)} %param.10) | copy-start | bytes 12292
  2.5 17.3 %copy-start.5 = (bf16[128,4,112]{0,2,1:T(8,128)(2,1)S(1)}, bf16[128,4,112]{0,2,1:T(8,128)(2,1)}, u32[]{:S(2)}) copy-start(bf16[128,4,112]{0,2,1:T(8,128)(2,1)} %param.9) | copy-start | bytes 344068
  3.4 33.7 %collective-permute-start = (bf16[256,256]{0,1:T(8,128)(2,1)S(1)}, bf16[256,256]{0,1:T(8,128)(2,1)S(1)}, u32[]{:S(2)}, u32[]{:S(2)}) collective-permute-start(bf16[256,256]{0,1:T(8,128)(2,1)S(1)} %fusion.6), channel_id=1, source_target_pairs={{0,16},{16,0},{32,48},{48,32},{64,80},{80,64},{96,112},{112,96},{1... | collective-permute-start | bytes 393224 | tf_op jit(solution)/shard_map/ppermute | solution.py:14
  20.7 41.3 %all-to-all-start = ((bf16[64,4,112]{2,1,0:T(4,128)(2,1)}), bf16[64,4,112]{2,1,0:T(4,128)(2,1)S(1)}, u32[]{:S(2)}, u32[]{:S(2)}) async-start(bf16[64,4,112]{2,1,0:T(4,128)(2,1)} %copy.61), calls=%async_computation | async-start | bytes 131072 | tf_op jit(solution)/shard_map/all_to_all | solution.py:60
  37.2 44.6 %copy-start.4 = (bf16[1792,128]{1,0:T(8,128)(2,1)S(1)}, bf16[1792,128]{1,0:T(8,128)(2,1)}, u32[]{:S(2)}) copy-start(bf16[1792,128]{1,0:T(8,128)(2,1)} %param.17) | copy-start | bytes 1376260
  37.2 8.5 %collective-permute-start.1 = (bf16[256,256]{0,1:T(8,128)(2,1)S(1)}, bf16[256,256]{0,1:T(8,128)(2,1)S(1)}, u32[]{:S(2)}, u32[]{:S(2)}) collective-permute-start(bf16[256,256]{0,1:T(8,128)(2,1)S(1)} %fusion.7), channel_id=1, source_target_pairs={{0,32},{32,0},{16,48},{48,16},{64,96},{96,64},{80,112},{112,80},{1... | collective-permute-start | bytes 393224 | tf_op jit(solution)/shard_map/ppermute | solution.py:14
  82.1 12.1 %copy-start.2 = (bf16[1792,128]{1,0:T(8,128)(2,1)S(1)}, bf16[1792,128]{1,0:T(8,128)(2,1)}, u32[]{:S(2)}) copy-start(bf16[1792,128]{1,0:T(8,128)(2,1)} %param.15) | copy-start | bytes 1376260
  82.1 6.3 %collective-permute-start.2 = (bf16[256,128]{0,1:T(8,128)(2,1)S(1)}, bf16[256,128]{0,1:T(8,128)(2,1)S(1)}, u32[]{:S(2)}, u32[]{:S(2)}) collective-permute-start(bf16[256,128]{0,1:T(8,128)(2,1)S(1)} %get-tuple-element.32), channel_id=1, source_target_pairs={{0,16},{16,0},{32,48},{48,32},{64,80},{80,64},{96,112},{112,96},{1... | collective-permute-start | bytes 196616 | tf_op jit(solution)/shard_map/ppermute | solution.py:14
  88.5 5.0 %collective-permute-start.3 = (bf16[256,128]{0,1:T(8,128)(2,1)S(1)}, bf16[256,128]{0,1:T(8,128)(2,1)S(1)}, u32[]{:S(2)}, u32[]{:S(2)}) collective-permute-start(bf16[256,128]{0,1:T(8,128)(2,1)S(1)} %fusion.9), channel_id=1, source_target_pairs={{0,32},{32,0},{16,48},{48,16},{64,96},{96,64},{80,112},{112,80},{1... | collective-permute-start | bytes 196616 | tf_op jit(solution)/shard_map/ppermute | solution.py:14
  93.6 0.6 copy-start.3
  96.0 17.5 %all-to-all-start.2 = ((bf16[16,112,256]{2,1,0:T(8,128)(2,1)}), bf16[16,112,256]{2,1,0:T(8,128)(2,1)S(1)}, u32[]{:S(2)}, u32[]{:S(2)}) async-start(bf16[16,112,256]{2,1,0:T(8,128)(2,1)} %bitcast.8), calls=%async_computation.2 | async-start | bytes 1835008 | tf_op jit(solution)/shard_map/all_to_all | solution.py:87
  114.4 34.4 %all-to-all-start.3 = ((bf16[64,4,112]{2,1,0:T(4,128)(2,1)}), bf16[64,4,112]{2,1,0:T(4,128)(2,1)S(1)}, u32[]{:S(2)}, u32[]{:S(2)}) async-start(bf16[64,4,112]{2,1,0:T(4,128)(2,1)} %bitcast.10), calls=%async_computation.3 | async-start | bytes 131072 | tf_op jit(solution)/shard_map/all_to_all | solution.py:90

commit v2 on v1

v2 whole, which is shorter than its diff:
```python
import jax
import jax.numpy as jnp
from jax import lax
from jax.experimental import pallas as pl
from jax.experimental.pallas import tpu as pltpu
from jax.sharding import PartitionSpec as P


def swapped(block, mask):
    count = lax.axis_size("node")
    return lax.ppermute(block, "node", [(at, at ^ mask) for at in range(count)])


def swapped_parts(block, mask, axis):
    parts = [swapped(part, mask) for part in jnp.split(block, 2, axis=axis)]
    return jnp.concatenate(parts, axis=axis)


def dot(lhs, rhs, lhs_dim, rhs_dim):
    return lax.dot_general(
        lhs, rhs, (((lhs_dim,), (rhs_dim,)), ((), ())), preferred_element_type=jnp.float32
    )


def call(kernel, outs, *args, flops=0):
    read = sum(a.size * a.dtype.itemsize for a in args)
    wrote = sum(o.size * o.dtype.itemsize for o in outs)
    space = pl.BlockSpec(memory_space=pltpu.VMEM)
    return pl.pallas_call(
        kernel,
        out_shape=outs,
        in_specs=[
            pl.BlockSpec(memory_space=pltpu.SMEM) if a.ndim == 1 else space for a in args
        ],
        out_specs=[space] * len(outs),
        compiler_params=pltpu.CompilerParams(vmem_limit_bytes=8 << 20),
        cost_estimate=pl.CostEstimate(
            flops=flops, bytes_accessed=read + wrote, transcendentals=0
        ),
    )(*args)


def rows_of(shape, dim):
    return lax.broadcasted_iota(jnp.int32, shape, dim)


def dispatch_kernel(capacity, ids, slots, kept, combine, grads, out, placed):
    choices, tokens = ids.shape
    rows = placed.shape[0]
    code = jnp.where(kept[...] == 1, ids[...] * capacity + slots[...], -1)
    row = rows_of((rows, tokens), 0)
    target = row // (4 * capacity) * capacity + row % capacity
    ones = jnp.zeros((rows, tokens), jnp.float32)
    weights = jnp.zeros((rows, tokens), jnp.float32)
    for k in range(choices):
        match = code[k : k + 1, :] == target
        ones = ones + jnp.where(match, 1.0, 0.0)
        weights = weights + jnp.where(match, combine[k : k + 1, :], 0.0)
    weight = jnp.sum(weights, axis=1, keepdims=True)
    hot = ones.astype(jnp.bfloat16)
    placed[...] = hot
    total = jnp.zeros(out.shape, jnp.float32)
    of_quarter = rows_of(out.shape, 0) // capacity % 4
    for q in range(4):
        total = jnp.where(of_quarter == q, dot(hot, grads[q], 1, 1), total)
    out[...] = (total * weight).astype(jnp.bfloat16)


def selection(rows, cols, capacity, half):
    row = rows_of((rows, cols), 0)
    col = rows_of((rows, cols), 1)
    keep = (row // (2 * capacity) * capacity + row % capacity == col) & (
        row // capacity % 2 == half
    )
    return jnp.where(keep, 1.0, 0.0).astype(jnp.bfloat16)


def spread_kernel(capacity, arrived, out):
    rows, piece = arrived.shape
    for half in range(2):
        chosen = selection(rows, rows // 2, capacity, half)
        turned = dot(arrived[...], chosen, 0, 0).astype(jnp.bfloat16)
        for at in range(out.shape[0]):
            out[at, pl.ds(half * piece, piece), :] = turned


def hidden_kernel(core, part, other, gate, up, other_gate, other_up, acts, out):
    piece = gate.shape[1]
    hidden = acts.shape[1] // 3
    joined = part[...] + other[...].astype(jnp.float32)
    pre_gate = joined[:, :hidden]
    pre_up = joined[:, hidden : 2 * hidden]
    grad_act = joined[:, 2 * hidden :]
    gate_sig = jax.nn.sigmoid(pre_gate)
    silu_gate = pre_gate * gate_sig
    gate_slope = pre_up * gate_sig * (1.0 + pre_gate * (1.0 - gate_sig))
    grad_gate = (grad_act * gate_slope).astype(jnp.bfloat16)
    grad_up = (grad_act * silu_gate).astype(jnp.bfloat16)
    acts[:, pl.ds(0, hidden)] = grad_gate
    acts[:, pl.ds(hidden, hidden)] = grad_up
    acts[:, pl.ds(2 * hidden, hidden)] = (silu_gate * pre_up).astype(jnp.bfloat16)
    here = pl.multiple_of(core[0] * piece, 16)
    there = pl.multiple_of((1 - core[0]) * piece, 16)
    for start, gates, ups in ((here, gate, up), (there, other_gate, other_up)):
        for at in range(out.shape[0]):
            total = dot(gates[at], grad_gate, 1, 1) + dot(ups[at], grad_up, 1, 1)
            out[at, pl.ds(start, piece), :] = total.astype(jnp.bfloat16)


def sum_kernel(capacity, pieces, out):
    rows, piece = out.shape
    total = pieces[0].astype(jnp.float32)
    for at in range(1, pieces.shape[0]):
        total = total + pieces[at].astype(jnp.float32)
    rounded = total.astype(jnp.bfloat16)
    result = jnp.zeros((rows, piece), jnp.float32)
    for half in range(2):
        chosen = selection(rows, rows // 2, capacity, half)
        result = result + dot(chosen, rounded[half * piece : (half + 1) * piece], 1, 1)
    out[...] = result.astype(jnp.bfloat16)


def combine_kernel(capacity, returned, placed, out):
    hot = placed[...]
    of_quarter = rows_of(hot.shape, 0) // capacity % 4
    for q in range(4):
        mine = jnp.where(of_quarter == q, hot, jnp.zeros_like(hot))
        out[q] = dot(returned[...], mine, 0, 0).astype(jnp.bfloat16)


def by_core(core, own, other):
    return jnp.where(core == 0, own, other), jnp.where(core == 0, other, own)


def per_device(
    out_grad,
    combine,
    expert_ids,
    slot_ids,
    kept_mask,
    saved_inputs,
    gate_weight,
    up_weight,
    down_weight_t,
):
    node_count = lax.axis_size("node")
    local_count = lax.axis_size("local")
    core = lax.axis_index("node") % 2
    chips = [[2 * z + c for z in range(node_count // 2)] for c in range(2)]
    capacity = saved_inputs.shape[1]
    quarter = saved_inputs.shape[2]
    token_count = out_grad.shape[0]
    piece = out_grad.shape[2]
    hidden = gate_weight.shape[1]
    rows = node_count * capacity
    half = rows // 2
    bf16 = lambda *shape: jax.ShapeDtypeStruct(shape, jnp.bfloat16)

    def across_chips(block):
        block = block.reshape(node_count // 2, 2 * capacity, piece)
        block = lax.all_to_all(
            block, "node", split_axis=0, concat_axis=0, tiled=True, axis_index_groups=chips
        )
        return block.reshape(rows, piece)

    outgoing, placed = call(
        lambda *refs: dispatch_kernel(capacity, *refs),
        [bf16(rows, piece), bf16(rows, token_count)],
        expert_ids.T,
        slot_ids.T,
        kept_mask.T,
        combine.T,
        out_grad.transpose(1, 2, 0),
    )
    placed, inputs = lax.optimization_barrier((placed, saved_inputs.reshape(rows, quarter)))
    arrived = across_chips(outgoing)

    pre = jnp.concatenate(
        [dot(inputs, gate_weight, 1, 0), dot(inputs, up_weight, 1, 0)], axis=1
    )
    pre = pre.reshape(node_count // 2, 2, capacity, 2 * hidden).transpose(1, 0, 2, 3)
    pre = pre.reshape(2, half, 2 * hidden)
    pre, away = by_core(core, pre[0], pre[1])
    pre = pre + swapped_parts(away.astype(jnp.bfloat16), 1, 1).astype(jnp.float32)
    arrived, pre = lax.optimization_barrier((arrived, pre))

    (copies,) = call(
        lambda *refs: spread_kernel(capacity, *refs),
        [bf16(local_count, 2 * piece, half)],
        arrived,
    )
    copies, *own_weights = lax.optimization_barrier(
        (copies, gate_weight, up_weight, down_weight_t)
    )
    grads_in = lax.all_to_all(copies, "local", split_axis=0, concat_axis=0, tiled=True)
    other_gate, other_up, other_down = [swapped(own, 1) for own in own_weights]
    grads_in, other_down, pre = lax.optimization_barrier((grads_in, other_down, pre))
    slots_in = grads_in.reshape(local_count, 2, piece, half)
    slots_in, slots_away = by_core(core, slots_in[:, 0], slots_in[:, 1])
    slots_in = slots_in.reshape(quarter, half)
    slots_away = slots_away.reshape(quarter, half)
    part = dot(slots_in, down_weight_t, 0, 0) + dot(slots_away, other_down, 0, 0)
    part = jnp.concatenate([pre, part], axis=1)
    other = swapped(part.astype(jnp.bfloat16), 2)
    acts, partial_value = call(
        hidden_kernel,
        [bf16(half, 3 * hidden), bf16(local_count, 2 * piece, half)],
        core.reshape(1),
        part,
        other,
        *[
            w.reshape(local_count, piece, hidden)
            for w in (gate_weight, up_weight, other_gate, other_up)
        ],
    )

    acts, slots_away, partial_value = lax.optimization_barrier((acts, slots_away, partial_value))
    pieces = lax.all_to_all(partial_value, "local", split_axis=0, concat_axis=0, tiled=True)
    (summed,) = call(
        lambda *refs: sum_kernel(capacity, *refs), [bf16(rows, piece)], pieces
    )
    other_acts = swapped(acts, 1)
    other_slots = swapped(slots_away, 1)
    summed, other_acts, other_slots = lax.optimization_barrier((summed, other_acts, other_slots))
    returned = across_chips(summed)
    all_acts = [
        a.reshape(node_count // 2, capacity, 3 * hidden) for a in by_core(core, acts, other_acts)
    ]
    all_acts = jnp.stack(all_acts, axis=1).reshape(rows, 3 * hidden)
    grad_gate = dot(inputs, all_acts[:, :hidden], 0, 0).astype(jnp.bfloat16)
    grad_up = dot(inputs, all_acts[:, hidden : 2 * hidden], 0, 0).astype(jnp.bfloat16)
    grad_down_t = dot(slots_in, acts[:, 2 * hidden :], 1, 0)
    grad_down_t = grad_down_t + dot(other_slots, other_acts[:, 2 * hidden :], 1, 0)
    grad_down_t = grad_down_t.astype(jnp.bfloat16)

    (token_grad,) = call(
        lambda *refs: combine_kernel(capacity, *refs),
        [bf16(4, piece, token_count)],
        returned,
        placed,
    )
    return (token_grad.transpose(2, 0, 1), grad_gate, grad_up, grad_down_t)


def solution(mesh):
    placed = (
        P("node", None, "local"),
        P("node", None),
        P("node", None),
        P("node", None),
        P("node", None),
        P(None, None, "node"),
        P("node", "local"),
        P("node", "local"),
        P("node", "local"),
    )
    return jax.shard_map(
        per_device,
        mesh=mesh,
        in_specs=placed,
        out_specs=(
            P("node", None, "local"),
            P("node", "local"),
            P("node", "local"),
            P("node", "local"),
        ),
        check_vma=False,
    )
```

time: 150 us -> 145 us (0.967)
  the two profiles are of different devices: /device:TPU:1 before, /device:TPU:8 now
where the time goes in v2:
time: 145 us; the launch traced here: 144 us
  starting transfers between devices  67.6 us (47%)
  waiting for transfers between devices  54.2 us (37%)
  matrix products  7.49 us (5%)
  Pallas kernels  6.3 us (4%)
  local copies, waits for them, and re-layouts  5.61 us (4%)
  other arithmetic  2.35 us (2%)
    all_to_all x2, starting transfers between devices, across_chips(): lax.all_to_all(block, 'node', split_axis=0, concat_axis=0, tiled=True, ax...  37.4 us
    all_to_all x2, waiting for transfers between devices, across_chips(): lax.all_to_all(block, 'node', split_axis=0, concat_axis=0, tiled=True, ax...  36.8 us
    ppermute x8, starting transfers between devices, swapped(): return lax.ppermute(block, 'node', [(at, at ^ mask) for at in range(count)])  17.7 us
    all_to_all x1, starting transfers between devices, per_device(): lax.all_to_all(copies, 'local', split_axis=0, concat_axis=0, tiled=True)  7.53 us
    dot_general x8, matrix products, dot(): lax.dot_general(lhs, rhs, (((lhs_dim,), (rhs_dim,)), ((), ())), preferred...  7.49 us
    all_to_all x1, waiting for transfers between devices, per_device(): lax.all_to_all(partial_value, 'local', split_axis=0, concat_axis=0, tiled...  6.8 us
    pallas_call x5, Pallas kernels, call(): pl.pallas_call(kernel, out_shape=outs, in_specs=[pl.BlockSpec(memory_spac...  6.3 us
    all_to_all x1, waiting for transfers between devices, per_device(): lax.all_to_all(copies, 'local', split_axis=0, concat_axis=0, tiled=True)  6.19 us
  transfers between devices with their start and end apart: 12, of which 6 were waited for; matrix products, arithmetic and copies ran while one was open for 8% of the time, Pallas kernels for 1%

profile of v2, /device:TPU:8, one launch (start us, length us, event | category | flops | bytes accessed | tf_op | source)
XLA Modules:
  0.0 144.4 jit_solution(14113631732428553173)
XLA Ops:
  0.6 0.0 copy-start.4
  0.6 0.0 copy-start.3
  0.7 0.7 copy-done.4
  1.3 0.0 copy-done.3
  1.3 0.0 copy-start.2
  1.3 0.9 copy-done.2
  2.2 0.0 copy-start.5
  2.2 0.7 copy-done.5
  2.9 0.0 copy-start.6
  2.9 0.7 copy-done.6
  3.6 1.0 shard_map.120
  4.6 28.7 %all-to-all-start = ((bf16[32,8,112]{2,1,0:T(8,128)(2,1)}), bf16[32,8,112]{2,1,0:T(8,128)(2,1)S(1)}, u32[]{:S(2)}, u32[]{:S(2)}) async-start(bf16[32,8,112]{2,1,0:T(8,128)(2,1)} %bitcast.6), calls=%async_computation | async-start | bytes 131072 | tf_op jit(solution)/shard_map/all_to_all | solution.py:161
  33.3 0.0 copy-start
  33.3 1.7 %reshape.70 = bf16[256,1792]{1,0:T(8,128)(2,1)S(1)} reshape(bf16[64,4,1792]{2,1,0:T(4,128)(2,1)} %param.14) | data formatting | bytes 1835008 | tf_op jit(solution)/shard_map/reshape | solution.py:175
  35.0 0.0 copy-done
  35.0 0.0 copy-start.1
  35.1 0.5 fusion.9
  35.5 0.5 copy-done.1
  36.1 0.5 fusion.8
  36.6 0.1 copy.16
  36.7 0.1 reshape.71
  36.9 1.9 %collective-permute-start = (bf16[128,128]{1,0:T(8,128)(2,1)S(1)}, bf16[128,128]{1,0:T(8,128)(2,1)S(1)}, u32[]{:S(2)}, u32[]{:S(2)}) collective-permute-start(bf16[128,128]{1,0:T(8,128)(2,1)S(1)} %get-tuple-element.50), channel_id=1, source_target_pairs={{0,16},{16,0},{32,48},{48,32},{64,80},{80,64},{96,112},{112,96},{1... | collective-permute-start | bytes 98312 | tf_op jit(solution)/shard_map/ppermute | solution.py:11
  38.8 2.4 %collective-permute-start.1 = (bf16[128,128]{1,0:T(8,128)(2,1)S(1)}, bf16[128,128]{1,0:T(8,128)(2,1)S(1)}, u32[]{:S(2)}, u32[]{:S(2)}) collective-permute-start(bf16[128,128]{1,0:T(8,128)(2,1)S(1)} %get-tuple-element.51), channel_id=1, source_target_pairs={{0,16},{16,0},{32,48},{48,32},{64,80},{80,64},{96,112},{112,96},{1... | collective-permute-start | bytes 98312 | tf_op jit(solution)/shard_map/ppermute | solution.py:11
  41.3 0.0 collective-permute-done
  41.3 0.7 collective-permute-done.1
  42.1 17.0 %all-to-all-done = bf16[32,8,112]{2,1,0:T(8,128)(2,1)S(1)} async-done(((bf16[32,8,112]{2,1,0:T(8,128)(2,1)}), bf16[32,8,112]{2,1,0:T(8,128)(2,1)S(1)}, u32[]{:S(2)}, u32[]{:S(2)}) %all-to-all-start) | async-done | bytes 57376 | tf_op jit(solution)/shard_map/all_to_all | solution.py:161
  59.1 1.2 shard_map.121
  60.3 0.0 copy-start.7
  60.3 7.5 %all-to-all-start.1 = ((bf16[16,224,128]{2,1,0:T(8,128)(2,1)}), bf16[16,224,128]{2,1,0:T(8,128)(2,1)}, u32[]{:S(2)}, u32[]{:S(2)}) async-start(bf16[16,224,128]{2,1,0:T(8,128)(2,1)} %shard_map.121), calls=%async_computation.1 | async-start | bytes 1835008 | tf_op jit(solution)/shard_map/all_to_all | solution.py:195
  67.8 0.0 copy-done.7
  67.8 1.9 %collective-permute-start.2 = (bf16[1792,128]{1,0:T(8,128)(2,1)S(1)}, bf16[1792,128]{1,0:T(8,128)(2,1)}, u32[]{:S(2)}, u32[]{:S(2)}) collective-permute-start(bf16[1792,128]{1,0:T(8,128)(2,1)S(1)} %copy-done.7), channel_id=1, source_target_pairs={{0,16},{16,0},{32,48},{48,32},{64,80},{80,64},{96,112},{112,96},{1... | collective-permute-start | bytes 1376264 | tf_op jit(solution)/shard_map/ppermute | solution.py:11
  69.7 2.4 %collective-permute-start.4 = (bf16[1792,128]{1,0:T(8,128)(2,1)S(1)}, bf16[1792,128]{1,0:T(8,128)(2,1)S(1)}, u32[]{:S(2)}, u32[]{:S(2)}) collective-permute-start(bf16[1792,128]{1,0:T(8,128)(2,1)S(1)} %copy-done.1), channel_id=1, source_target_pairs={{0,16},{16,0},{32,48},{48,32},{64,80},{80,64},{96,112},{112,96},{1... | collective-permute-start | bytes 1376264 | tf_op jit(solution)/shard_map/ppermute | solution.py:11
  72.1 1.9 %collective-permute-start.5 = (bf16[1792,128]{1,0:T(8,128)(2,1)S(1)}, bf16[1792,128]{1,0:T(8,128)(2,1)S(1)}, u32[]{:S(2)}, u32[]{:S(2)}) collective-permute-start(bf16[1792,128]{1,0:T(8,128)(2,1)S(1)} %copy-done), channel_id=1, source_target_pairs={{0,16},{16,0},{32,48},{48,32},{64,80},{80,64},{96,112},{112,96},{1... | collective-permute-start | bytes 1376264 | tf_op jit(solution)/shard_map/ppermute | solution.py:11
  74.1 0.0 collective-permute-done.2
  74.1 6.2 %all-to-all-done.1 = bf16[16,224,128]{2,1,0:T(8,128)(2,1)} async-done(((bf16[16,224,128]{2,1,0:T(8,128)(2,1)}), bf16[16,224,128]{2,1,0:T(8,128)(2,1)}, u32[]{:S(2)}, u32[]{:S(2)}) %all-to-all-start.1) | async-done | bytes 917536 | tf_op jit(solution)/shard_map/all_to_all | solution.py:195
  80.3 0.0 copy-start.8
  80.3 2.0 %broadcast_select_fusion = (bf16[16,1,112,128]{3,2,1,0:T(8,128)(2,1)}, bf16[16,1,112,128]{3,2,1,0:T(8,128)(2,1)S(1)}) fusion(pred[]{:T(512)S(6)} %eq.4, bf16[16,2,112,128]{3,2,1,0:T(8,128)(2,1)} %bitcast.9), kind=kLoop, calls=%fused_computation.5 | loop fusion | flops 458752 | bytes 1835009 | tf_op jit(solution)/shard_map/jit(_where)/select_n | solution.py:132
  82.3 0.0 copy-done.8
  82.3 0.3 fusion.10
  82.6 1.5 %convolution_add_fusion.1 = f32[128,128]{1,0:T(8,128)S(1)} fusion(f32[128,128]{1,0:T(8,128)S(1)} %fusion.10, bf16[1792,128]{1,0:T(8,128)(2,1)} %bitcast.11, bf16[1792,128]{1,0:T(8,128)(2,1)} %collective-permute-done.2), kind=kOutput, calls=%fused_computation.4 | convolution fusion | flops 58736640 | bytes 1048576 | tf_op jit(solution)/shard_map/dot_general | solution.py:20
  84.2 2.8 %collective-permute-start.3 = (bf16[128,384]{1,0:T(8,128)(2,1)S(1)}, bf16[128,384]{1,0:T(8,128)(2,1)S(1)}, u32[]{:S(2)}, u32[]{:S(2)}) collective-permute-start(bf16[128,384]{1,0:T(8,128)(2,1)S(1)} %fusion.6), channel_id=1, source_target_pairs={{0,32},{16,48},{32,0},{48,16},{64,96},{80,112},{96,64},{112,80},{1... | collective-permute-start | bytes 294920 | tf_op jit(solution)/shard_map/ppermute | solution.py:11
  87.0 0.0 collective-permute-done.4
  87.0 0.0 collective-permute-done.5
  87.0 3.7 %collective-permute-done.3.other = bf16[128,384]{1,0:T(8,128)(2,1)S(1)} collective-permute-done((bf16[128,384]{1,0:T(8,128)(2,1)S(1)}, bf16[128,384]{1,0:T(8,128)(2,1)S(1)}, u32[]{:S(2)}, u32[]{:S(2)}) %collective-permute-start.3) | collective-permute-done | bytes 98336 | tf_op jit(solution)/shard_map/ppermute | solution.py:11
  90.7 2.3 %shard_map.122 = (bf16[128,384]{1,0:T(8,128)(2,1)S(1)}, bf16[16,224,128]{2,1,0:T(8,128)(2,1)}) custom-call(s32[1]{0:T(128)} %bitcast.core, f32[128,384]{1,0:T(8,128)S(1)} %pad_maximum_fusion.1.part, bf16[128,384]{1,0:T(8,128)(2,1)S(1)} %collective-permute-done.3.other, bf16[16,112,128]{2,1,0:T(8,128)(2,1)S(1)} %bitcast.38, ...), custom_call_target="tpu_custom_call" | custom-call | bytes 3145732 | tf_op jit(solution)/shard_map/pallas_call | solution.py:29
  93.0 4.9 %all-to-all-start.2 = ((bf16[16,224,128]{2,1,0:T(8,128)(2,1)}), bf16[16,224,128]{2,1,0:T(8,128)(2,1)S(1)}, u32[]{:S(2)}, u32[]{:S(2)}) async-start(bf16[16,224,128]{2,1,0:T(8,128)(2,1)} %get-tuple-element.39), calls=%async_computation.2 | async-start | bytes 1835008 | tf_op jit(solution)/shard_map/all_to_all | solution.py:218
  97.9 1.9 %collective-permute-start.7 = (bf16[1792,128]{1,0:T(8,128)(2,1)}, bf16[1792,128]{1,0:T(8,128)(2,1)}, u32[]{:S(2)}, u32[]{:S(2)}) collective-permute-start(bf16[1792,128]{1,0:T(8,128)(2,1)} %bitcast.11), channel_id=1, source_target_pairs={{0,16},{16,0},{32,48},{48,32},{64,80},{80,64},{96,112},{112,96},{1... | collective-permute-start | bytes 1376264 | tf_op jit(solution)/shard_map/ppermute | solution.py:11
  99.8 2.4 %collective-permute-start.6 = (bf16[128,384]{1,0:T(8,128)(2,1)S(1)}, bf16[128,384]{1,0:T(8,128)(2,1)S(1)}, u32[]{:S(2)}, u32[]{:S(2)}) collective-permute-start(bf16[128,384]{1,0:T(8,128)(2,1)S(1)} %get-tuple-element.40), channel_id=1, source_target_pairs={{0,16},{16,0},{32,48},{48,32},{64,80},{80,64},{96,112},{112,96},{1... | collective-permute-start | bytes 294920 | tf_op jit(solution)/shard_map/ppermute | solution.py:11
  102.2 0.3 fusion.4
  102.5 6.8 %all-to-all-done.2.refs_0_ = bf16[16,224,128]{2,1,0:T(8,128)(2,1)S(1)} async-done(((bf16[16,224,128]{2,1,0:T(8,128)(2,1)}), bf16[16,224,128]{2,1,0:T(8,128)(2,1)S(1)}, u32[]{:S(2)}, u32[]{:S(2)}) %all-to-all-start.2) | async-done | bytes 917536 | tf_op jit(solution)/shard_map/all_to_all | solution.py:218
  109.3 0.9 shard_map.123
  110.2 0.0 collective-permute-done.6
  110.2 0.0 collective-permute-done.7
  110.2 8.7 %all-to-all-start.3 = ((bf16[32,8,112]{2,1,0:T(8,128)(2,1)}), bf16[32,8,112]{2,1,0:T(8,128)(2,1)S(1)}, u32[]{:S(2)}, u32[]{:S(2)}) async-start(bf16[32,8,112]{2,1,0:T(8,128)(2,1)} %bitcast.16), calls=%async_computation.3 | async-start | bytes 131072 | tf_op jit(solution)/shard_map/all_to_all | solution.py:161
  119.1 0.1 pad_maximum_fusion.2
  119.2 0.1 reshape.79
  119.3 1.2 convolution_convert_fusion
  120.5 1.2 convolution_convert_fusion.1
  121.7 2.0 %fusion = bf16[1792,128]{1,0:T(8,128)(2,1)} fusion(f32[1792,128]{1,0:T(8,128)S(1)} %fusion.4, bf16[1792,128]{1,0:T(8,128)(2,1)} %collective-permute-done.7, bf16[128,384]{1,0:T(8,128)(2,1)S(1)} %collective-permute-done.6), kind=kOutput, calls=%fused_computation.1 | convolution fusion | flops 59179008 | bytes 1867776 | tf_op jit(solution)/shard_map/dot_general | solution.py:20
  123.7 19.8 %all-to-all-done.3 = bf16[32,8,112]{2,1,0:T(8,128)(2,1)S(1)} async-done(((bf16[32,8,112]{2,1,0:T(8,128)(2,1)}), bf16[32,8,112]{2,1,0:T(8,128)(2,1)S(1)}, u32[]{:S(2)}, u32[]{:S(2)}) %all-to-all-start.3) | async-done | bytes 57376 | tf_op jit(solution)/shard_map/all_to_all | solution.py:161
  143.5 0.9 shard_map.124
  (12 shorter events, 0.3 us)
Async XLA Ops:
  0.6 0.7 copy-start.4
  0.6 0.7 copy-start.3
  1.3 0.9 copy-start.2
  2.2 0.7 copy-start.5
  2.9 0.7 copy-start.6
  4.6 54.5 %all-to-all-start = ((bf16[32,8,112]{2,1,0:T(8,128)(2,1)}), bf16[32,8,112]{2,1,0:T(8,128)(2,1)S(1)}, u32[]{:S(2)}, u32[]{:S(2)}) async-start(bf16[32,8,112]{2,1,0:T(8,128)(2,1)} %bitcast.6), calls=%async_computation | async-start | bytes 131072 | tf_op jit(solution)/shard_map/all_to_all | solution.py:161
  33.3 1.7 %copy-start = (bf16[1792,128]{1,0:T(8,128)(2,1)S(1)}, bf16[1792,128]{1,0:T(8,128)(2,1)}, u32[]{:S(2)}) copy-start(bf16[1792,128]{1,0:T(8,128)(2,1)} %param.16) | copy-start | bytes 1376260
  35.0 1.0 copy-start.1
  36.9 4.4 %collective-permute-start = (bf16[128,128]{1,0:T(8,128)(2,1)S(1)}, bf16[128,128]{1,0:T(8,128)(2,1)S(1)}, u32[]{:S(2)}, u32[]{:S(2)}) collective-permute-start(bf16[128,128]{1,0:T(8,128)(2,1)S(1)} %get-tuple-element.50), channel_id=1, source_target_pairs={{0,16},{16,0},{32,48},{48,32},{64,80},{80,64},{96,112},{112,96},{1... | collective-permute-start | bytes 98312 | tf_op jit(solution)/shard_map/ppermute | solution.py:11
  38.8 3.3 %collective-permute-start.1 = (bf16[128,128]{1,0:T(8,128)(2,1)S(1)}, bf16[128,128]{1,0:T(8,128)(2,1)S(1)}, u32[]{:S(2)}, u32[]{:S(2)}) collective-permute-start(bf16[128,128]{1,0:T(8,128)(2,1)S(1)} %get-tuple-element.51), channel_id=1, source_target_pairs={{0,16},{16,0},{32,48},{48,32},{64,80},{80,64},{96,112},{112,96},{1... | collective-permute-start | bytes 98312 | tf_op jit(solution)/shard_map/ppermute | solution.py:11
  60.3 7.5 %copy-start.7 = (bf16[1792,128]{1,0:T(8,128)(2,1)S(1)}, bf16[1792,128]{1,0:T(8,128)(2,1)}, u32[]{:S(2)}) copy-start(bf16[1792,128]{1,0:T(8,128)(2,1)} %param.17) | copy-start | bytes 1376260
  60.3 20.0 %all-to-all-start.1 = ((bf16[16,224,128]{2,1,0:T(8,128)(2,1)}), bf16[16,224,128]{2,1,0:T(8,128)(2,1)}, u32[]{:S(2)}, u32[]{:S(2)}) async-start(bf16[16,224,128]{2,1,0:T(8,128)(2,1)} %shard_map.121), calls=%async_computation.1 | async-start | bytes 1835008 | tf_op jit(solution)/shard_map/all_to_all | solution.py:195
  67.8 6.3 %collective-permute-start.2 = (bf16[1792,128]{1,0:T(8,128)(2,1)S(1)}, bf16[1792,128]{1,0:T(8,128)(2,1)}, u32[]{:S(2)}, u32[]{:S(2)}) collective-permute-start(bf16[1792,128]{1,0:T(8,128)(2,1)S(1)} %copy-done.7), channel_id=1, source_target_pairs={{0,16},{16,0},{32,48},{48,32},{64,80},{80,64},{96,112},{112,96},{1... | collective-permute-start | bytes 1376264 | tf_op jit(solution)/shard_map/ppermute | solution.py:11
  69.7 17.3 %collective-permute-start.4 = (bf16[1792,128]{1,0:T(8,128)(2,1)S(1)}, bf16[1792,128]{1,0:T(8,128)(2,1)S(1)}, u32[]{:S(2)}, u32[]{:S(2)}) collective-permute-start(bf16[1792,128]{1,0:T(8,128)(2,1)S(1)} %copy-done.1), channel_id=1, source_target_pairs={{0,16},{16,0},{32,48},{48,32},{64,80},{80,64},{96,112},{112,96},{1... | collective-permute-start | bytes 1376264 | tf_op jit(solution)/shard_map/ppermute | solution.py:11
  72.1 14.9 %collective-permute-start.5 = (bf16[1792,128]{1,0:T(8,128)(2,1)S(1)}, bf16[1792,128]{1,0:T(8,128)(2,1)S(1)}, u32[]{:S(2)}, u32[]{:S(2)}) collective-permute-start(bf16[1792,128]{1,0:T(8,128)(2,1)S(1)} %copy-done), channel_id=1, source_target_pairs={{0,16},{16,0},{32,48},{48,32},{64,80},{80,64},{96,112},{112,96},{1... | collective-permute-start | bytes 1376264 | tf_op jit(solution)/shard_map/ppermute | solution.py:11
  80.3 2.0 %copy-start.8 = (bf16[1792,128]{1,0:T(8,128)(2,1)S(1)}, bf16[1792,128]{1,0:T(8,128)(2,1)}, u32[]{:S(2)}) copy-start(bf16[1792,128]{1,0:T(8,128)(2,1)} %param.17) | copy-start | bytes 1376260
  84.2 6.5 %collective-permute-start.3 = (bf16[128,384]{1,0:T(8,128)(2,1)S(1)}, bf16[128,384]{1,0:T(8,128)(2,1)S(1)}, u32[]{:S(2)}, u32[]{:S(2)}) collective-permute-start(bf16[128,384]{1,0:T(8,128)(2,1)S(1)} %fusion.6), channel_id=1, source_target_pairs={{0,32},{16,48},{32,0},{48,16},{64,96},{80,112},{96,64},{112,80},{1... | collective-permute-start | bytes 294920 | tf_op jit(solution)/shard_map/ppermute | solution.py:11
  93.0 16.3 %all-to-all-start.2 = ((bf16[16,224,128]{2,1,0:T(8,128)(2,1)}), bf16[16,224,128]{2,1,0:T(8,128)(2,1)S(1)}, u32[]{:S(2)}, u32[]{:S(2)}) async-start(bf16[16,224,128]{2,1,0:T(8,128)(2,1)} %get-tuple-element.39), calls=%async_computation.2 | async-start | bytes 1835008 | tf_op jit(solution)/shard_map/all_to_all | solution.py:218
  97.9 12.3 %collective-permute-start.7 = (bf16[1792,128]{1,0:T(8,128)(2,1)}, bf16[1792,128]{1,0:T(8,128)(2,1)}, u32[]{:S(2)}, u32[]{:S(2)}) collective-permute-start(bf16[1792,128]{1,0:T(8,128)(2,1)} %bitcast.11), channel_id=1, source_target_pairs={{0,16},{16,0},{32,48},{48,32},{64,80},{80,64},{96,112},{112,96},{1... | collective-permute-start | bytes 1376264 | tf_op jit(solution)/shard_map/ppermute | solution.py:11
  99.8 10.4 %collective-permute-start.6 = (bf16[128,384]{1,0:T(8,128)(2,1)S(1)}, bf16[128,384]{1,0:T(8,128)(2,1)S(1)}, u32[]{:S(2)}, u32[]{:S(2)}) collective-permute-start(bf16[128,384]{1,0:T(8,128)(2,1)S(1)} %get-tuple-element.40), channel_id=1, source_target_pairs={{0,16},{16,0},{32,48},{48,32},{64,80},{80,64},{96,112},{112,96},{1... | collective-permute-start | bytes 294920 | tf_op jit(solution)/shard_map/ppermute | solution.py:11
  110.2 33.3 %all-to-all-start.3 = ((bf16[32,8,112]{2,1,0:T(8,128)(2,1)}), bf16[32,8,112]{2,1,0:T(8,128)(2,1)S(1)}, u32[]{:S(2)}, u32[]{:S(2)}) async-start(bf16[32,8,112]{2,1,0:T(8,128)(2,1)} %bitcast.16), calls=%async_computation.3 | async-start | bytes 131072 | tf_op jit(solution)/shard_map/all_to_all | solution.py:161

commit v3 on v2

--- a/solution.py
+++ b/solution.py
@@ -22,7 +22,7 @@
     )
 
 
-def call(kernel, outs, *args, flops=0):
+def call(kernel, outs, *args, flops=0, vmem=8 << 20):
     read = sum(a.size * a.dtype.itemsize for a in args)
     wrote = sum(o.size * o.dtype.itemsize for o in outs)
     space = pl.BlockSpec(memory_space=pltpu.VMEM)
@@ -33,7 +33,7 @@
             pl.BlockSpec(memory_space=pltpu.SMEM) if a.ndim == 1 else space for a in args
         ],
         out_specs=[space] * len(outs),
-        compiler_params=pltpu.CompilerParams(vmem_limit_bytes=8 << 20),
+        compiler_params=pltpu.CompilerParams(vmem_limit_bytes=vmem),
         cost_estimate=pl.CostEstimate(
             flops=flops, bytes_accessed=read + wrote, transcendentals=0
         ),
@@ -84,27 +84,35 @@
             out[at, pl.ds(half * piece, piece), :] = turned
 
 
-def hidden_kernel(core, part, other, gate, up, other_gate, other_up, acts, out):
-    piece = gate.shape[1]
-    hidden = acts.shape[1] // 3
-    joined = part[...] + other[...].astype(jnp.float32)
-    pre_gate = joined[:, :hidden]
-    pre_up = joined[:, hidden : 2 * hidden]
-    grad_act = joined[:, 2 * hidden :]
+def starts(core, piece):
+    return pl.multiple_of(core[0] * piece, 16), pl.multiple_of((1 - core[0]) * piece, 16)
+
+
+def pair_kernel(core, own, other, out):
+    here, there = starts(core, own.shape[1])
+    for at in range(out.shape[0]):
+        out[at, pl.ds(here, own.shape[1]), :] = own[at]
+        out[at, pl.ds(there, own.shape[1]), :] = other[at]
+
+
+def hidden_kernel(core, pre, part, other, gate_up, other_gate_up, acts, out):
+    piece = gate_up.shape[1]
+    hidden = part.shape[1]
+    pre_gate = pre[:, :hidden]
+    pre_up = pre[:, hidden:]
+    grad_act = part[...] + other[...].astype(jnp.float32)
     gate_sig = jax.nn.sigmoid(pre_gate)
     silu_gate = pre_gate * gate_sig
     gate_slope = pre_up * gate_sig * (1.0 + pre_gate * (1.0 - gate_sig))
     grad_gate = (grad_act * gate_slope).astype(jnp.bfloat16)
     grad_up = (grad_act * silu_gate).astype(jnp.bfloat16)
-    acts[:, pl.ds(0, hidden)] = grad_gate
-    acts[:, pl.ds(hidden, hidden)] = grad_up
+    both = jnp.concatenate([grad_gate, grad_up], axis=1)
+    acts[:, pl.ds(0, 2 * hidden)] = both
     acts[:, pl.ds(2 * hidden, hidden)] = (silu_gate * pre_up).astype(jnp.bfloat16)
-    here = pl.multiple_of(core[0] * piece, 16)
-    there = pl.multiple_of((1 - core[0]) * piece, 16)
-    for start, gates, ups in ((here, gate, up), (there, other_gate, other_up)):
+    here, there = starts(core, piece)
+    for start, weights in ((here, gate_up), (there, other_gate_up)):
         for at in range(out.shape[0]):
-            total = dot(gates[at], grad_gate, 1, 1) + dot(ups[at], grad_up, 1, 1)
-            out[at, pl.ds(start, piece), :] = total.astype(jnp.bfloat16)
+            out[at, pl.ds(start, piece), :] = dot(weights[at], both, 1, 1).astype(jnp.bfloat16)
 
 
 def sum_kernel(capacity, pieces, out):
@@ -171,13 +179,15 @@
         kept_mask.T,
         combine.T,
         out_grad.transpose(1, 2, 0),
-    )
-    placed, inputs = lax.optimization_barrier((placed, saved_inputs.reshape(rows, quarter)))
+        vmem=56 << 20,
+    )
+    placed, inputs, *gate_up = lax.optimization_barrier(
+        (placed, saved_inputs.reshape(rows, quarter), gate_weight, up_weight)
+    )
+    gate_up = jnp.concatenate(gate_up, axis=1)
     arrived = across_chips(outgoing)
 
-    pre = jnp.concatenate(
-        [dot(inputs, gate_weight, 1, 0), dot(inputs, up_weight, 1, 0)], axis=1
-    )
+    pre = dot(inputs, gate_up, 1, 0)
     pre = pre.reshape(node_count // 2, 2, capacity, 2 * hidden).transpose(1, 0, 2, 3)
     pre = pre.reshape(2, half, 2 * hidden)
     pre, away = by_core(core, pre[0], pre[1])
@@ -189,31 +199,40 @@
         [bf16(local_count, 2 * piece, half)],
         arrived,
     )
-    copies, *own_weights = lax.optimization_barrier(
-        (copies, gate_weight, up_weight, down_weight_t)
-    )
+    copies, own_down, gate_up = lax.optimization_barrier((copies, down_weight_t, gate_up))
     grads_in = lax.all_to_all(copies, "local", split_axis=0, concat_axis=0, tiled=True)
-    other_gate, other_up, other_down = [swapped(own, 1) for own in own_weights]
-    grads_in, other_down, pre = lax.optimization_barrier((grads_in, other_down, pre))
-    slots_in = grads_in.reshape(local_count, 2, piece, half)
-    slots_in, slots_away = by_core(core, slots_in[:, 0], slots_in[:, 1])
-    slots_in = slots_in.reshape(quarter, half)
-    slots_away = slots_away.reshape(quarter, half)
-    part = dot(slots_in, down_weight_t, 0, 0) + dot(slots_away, other_down, 0, 0)
-    part = jnp.concatenate([pre, part], axis=1)
+    other_down = swapped(own_down, 1)
+    other_gate_up = swapped(gate_up, 1)
+    other_down, pre = lax.optimization_barrier((other_down, pre))
+    pre = pre + swapped(pre.astype(jnp.bfloat16), 2).astype(jnp.float32)
+    by_piece = lambda block: block.reshape(local_count, piece, block.shape[1])
+    (down_pair,) = call(
+        pair_kernel,
+        [bf16(local_count, 2 * piece, hidden)],
+        core.reshape(1),
+        by_piece(own_down),
+        by_piece(other_down),
+    )
+    grads_in, down_pair = lax.optimization_barrier((grads_in, down_pair))
+    part = dot(
+        grads_in.reshape(2 * quarter, half), down_pair.reshape(2 * quarter, hidden), 0, 0
+    )
     other = swapped(part.astype(jnp.bfloat16), 2)
     acts, partial_value = call(
         hidden_kernel,
         [bf16(half, 3 * hidden), bf16(local_count, 2 * piece, half)],
         core.reshape(1),
+        pre,
         part,
         other,
-        *[
-            w.reshape(local_count, piece, hidden)
-            for w in (gate_weight, up_weight, other_gate, other_up)
-        ],
-    )
-
+        by_piece(gate_up),
+        by_piece(other_gate_up),
+    )
+
+    slots_in = grads_in.reshape(local_count, 2, piece, half)
+    slots_in, slots_away = by_core(core, slots_in[:, 0], slots_in[:, 1])
+    slots_in = slots_in.reshape(quarter, half)
+    slots_away = slots_away.reshape(quarter, half)
     acts, slots_away, partial_value = lax.optimization_barrier((acts, slots_away, partial_value))
     pieces = lax.all_to_all(partial_value, "local", split_axis=0, concat_axis=0, tiled=True)
     (summed,) = call(

time: 145 us -> 140 us (0.966)
  local copies, waits for them, and re-layouts: 5.61 us -> 3.45 us
  matrix products: 7.49 us -> 5.76 us
  waiting for transfers between devices: 54.2 us -> 52.6 us
    all_to_all x1, waiting for transfers between devices: 6.19 us -> 1.92 us  [per_device(): lax.all_to_all(copies, 'local', split_axis=0, concat_axis=0, tiled=True)]
    unnamed x18 -> x13, local copies, waits for them, and re-layouts: 3.52 us -> 1.36 us
    dot_general x8 -> x6, matrix products: 7.49 us -> 5.76 us  [dot(): lax.dot_general(lhs, rhs, (((lhs_dim,), (rhs_dim,)), ((), ())), preferred...]
    pallas_call x5 -> x6, Pallas kernels: 6.3 us -> 6.8 us  [call(): pl.pallas_call(kernel, out_shape=outs, in_specs=[pl.BlockSpec(memory_spac...]
  transfers between devices with their start and end apart: 12 -> 12, of which waited for: 6 -> 7; matrix products, arithmetic and copies ran while one was open for 8% -> 7% of each run, Pallas kernels for 1% -> 1%
where the time goes in v3:
time: 140 us; the launch traced here: 139 us
  starting transfers between devices  67.5 us (48%)
  waiting for transfers between devices  52.6 us (38%)
  Pallas kernels  6.8 us (5%)
  matrix products  5.76 us (4%)
  local copies, waits for them, and re-layouts  3.45 us (2%)
  other arithmetic  2.28 us (2%)
    all_to_all x2, waiting for transfers between devices, across_chips(): lax.all_to_all(block, 'node', split_axis=0, concat_axis=0, tiled=True, ax...  37.5 us
    all_to_all x2, starting transfers between devices, across_chips(): lax.all_to_all(block, 'node', split_axis=0, concat_axis=0, tiled=True, ax...  36.3 us
    ppermute x8, starting transfers between devices, swapped(): return lax.ppermute(block, 'node', [(at, at ^ mask) for at in range(count)])  18.4 us
    all_to_all x1, waiting for transfers between devices, per_device(): lax.all_to_all(partial_value, 'local', split_axis=0, concat_axis=0, tiled...  8.03 us
    all_to_all x1, starting transfers between devices, per_device(): lax.all_to_all(copies, 'local', split_axis=0, concat_axis=0, tiled=True)  7.52 us
    pallas_call x6, Pallas kernels, call(): pl.pallas_call(kernel, out_shape=outs, in_specs=[pl.BlockSpec(memory_spac...  6.8 us
    dot_general x6, matrix products, dot(): lax.dot_general(lhs, rhs, (((lhs_dim,), (rhs_dim,)), ((), ())), preferred...  5.76 us
    all_to_all x1, starting transfers between devices, per_device(): lax.all_to_all(partial_value, 'local', split_axis=0, concat_axis=0, tiled...  5.29 us
  transfers between devices with their start and end apart: 12, of which 7 were waited for; matrix products, arithmetic and copies ran while one was open for 7% of the time, Pallas kernels for 1%

profile of v3, /device:TPU:8, one launch (start us, length us, event | category | flops | bytes accessed | tf_op | source)
XLA Modules:
  0.0 139.3 jit_solution(8019368908362024110)
XLA Ops:
  0.6 1.9 %shard_map.120 = (bf16[256,112]{1,0:T(8,128)(2,1)}, bf16[256,128]{1,0:T(8,128)(2,1)}) custom-call(s32[8,128]{1,0:T(8,128)} %bitcast.47, s32[8,128]{1,0:T(8,128)} %bitcast.48, s32[8,128]{1,0:T(8,128)} %bitcast.49, f32[8,128]{1,0:T(8,128)} %bitcast.50, bf16[4,112,128]{2,1,0:T(8,128)(2,1)} %bitcast.44), custom_call_target="tpu_custom_call" | custom-call | bytes 253952 | tf_op jit(solution)/shard_map/pallas_call | solution.py:29
  2.6 28.7 %all-to-all-start = ((bf16[32,8,112]{2,1,0:T(8,128)(2,1)}), bf16[32,8,112]{2,1,0:T(8,128)(2,1)S(1)}, u32[]{:S(2)}, u32[]{:S(2)}) async-start(bf16[32,8,112]{2,1,0:T(8,128)(2,1)} %bitcast.46), calls=%async_computation | async-start | bytes 131072 | tf_op jit(solution)/shard_map/all_to_all | solution.py:169
  31.3 0.0 copy-start.4
  31.3 1.7 %reshape.73 = bf16[256,1792]{1,0:T(8,128)(2,1)S(1)} reshape(bf16[64,4,1792]{2,1,0:T(4,128)(2,1)} %param.14) | data formatting | bytes 1835008 | tf_op jit(solution)/shard_map/reshape | solution.py:185
  33.0 0.0 copy-start.2
  33.0 0.0 copy-done.4
  33.0 0.0 copy-start.5
  33.1 0.1 constant_dynamic-update-slice_fusion.1
  33.1 1.3 copy-done.5
  34.4 0.1 constant_dynamic-update-slice_fusion
  34.5 0.0 copy-done.2
  34.5 0.4 fusion.8
  34.9 0.1 reshape.74
  35.1 1.9 %collective-permute-start = (bf16[128,128]{1,0:T(8,128)(2,1)S(1)}, bf16[128,128]{1,0:T(8,128)(2,1)S(1)}, u32[]{:S(2)}, u32[]{:S(2)}) collective-permute-start(bf16[128,128]{1,0:T(8,128)(2,1)S(1)} %get-tuple-element.54), channel_id=1, source_target_pairs={{0,16},{16,0},{32,48},{48,32},{64,80},{80,64},{96,112},{112,96},{1... | collective-permute-start | bytes 98312 | tf_op jit(solution)/shard_map/ppermute | solution.py:11
  37.1 2.4 %collective-permute-start.1 = (bf16[128,128]{1,0:T(8,128)(2,1)S(1)}, bf16[128,128]{1,0:T(8,128)(2,1)S(1)}, u32[]{:S(2)}, u32[]{:S(2)}) collective-permute-start(bf16[128,128]{1,0:T(8,128)(2,1)S(1)} %get-tuple-element.55), channel_id=1, source_target_pairs={{0,16},{16,0},{32,48},{48,32},{64,80},{80,64},{96,112},{112,96},{1... | collective-permute-start | bytes 98312 | tf_op jit(solution)/shard_map/ppermute | solution.py:11
  39.6 0.0 collective-permute-done
  39.6 0.7 collective-permute-done.1
  40.3 16.7 %all-to-all-done = bf16[32,8,112]{2,1,0:T(8,128)(2,1)S(1)} async-done(((bf16[32,8,112]{2,1,0:T(8,128)(2,1)}), bf16[32,8,112]{2,1,0:T(8,128)(2,1)S(1)}, u32[]{:S(2)}, u32[]{:S(2)}) %all-to-all-start) | async-done | bytes 57376 | tf_op jit(solution)/shard_map/all_to_all | solution.py:169
  57.1 1.2 shard_map.121
  58.3 0.0 copy-start
  58.3 7.5 %all-to-all-start.1 = ((bf16[16,224,128]{2,1,0:T(8,128)(2,1)}), bf16[16,224,128]{2,1,0:T(8,128)(2,1)}, u32[]{:S(2)}, u32[]{:S(2)}) async-start(bf16[16,224,128]{2,1,0:T(8,128)(2,1)} %shard_map.121), calls=%async_computation.1 | async-start | bytes 1835008 | tf_op jit(solution)/shard_map/all_to_all | solution.py:203
  65.8 0.0 copy-done
  65.8 1.9 %collective-permute-start.2 = (bf16[1792,128]{1,0:T(8,128)(2,1)S(1)}, bf16[1792,128]{1,0:T(8,128)(2,1)S(1)}, u32[]{:S(2)}, u32[]{:S(2)}) collective-permute-start(bf16[1792,128]{1,0:T(8,128)(2,1)S(1)} %copy-done), channel_id=1, source_target_pairs={{0,16},{16,0},{32,48},{48,32},{64,80},{80,64},{96,112},{112,96},{1... | collective-permute-start | bytes 1376264 | tf_op jit(solution)/shard_map/ppermute | solution.py:11
  67.7 2.4 %collective-permute-start.5 = (bf16[1792,256]{1,0:T(8,128)(2,1)S(1)}, bf16[1792,256]{1,0:T(8,128)(2,1)S(1)}, u32[]{:S(2)}, u32[]{:S(2)}) collective-permute-start(bf16[1792,256]{1,0:T(8,128)(2,1)S(1)} %constant_dynamic-update-slice_fusion), channel_id=1, source_target_pairs={{0,16},{16,0},{32,48},{48,32},{64,80},{80,64},{96,112},{112,96},{1... | collective-permute-start | bytes 2752520 | tf_op jit(solution)/shard_map/ppermute | solution.py:11
  70.2 0.0 collective-permute-done.2
  70.2 2.7 %collective-permute-start.3 = (bf16[128,256]{1,0:T(8,128)(2,1)S(1)}, bf16[128,256]{1,0:T(8,128)(2,1)S(1)}, u32[]{:S(2)}, u32[]{:S(2)}) collective-permute-start(bf16[128,256]{1,0:T(8,128)(2,1)S(1)} %convert_element_type.30), channel_id=1, source_target_pairs={{0,32},{16,48},{32,0},{48,16},{64,96},{80,112},{96,64},{112,80},{1... | collective-permute-start | bytes 196616 | tf_op jit(solution)/shard_map/ppermute | solution.py:11
  72.8 0.1 shard_map.122
  72.9 3.4 %collective-permute-done.3 = bf16[128,256]{1,0:T(8,128)(2,1)S(1)} collective-permute-done((bf16[128,256]{1,0:T(8,128)(2,1)S(1)}, bf16[128,256]{1,0:T(8,128)(2,1)S(1)}, u32[]{:S(2)}, u32[]{:S(2)}) %collective-permute-start.3) | collective-permute-done | bytes 65568 | tf_op jit(solution)/shard_map/ppermute | solution.py:11
  76.4 1.9 %all-to-all-done.1 = bf16[16,224,128]{2,1,0:T(8,128)(2,1)} async-done(((bf16[16,224,128]{2,1,0:T(8,128)(2,1)}), bf16[16,224,128]{2,1,0:T(8,128)(2,1)}, u32[]{:S(2)}, u32[]{:S(2)}) %all-to-all-start.1) | async-done | bytes 917536 | tf_op jit(solution)/shard_map/all_to_all | solution.py:203
  78.3 1.6 %fusion.7 = (bf16[128,128]{1,0:T(8,128)(2,1)S(1)}, f32[128,128]{1,0:T(8,128)S(1)}) fusion(bf16[16,224,128]{2,1,0:T(8,128)(2,1)} %all-to-all-done.1, bf16[16,224,128]{2,1,0:T(8,128)(2,1)S(1)} %shard_map.122), kind=kOutput, calls=%fused_computation.23 | convolution fusion | flops 117456896 | bytes 1933312 | tf_op jit(solution)/shard_map/dot_general | solution.py:20
  79.9 2.8 %collective-permute-start.4 = (bf16[128,128]{1,0:T(8,128)(2,1)S(1)}, bf16[128,128]{1,0:T(8,128)(2,1)S(1)}, u32[]{:S(2)}, u32[]{:S(2)}) collective-permute-start(bf16[128,128]{1,0:T(8,128)(2,1)S(1)} %get-tuple-element.56), channel_id=1, source_target_pairs={{0,32},{16,48},{32,0},{48,16},{64,96},{80,112},{96,64},{112,80},{1... | collective-permute-start | bytes 98312 | tf_op jit(solution)/shard_map/ppermute | solution.py:11
  82.7 2.0 %broadcast_select_fusion = (bf16[16,1,112,128]{3,2,1,0:T(8,128)(2,1)S(1)}, bf16[16,1,112,128]{3,2,1,0:T(8,128)(2,1)}) fusion(pred[]{:T(512)S(6)} %eq.4, bf16[16,2,112,128]{3,2,1,0:T(8,128)(2,1)} %bitcast.14), kind=kLoop, calls=%fused_computation.5 | loop fusion | flops 458752 | bytes 1835009 | tf_op jit(solution)/shard_map/jit(_where)/select_n | solution.py:140
  84.7 1.0 collective-permute-done.4.other
  85.7 0.0 collective-permute-done.5
  85.7 1.7 %shard_map.123 = (bf16[128,384]{1,0:T(8,128)(2,1)S(1)}, bf16[16,224,128]{2,1,0:T(8,128)(2,1)}) custom-call(s32[1]{0:T(128)} %bitcast.core, f32[128,256]{1,0:T(8,128)S(1)} %convert_add_fusion.pre, f32[128,128]{1,0:T(8,128)S(1)} %get-tuple-element.57.part, bf16[128,128]{1,0:T(8,128)(2,1)S(1)} %collective-permute-done.4.other, ...), custom_call_target="tpu_custom_call" | custom-call | bytes 3080196 | tf_op jit(solution)/shard_map/pallas_call | solution.py:29
  87.5 5.3 %all-to-all-start.2 = ((bf16[16,224,128]{2,1,0:T(8,128)(2,1)}), bf16[16,224,128]{2,1,0:T(8,128)(2,1)S(1)}, u32[]{:S(2)}, u32[]{:S(2)}) async-start(bf16[16,224,128]{2,1,0:T(8,128)(2,1)} %get-tuple-element.43), calls=%async_computation.2 | async-start | bytes 1835008 | tf_op jit(solution)/shard_map/all_to_all | solution.py:237
  92.7 1.9 %collective-permute-start.7 = (bf16[1792,128]{1,0:T(8,128)(2,1)}, bf16[1792,128]{1,0:T(8,128)(2,1)S(1)}, u32[]{:S(2)}, u32[]{:S(2)}) collective-permute-start(bf16[1792,128]{1,0:T(8,128)(2,1)} %bitcast.15), channel_id=1, source_target_pairs={{0,16},{16,0},{32,48},{48,32},{64,80},{80,64},{96,112},{112,96},{1... | collective-permute-start | bytes 1376264 | tf_op jit(solution)/shard_map/ppermute | solution.py:11
  94.7 2.4 %collective-permute-start.6 = (bf16[128,384]{1,0:T(8,128)(2,1)S(1)}, bf16[128,384]{1,0:T(8,128)(2,1)S(1)}, u32[]{:S(2)}, u32[]{:S(2)}) collective-permute-start(bf16[128,384]{1,0:T(8,128)(2,1)S(1)} %get-tuple-element.44), channel_id=1, source_target_pairs={{0,16},{16,0},{32,48},{48,32},{64,80},{80,64},{96,112},{112,96},{1... | collective-permute-start | bytes 294920 | tf_op jit(solution)/shard_map/ppermute | solution.py:11
  97.1 0.3 fusion.4
  97.3 8.0 %all-to-all-done.2.refs_0_ = bf16[16,224,128]{2,1,0:T(8,128)(2,1)S(1)} async-done(((bf16[16,224,128]{2,1,0:T(8,128)(2,1)}), bf16[16,224,128]{2,1,0:T(8,128)(2,1)S(1)}, u32[]{:S(2)}, u32[]{:S(2)}) %all-to-all-start.2) | async-done | bytes 917536 | tf_op jit(solution)/shard_map/all_to_all | solution.py:237
  105.4 0.9 shard_map.124
  106.3 0.0 copy-start.3
  106.3 0.0 collective-permute-done.6
  106.3 0.0 collective-permute-done.7
  106.3 7.5 %all-to-all-start.3 = ((bf16[32,8,112]{2,1,0:T(8,128)(2,1)}), bf16[32,8,112]{2,1,0:T(8,128)(2,1)S(1)}, u32[]{:S(2)}, u32[]{:S(2)}) async-start(bf16[32,8,112]{2,1,0:T(8,128)(2,1)} %bitcast.16), calls=%async_computation.3 | async-start | bytes 131072 | tf_op jit(solution)/shard_map/all_to_all | solution.py:169
  114.0 0.1 pad_maximum_fusion
  114.1 0.1 reshape.82
  114.2 0.0 copy-done.3
  114.2 1.2 convolution_convert_fusion
  115.4 1.2 convolution_convert_fusion.1
  116.6 0.0 copy-start.1
  116.6 1.0 fusion
  117.6 20.8 %all-to-all-done.3 = bf16[32,8,112]{2,1,0:T(8,128)(2,1)S(1)} async-done(((bf16[32,8,112]{2,1,0:T(8,128)(2,1)}), bf16[32,8,112]{2,1,0:T(8,128)(2,1)S(1)}, u32[]{:S(2)}, u32[]{:S(2)}) %all-to-all-start.3) | async-done | bytes 57376 | tf_op jit(solution)/shard_map/all_to_all | solution.py:169
  138.4 0.0 copy-done.1
  138.4 0.9 shard_map.125
  (12 shorter events, 0.3 us)
Async XLA Ops:
  2.6 54.5 %all-to-all-start = ((bf16[32,8,112]{2,1,0:T(8,128)(2,1)}), bf16[32,8,112]{2,1,0:T(8,128)(2,1)S(1)}, u32[]{:S(2)}, u32[]{:S(2)}) async-start(bf16[32,8,112]{2,1,0:T(8,128)(2,1)} %bitcast.46), calls=%async_computation | async-start | bytes 131072 | tf_op jit(solution)/shard_map/all_to_all | solution.py:169
  31.3 1.7 %copy-start.4 = (bf16[1792,128]{1,0:T(8,128)(2,1)S(1)}, bf16[1792,128]{1,0:T(8,128)(2,1)}, u32[]{:S(2)}) copy-start(bf16[1792,128]{1,0:T(8,128)(2,1)} %param.15) | copy-start | bytes 1376260
  33.0 1.5 %copy-start.2 = (bf16[256,1792]{1,0:T(8,128)(2,1)}, bf16[256,1792]{1,0:T(8,128)(2,1)S(1)}, u32[]{:S(2)}) copy-start(bf16[256,1792]{1,0:T(8,128)(2,1)S(1)} %reshape.73) | copy-start | bytes 2752516
  33.0 1.4 copy-start.5
  35.1 4.4 %collective-permute-start = (bf16[128,128]{1,0:T(8,128)(2,1)S(1)}, bf16[128,128]{1,0:T(8,128)(2,1)S(1)}, u32[]{:S(2)}, u32[]{:S(2)}) collective-permute-start(bf16[128,128]{1,0:T(8,128)(2,1)S(1)} %get-tuple-element.54), channel_id=1, source_target_pairs={{0,16},{16,0},{32,48},{48,32},{64,80},{80,64},{96,112},{112,96},{1... | collective-permute-start | bytes 98312 | tf_op jit(solution)/shard_map/ppermute | solution.py:11
  37.1 3.3 %collective-permute-start.1 = (bf16[128,128]{1,0:T(8,128)(2,1)S(1)}, bf16[128,128]{1,0:T(8,128)(2,1)S(1)}, u32[]{:S(2)}, u32[]{:S(2)}) collective-permute-start(bf16[128,128]{1,0:T(8,128)(2,1)S(1)} %get-tuple-element.55), channel_id=1, source_target_pairs={{0,16},{16,0},{32,48},{48,32},{64,80},{80,64},{96,112},{112,96},{1... | collective-permute-start | bytes 98312 | tf_op jit(solution)/shard_map/ppermute | solution.py:11
  58.3 7.5 %copy-start = (bf16[1792,128]{1,0:T(8,128)(2,1)S(1)}, bf16[1792,128]{1,0:T(8,128)(2,1)}, u32[]{:S(2)}) copy-start(bf16[1792,128]{1,0:T(8,128)(2,1)} %param.17) | copy-start | bytes 1376260
  58.3 20.0 %all-to-all-start.1 = ((bf16[16,224,128]{2,1,0:T(8,128)(2,1)}), bf16[16,224,128]{2,1,0:T(8,128)(2,1)}, u32[]{:S(2)}, u32[]{:S(2)}) async-start(bf16[16,224,128]{2,1,0:T(8,128)(2,1)} %shard_map.121), calls=%async_computation.1 | async-start | bytes 1835008 | tf_op jit(solution)/shard_map/all_to_all | solution.py:203
  65.8 4.3 %collective-permute-start.2 = (bf16[1792,128]{1,0:T(8,128)(2,1)S(1)}, bf16[1792,128]{1,0:T(8,128)(2,1)S(1)}, u32[]{:S(2)}, u32[]{:S(2)}) collective-permute-start(bf16[1792,128]{1,0:T(8,128)(2,1)S(1)} %copy-done), channel_id=1, source_target_pairs={{0,16},{16,0},{32,48},{48,32},{64,80},{80,64},{96,112},{112,96},{1... | collective-permute-start | bytes 1376264 | tf_op jit(solution)/shard_map/ppermute | solution.py:11
  67.7 18.0 %collective-permute-start.5 = (bf16[1792,256]{1,0:T(8,128)(2,1)S(1)}, bf16[1792,256]{1,0:T(8,128)(2,1)S(1)}, u32[]{:S(2)}, u32[]{:S(2)}) collective-permute-start(bf16[1792,256]{1,0:T(8,128)(2,1)S(1)} %constant_dynamic-update-slice_fusion), channel_id=1, source_target_pairs={{0,16},{16,0},{32,48},{48,32},{64,80},{80,64},{96,112},{112,96},{1... | collective-permute-start | bytes 2752520 | tf_op jit(solution)/shard_map/ppermute | solution.py:11
  70.2 6.2 %collective-permute-start.3 = (bf16[128,256]{1,0:T(8,128)(2,1)S(1)}, bf16[128,256]{1,0:T(8,128)(2,1)S(1)}, u32[]{:S(2)}, u32[]{:S(2)}) collective-permute-start(bf16[128,256]{1,0:T(8,128)(2,1)S(1)} %convert_element_type.30), channel_id=1, source_target_pairs={{0,32},{16,48},{32,0},{48,16},{64,96},{80,112},{96,64},{112,80},{1... | collective-permute-start | bytes 196616 | tf_op jit(solution)/shard_map/ppermute | solution.py:11
  79.9 5.8 %collective-permute-start.4 = (bf16[128,128]{1,0:T(8,128)(2,1)S(1)}, bf16[128,128]{1,0:T(8,128)(2,1)S(1)}, u32[]{:S(2)}, u32[]{:S(2)}) collective-permute-start(bf16[128,128]{1,0:T(8,128)(2,1)S(1)} %get-tuple-element.56), channel_id=1, source_target_pairs={{0,32},{16,48},{32,0},{48,16},{64,96},{80,112},{96,64},{112,80},{1... | collective-permute-start | bytes 98312 | tf_op jit(solution)/shard_map/ppermute | solution.py:11
  87.5 17.9 %all-to-all-start.2 = ((bf16[16,224,128]{2,1,0:T(8,128)(2,1)}), bf16[16,224,128]{2,1,0:T(8,128)(2,1)S(1)}, u32[]{:S(2)}, u32[]{:S(2)}) async-start(bf16[16,224,128]{2,1,0:T(8,128)(2,1)} %get-tuple-element.43), calls=%async_computation.2 | async-start | bytes 1835008 | tf_op jit(solution)/shard_map/all_to_all | solution.py:237
  92.7 13.6 %collective-permute-start.7 = (bf16[1792,128]{1,0:T(8,128)(2,1)}, bf16[1792,128]{1,0:T(8,128)(2,1)S(1)}, u32[]{:S(2)}, u32[]{:S(2)}) collective-permute-start(bf16[1792,128]{1,0:T(8,128)(2,1)} %bitcast.15), channel_id=1, source_target_pairs={{0,16},{16,0},{32,48},{48,32},{64,80},{80,64},{96,112},{112,96},{1... | collective-permute-start | bytes 1376264 | tf_op jit(solution)/shard_map/ppermute | solution.py:11
  94.7 11.7 %collective-permute-start.6 = (bf16[128,384]{1,0:T(8,128)(2,1)S(1)}, bf16[128,384]{1,0:T(8,128)(2,1)S(1)}, u32[]{:S(2)}, u32[]{:S(2)}) collective-permute-start(bf16[128,384]{1,0:T(8,128)(2,1)S(1)} %get-tuple-element.44), channel_id=1, source_target_pairs={{0,16},{16,0},{32,48},{48,32},{64,80},{80,64},{96,112},{112,96},{1... | collective-permute-start | bytes 294920 | tf_op jit(solution)/shard_map/ppermute | solution.py:11
  106.3 7.8 %copy-start.3 = (bf16[256,1792]{1,0:T(8,128)(2,1)S(1)}, bf16[256,1792]{1,0:T(8,128)(2,1)}, u32[]{:S(2)}) copy-start(bf16[256,1792]{1,0:T(8,128)(2,1)} %copy-done.2) | copy-start | bytes 2752516
  106.3 32.1 %all-to-all-start.3 = ((bf16[32,8,112]{2,1,0:T(8,128)(2,1)}), bf16[32,8,112]{2,1,0:T(8,128)(2,1)S(1)}, u32[]{:S(2)}, u32[]{:S(2)}) async-start(bf16[32,8,112]{2,1,0:T(8,128)(2,1)} %bitcast.16), calls=%async_computation.3 | async-start | bytes 131072 | tf_op jit(solution)/shard_map/all_to_all | solution.py:169
  116.6 21.8 %copy-start.1 = (bf16[256,128]{1,0:T(8,128)(2,1)S(1)}, bf16[256,128]{1,0:T(8,128)(2,1)}, u32[]{:S(2)}) copy-start(bf16[256,128]{1,0:T(8,128)(2,1)} %get-tuple-element.47.refs_1_) | copy-start | bytes 196612

commit v4 on v3

--- a/solution.py
+++ b/solution.py
@@ -44,11 +44,17 @@
     return lax.broadcasted_iota(jnp.int32, shape, dim)
 
 
+def turned_rows(shape):
+    row = rows_of(shape, 0)
+    middle = shape[0] // 2
+    return jnp.where(row < middle, row + middle, row - middle)
+
+
 def dispatch_kernel(capacity, ids, slots, kept, combine, grads, out, placed):
     choices, tokens = ids.shape
     rows = placed.shape[0]
     code = jnp.where(kept[...] == 1, ids[...] * capacity + slots[...], -1)
-    row = rows_of((rows, tokens), 0)
+    row = turned_rows((rows, tokens))
     target = row // (4 * capacity) * capacity + row % capacity
     ones = jnp.zeros((rows, tokens), jnp.float32)
     weights = jnp.zeros((rows, tokens), jnp.float32)
@@ -67,7 +73,7 @@
 
 
 def selection(rows, cols, capacity, half):
-    row = rows_of((rows, cols), 0)
+    row = turned_rows((rows, cols))
     col = rows_of((rows, cols), 1)
     keep = (row // (2 * capacity) * capacity + row % capacity == col) & (
         row // capacity % 2 == half
@@ -154,7 +160,8 @@
     node_count = lax.axis_size("node")
     local_count = lax.axis_size("local")
     core = lax.axis_index("node") % 2
-    chips = [[2 * z + c for z in range(node_count // 2)] for c in range(2)]
+    ring = node_count // 2
+    chips = [[2 * ((z + ring // 2) % ring) + c for z in range(ring)] for c in range(2)]
     capacity = saved_inputs.shape[1]
     quarter = saved_inputs.shape[2]
     token_count = out_grad.shape[0]

time: 140 us -> 128 us (0.914)
  the two profiles are of different devices: /device:TPU:8 before, /device:TPU:32 now
where the time goes in v4:
time: 128 us; the launch traced here: 127 us
  starting transfers between devices  86.6 us (68%)
  waiting for transfers between devices  21.6 us (17%)
  Pallas kernels  6.85 us (5%)
  matrix products  5.76 us (4%)
  local copies, waits for them, and re-layouts  3.45 us (3%)
  other arithmetic  2.28 us (2%)
    all_to_all x2, starting transfers between devices, across_chips(): lax.all_to_all(block, 'node', split_axis=0, concat_axis=0, tiled=True, ax...  56 us
    ppermute x8, starting transfers between devices, swapped(): return lax.ppermute(block, 'node', [(at, at ^ mask) for at in range(count)])  19.7 us
    all_to_all x1, waiting for transfers between devices, per_device(): lax.all_to_all(partial_value, 'local', split_axis=0, concat_axis=0, tiled...  9.46 us
    all_to_all x1, starting transfers between devices, per_device(): lax.all_to_all(copies, 'local', split_axis=0, concat_axis=0, tiled=True)  7.21 us
    pallas_call x6, Pallas kernels, call(): pl.pallas_call(kernel, out_shape=outs, in_specs=[pl.BlockSpec(memory_spac...  6.85 us
    all_to_all x1, waiting for transfers between devices, per_device(): lax.all_to_all(copies, 'local', split_axis=0, concat_axis=0, tiled=True)  6.22 us
    dot_general x6, matrix products, dot(): lax.dot_general(lhs, rhs, (((lhs_dim,), (rhs_dim,)), ((), ())), preferred...  5.76 us
    ppermute x8, waiting for transfers between devices, swapped(): return lax.ppermute(block, 'node', [(at, at ^ mask) for at in range(count)])  3.86 us
  transfers between devices with their start and end apart: 12, of which 6 were waited for; matrix products, arithmetic and copies ran while one was open for 8% of the time, Pallas kernels for 1%

profile of v4, /device:TPU:32, one launch (start us, length us, event | category | flops | bytes accessed | tf_op | source)
XLA Modules:
  0.0 127.5 jit_solution(7347549242772914518)
XLA Ops:
  0.6 1.9 %shard_map.120 = (bf16[256,112]{1,0:T(8,128)(2,1)}, bf16[256,128]{1,0:T(8,128)(2,1)}) custom-call(s32[8,128]{1,0:T(8,128)} %bitcast.47, s32[8,128]{1,0:T(8,128)} %bitcast.48, s32[8,128]{1,0:T(8,128)} %bitcast.49, f32[8,128]{1,0:T(8,128)} %bitcast.50, bf16[4,112,128]{2,1,0:T(8,128)(2,1)} %bitcast.44), custom_call_target="tpu_custom_call" | custom-call | bytes 253952 | tf_op jit(solution)/shard_map/pallas_call | solution.py:29
  2.6 34.5 %all-to-all-start = ((bf16[32,8,112]{2,1,0:T(8,128)(2,1)}), bf16[32,8,112]{2,1,0:T(8,128)(2,1)S(1)}, u32[]{:S(2)}, u32[]{:S(2)}) async-start(bf16[32,8,112]{2,1,0:T(8,128)(2,1)} %bitcast.46), calls=%async_computation | async-start | bytes 131072 | tf_op jit(solution)/shard_map/all_to_all | solution.py:176
  37.1 0.0 copy-start.4
  37.1 1.7 %reshape.73 = bf16[256,1792]{1,0:T(8,128)(2,1)S(1)} reshape(bf16[64,4,1792]{2,1,0:T(4,128)(2,1)} %param.14) | data formatting | bytes 1835008 | tf_op jit(solution)/shard_map/reshape | solution.py:192
  38.8 0.0 copy-start.2
  38.9 0.0 copy-done.4
  38.9 0.0 copy-start.5
  38.9 0.1 constant_dynamic-update-slice_fusion.1
  39.0 1.3 copy-done.5
  40.2 0.1 constant_dynamic-update-slice_fusion
  40.3 0.0 copy-done.2
  40.3 0.4 fusion.8
  40.8 0.1 reshape.74
  41.0 1.9 %collective-permute-start = (bf16[128,128]{1,0:T(8,128)(2,1)S(1)}, bf16[128,128]{1,0:T(8,128)(2,1)S(1)}, u32[]{:S(2)}, u32[]{:S(2)}) collective-permute-start(bf16[128,128]{1,0:T(8,128)(2,1)S(1)} %get-tuple-element.54), channel_id=1, source_target_pairs={{0,16},{16,0},{32,48},{48,32},{64,80},{80,64},{96,112},{112,96},{1... | collective-permute-start | bytes 98312 | tf_op jit(solution)/shard_map/ppermute | solution.py:11
  42.9 2.4 %collective-permute-start.1 = (bf16[128,128]{1,0:T(8,128)(2,1)S(1)}, bf16[128,128]{1,0:T(8,128)(2,1)S(1)}, u32[]{:S(2)}, u32[]{:S(2)}) collective-permute-start(bf16[128,128]{1,0:T(8,128)(2,1)S(1)} %get-tuple-element.55), channel_id=1, source_target_pairs={{0,16},{16,0},{32,48},{48,32},{64,80},{80,64},{96,112},{112,96},{1... | collective-permute-start | bytes 98312 | tf_op jit(solution)/shard_map/ppermute | solution.py:11
  45.4 0.0 collective-permute-done
  45.4 0.7 collective-permute-done.1
  46.2 0.0 all-to-all-done
  46.2 1.2 shard_map.121
  47.4 0.0 copy-start
  47.4 7.2 %all-to-all-start.1 = ((bf16[16,224,128]{2,1,0:T(8,128)(2,1)}), bf16[16,224,128]{2,1,0:T(8,128)(2,1)}, u32[]{:S(2)}, u32[]{:S(2)}) async-start(bf16[16,224,128]{2,1,0:T(8,128)(2,1)} %shard_map.121), calls=%async_computation.1 | async-start | bytes 1835008 | tf_op jit(solution)/shard_map/all_to_all | solution.py:210
  54.6 0.0 copy-done
  54.6 2.0 %collective-permute-start.2 = (bf16[1792,128]{1,0:T(8,128)(2,1)S(1)}, bf16[1792,128]{1,0:T(8,128)(2,1)S(1)}, u32[]{:S(2)}, u32[]{:S(2)}) collective-permute-start(bf16[1792,128]{1,0:T(8,128)(2,1)S(1)} %copy-done), channel_id=1, source_target_pairs={{0,16},{16,0},{32,48},{48,32},{64,80},{80,64},{96,112},{112,96},{1... | collective-permute-start | bytes 1376264 | tf_op jit(solution)/shard_map/ppermute | solution.py:11
  56.6 2.3 %collective-permute-start.5 = (bf16[1792,256]{1,0:T(8,128)(2,1)S(1)}, bf16[1792,256]{1,0:T(8,128)(2,1)S(1)}, u32[]{:S(2)}, u32[]{:S(2)}) collective-permute-start(bf16[1792,256]{1,0:T(8,128)(2,1)S(1)} %constant_dynamic-update-slice_fusion), channel_id=1, source_target_pairs={{0,16},{16,0},{32,48},{48,32},{64,80},{80,64},{96,112},{112,96},{1... | collective-permute-start | bytes 2752520 | tf_op jit(solution)/shard_map/ppermute | solution.py:11
  59.0 0.0 collective-permute-done.2
  59.0 3.4 %collective-permute-start.3 = (bf16[128,256]{1,0:T(8,128)(2,1)S(1)}, bf16[128,256]{1,0:T(8,128)(2,1)S(1)}, u32[]{:S(2)}, u32[]{:S(2)}) collective-permute-start(bf16[128,256]{1,0:T(8,128)(2,1)S(1)} %convert_element_type.30), channel_id=1, source_target_pairs={{0,32},{16,48},{32,0},{48,16},{64,96},{80,112},{96,64},{112,80},{1... | collective-permute-start | bytes 196616 | tf_op jit(solution)/shard_map/ppermute | solution.py:11
  62.4 0.1 shard_map.122
  62.5 2.7 %collective-permute-done.3 = bf16[128,256]{1,0:T(8,128)(2,1)S(1)} collective-permute-done((bf16[128,256]{1,0:T(8,128)(2,1)S(1)}, bf16[128,256]{1,0:T(8,128)(2,1)S(1)}, u32[]{:S(2)}, u32[]{:S(2)}) %collective-permute-start.3) | collective-permute-done | bytes 65568 | tf_op jit(solution)/shard_map/ppermute | solution.py:11
  65.2 6.2 %all-to-all-done.1 = bf16[16,224,128]{2,1,0:T(8,128)(2,1)} async-done(((bf16[16,224,128]{2,1,0:T(8,128)(2,1)}), bf16[16,224,128]{2,1,0:T(8,128)(2,1)}, u32[]{:S(2)}, u32[]{:S(2)}) %all-to-all-start.1) | async-done | bytes 917536 | tf_op jit(solution)/shard_map/all_to_all | solution.py:210
  71.4 1.6 %fusion.7 = (bf16[128,128]{1,0:T(8,128)(2,1)S(1)}, f32[128,128]{1,0:T(8,128)S(1)}) fusion(bf16[16,224,128]{2,1,0:T(8,128)(2,1)} %all-to-all-done.1, bf16[16,224,128]{2,1,0:T(8,128)(2,1)S(1)} %shard_map.122), kind=kOutput, calls=%fused_computation.23 | convolution fusion | flops 117456896 | bytes 1933312 | tf_op jit(solution)/shard_map/dot_general | solution.py:20
  73.0 3.4 %collective-permute-start.4 = (bf16[128,128]{1,0:T(8,128)(2,1)S(1)}, bf16[128,128]{1,0:T(8,128)(2,1)S(1)}, u32[]{:S(2)}, u32[]{:S(2)}) collective-permute-start(bf16[128,128]{1,0:T(8,128)(2,1)S(1)} %get-tuple-element.56), channel_id=1, source_target_pairs={{0,32},{16,48},{32,0},{48,16},{64,96},{80,112},{96,64},{112,80},{1... | collective-permute-start | bytes 98312 | tf_op jit(solution)/shard_map/ppermute | solution.py:11
  76.4 2.0 %broadcast_select_fusion = (bf16[16,1,112,128]{3,2,1,0:T(8,128)(2,1)S(1)}, bf16[16,1,112,128]{3,2,1,0:T(8,128)(2,1)}) fusion(pred[]{:T(512)S(6)} %eq.4, bf16[16,2,112,128]{3,2,1,0:T(8,128)(2,1)} %bitcast.14), kind=kLoop, calls=%fused_computation.5 | loop fusion | flops 458752 | bytes 1835009 | tf_op jit(solution)/shard_map/jit(_where)/select_n | solution.py:146
  78.4 0.4 collective-permute-done.4.other
  78.8 0.0 collective-permute-done.5
  78.8 1.7 %shard_map.123 = (bf16[128,384]{1,0:T(8,128)(2,1)S(1)}, bf16[16,224,128]{2,1,0:T(8,128)(2,1)}) custom-call(s32[1]{0:T(128)} %bitcast.core, f32[128,256]{1,0:T(8,128)S(1)} %convert_add_fusion.pre, f32[128,128]{1,0:T(8,128)S(1)} %get-tuple-element.57.part, bf16[128,128]{1,0:T(8,128)(2,1)S(1)} %collective-permute-done.4.other, ...), custom_call_target="tpu_custom_call" | custom-call | bytes 3080196 | tf_op jit(solution)/shard_map/pallas_call | solution.py:29
  80.6 3.6 %all-to-all-start.2 = ((bf16[16,224,128]{2,1,0:T(8,128)(2,1)}), bf16[16,224,128]{2,1,0:T(8,128)(2,1)S(1)}, u32[]{:S(2)}, u32[]{:S(2)}) async-start(bf16[16,224,128]{2,1,0:T(8,128)(2,1)} %get-tuple-element.43), calls=%async_computation.2 | async-start | bytes 1835008 | tf_op jit(solution)/shard_map/all_to_all | solution.py:244
  84.2 1.9 %collective-permute-start.7 = (bf16[1792,128]{1,0:T(8,128)(2,1)}, bf16[1792,128]{1,0:T(8,128)(2,1)S(1)}, u32[]{:S(2)}, u32[]{:S(2)}) collective-permute-start(bf16[1792,128]{1,0:T(8,128)(2,1)} %bitcast.15), channel_id=1, source_target_pairs={{0,16},{16,0},{32,48},{48,32},{64,80},{80,64},{96,112},{112,96},{1... | collective-permute-start | bytes 1376264 | tf_op jit(solution)/shard_map/ppermute | solution.py:11
  86.1 2.4 %collective-permute-start.6 = (bf16[128,384]{1,0:T(8,128)(2,1)S(1)}, bf16[128,384]{1,0:T(8,128)(2,1)S(1)}, u32[]{:S(2)}, u32[]{:S(2)}) collective-permute-start(bf16[128,384]{1,0:T(8,128)(2,1)S(1)} %get-tuple-element.44), channel_id=1, source_target_pairs={{0,16},{16,0},{32,48},{48,32},{64,80},{80,64},{96,112},{112,96},{1... | collective-permute-start | bytes 294920 | tf_op jit(solution)/shard_map/ppermute | solution.py:11
  88.5 0.3 fusion.4
  88.8 9.5 %all-to-all-done.2.refs_0_ = bf16[16,224,128]{2,1,0:T(8,128)(2,1)S(1)} async-done(((bf16[16,224,128]{2,1,0:T(8,128)(2,1)}), bf16[16,224,128]{2,1,0:T(8,128)(2,1)S(1)}, u32[]{:S(2)}, u32[]{:S(2)}) %all-to-all-start.2) | async-done | bytes 917536 | tf_op jit(solution)/shard_map/all_to_all | solution.py:244
  98.3 1.0 shard_map.124
  99.2 0.0 copy-start.3
  99.2 0.0 collective-permute-done.6
  99.2 0.0 collective-permute-done.7
  99.2 21.5 %all-to-all-start.3 = ((bf16[32,8,112]{2,1,0:T(8,128)(2,1)}), bf16[32,8,112]{2,1,0:T(8,128)(2,1)S(1)}, u32[]{:S(2)}, u32[]{:S(2)}) async-start(bf16[32,8,112]{2,1,0:T(8,128)(2,1)} %bitcast.16), calls=%async_computation.3 | async-start | bytes 131072 | tf_op jit(solution)/shard_map/all_to_all | solution.py:176
  120.8 0.1 pad_maximum_fusion
  121.0 0.1 reshape.82
  121.0 0.0 copy-done.3
  121.0 1.2 convolution_convert_fusion
  122.2 1.2 convolution_convert_fusion.1
  123.5 0.0 copy-start.1
  123.5 1.0 fusion
  124.5 2.1 %all-to-all-done.3 = bf16[32,8,112]{2,1,0:T(8,128)(2,1)S(1)} async-done(((bf16[32,8,112]{2,1,0:T(8,128)(2,1)}), bf16[32,8,112]{2,1,0:T(8,128)(2,1)S(1)}, u32[]{:S(2)}, u32[]{:S(2)}) %all-to-all-start.3) | async-done | bytes 57376 | tf_op jit(solution)/shard_map/all_to_all | solution.py:176
  126.5 0.0 copy-done.1
  126.5 0.9 shard_map.125
  (12 shorter events, 0.3 us)
Async XLA Ops:
  2.6 43.6 %all-to-all-start = ((bf16[32,8,112]{2,1,0:T(8,128)(2,1)}), bf16[32,8,112]{2,1,0:T(8,128)(2,1)S(1)}, u32[]{:S(2)}, u32[]{:S(2)}) async-start(bf16[32,8,112]{2,1,0:T(8,128)(2,1)} %bitcast.46), calls=%async_computation | async-start | bytes 131072 | tf_op jit(solution)/shard_map/all_to_all | solution.py:176
  37.1 1.7 %copy-start.4 = (bf16[1792,128]{1,0:T(8,128)(2,1)S(1)}, bf16[1792,128]{1,0:T(8,128)(2,1)}, u32[]{:S(2)}) copy-start(bf16[1792,128]{1,0:T(8,128)(2,1)} %param.15) | copy-start | bytes 1376260
  38.8 1.5 %copy-start.2 = (bf16[256,1792]{1,0:T(8,128)(2,1)}, bf16[256,1792]{1,0:T(8,128)(2,1)S(1)}, u32[]{:S(2)}) copy-start(bf16[256,1792]{1,0:T(8,128)(2,1)S(1)} %reshape.73) | copy-start | bytes 2752516
  38.9 1.4 %copy-start.5 = (bf16[1792,128]{1,0:T(8,128)(2,1)S(1)}, bf16[1792,128]{1,0:T(8,128)(2,1)}, u32[]{:S(2)}) copy-start(bf16[1792,128]{1,0:T(8,128)(2,1)} %param.16) | copy-start | bytes 1376260
  41.0 4.4 %collective-permute-start = (bf16[128,128]{1,0:T(8,128)(2,1)S(1)}, bf16[128,128]{1,0:T(8,128)(2,1)S(1)}, u32[]{:S(2)}, u32[]{:S(2)}) collective-permute-start(bf16[128,128]{1,0:T(8,128)(2,1)S(1)} %get-tuple-element.54), channel_id=1, source_target_pairs={{0,16},{16,0},{32,48},{48,32},{64,80},{80,64},{96,112},{112,96},{1... | collective-permute-start | bytes 98312 | tf_op jit(solution)/shard_map/ppermute | solution.py:11
  42.9 3.3 %collective-permute-start.1 = (bf16[128,128]{1,0:T(8,128)(2,1)S(1)}, bf16[128,128]{1,0:T(8,128)(2,1)S(1)}, u32[]{:S(2)}, u32[]{:S(2)}) collective-permute-start(bf16[128,128]{1,0:T(8,128)(2,1)S(1)} %get-tuple-element.55), channel_id=1, source_target_pairs={{0,16},{16,0},{32,48},{48,32},{64,80},{80,64},{96,112},{112,96},{1... | collective-permute-start | bytes 98312 | tf_op jit(solution)/shard_map/ppermute | solution.py:11
  47.4 7.2 %copy-start = (bf16[1792,128]{1,0:T(8,128)(2,1)S(1)}, bf16[1792,128]{1,0:T(8,128)(2,1)}, u32[]{:S(2)}) copy-start(bf16[1792,128]{1,0:T(8,128)(2,1)} %param.17) | copy-start | bytes 1376260
  47.4 24.0 %all-to-all-start.1 = ((bf16[16,224,128]{2,1,0:T(8,128)(2,1)}), bf16[16,224,128]{2,1,0:T(8,128)(2,1)}, u32[]{:S(2)}, u32[]{:S(2)}) async-start(bf16[16,224,128]{2,1,0:T(8,128)(2,1)} %shard_map.121), calls=%async_computation.1 | async-start | bytes 1835008 | tf_op jit(solution)/shard_map/all_to_all | solution.py:210
  54.6 4.3 %collective-permute-start.2 = (bf16[1792,128]{1,0:T(8,128)(2,1)S(1)}, bf16[1792,128]{1,0:T(8,128)(2,1)S(1)}, u32[]{:S(2)}, u32[]{:S(2)}) collective-permute-start(bf16[1792,128]{1,0:T(8,128)(2,1)S(1)} %copy-done), channel_id=1, source_target_pairs={{0,16},{16,0},{32,48},{48,32},{64,80},{80,64},{96,112},{112,96},{1... | collective-permute-start | bytes 1376264 | tf_op jit(solution)/shard_map/ppermute | solution.py:11
  56.6 22.2 %collective-permute-start.5 = (bf16[1792,256]{1,0:T(8,128)(2,1)S(1)}, bf16[1792,256]{1,0:T(8,128)(2,1)S(1)}, u32[]{:S(2)}, u32[]{:S(2)}) collective-permute-start(bf16[1792,256]{1,0:T(8,128)(2,1)S(1)} %constant_dynamic-update-slice_fusion), channel_id=1, source_target_pairs={{0,16},{16,0},{32,48},{48,32},{64,80},{80,64},{96,112},{112,96},{1... | collective-permute-start | bytes 2752520 | tf_op jit(solution)/shard_map/ppermute | solution.py:11
  59.0 6.2 %collective-permute-start.3 = (bf16[128,256]{1,0:T(8,128)(2,1)S(1)}, bf16[128,256]{1,0:T(8,128)(2,1)S(1)}, u32[]{:S(2)}, u32[]{:S(2)}) collective-permute-start(bf16[128,256]{1,0:T(8,128)(2,1)S(1)} %convert_element_type.30), channel_id=1, source_target_pairs={{0,32},{16,48},{32,0},{48,16},{64,96},{80,112},{96,64},{112,80},{1... | collective-permute-start | bytes 196616 | tf_op jit(solution)/shard_map/ppermute | solution.py:11
  73.0 5.8 %collective-permute-start.4 = (bf16[128,128]{1,0:T(8,128)(2,1)S(1)}, bf16[128,128]{1,0:T(8,128)(2,1)S(1)}, u32[]{:S(2)}, u32[]{:S(2)}) collective-permute-start(bf16[128,128]{1,0:T(8,128)(2,1)S(1)} %get-tuple-element.56), channel_id=1, source_target_pairs={{0,32},{16,48},{32,0},{48,16},{64,96},{80,112},{96,64},{112,80},{1... | collective-permute-start | bytes 98312 | tf_op jit(solution)/shard_map/ppermute | solution.py:11
  80.6 17.7 %all-to-all-start.2 = ((bf16[16,224,128]{2,1,0:T(8,128)(2,1)}), bf16[16,224,128]{2,1,0:T(8,128)(2,1)S(1)}, u32[]{:S(2)}, u32[]{:S(2)}) async-start(bf16[16,224,128]{2,1,0:T(8,128)(2,1)} %get-tuple-element.43), calls=%async_computation.2 | async-start | bytes 1835008 | tf_op jit(solution)/shard_map/all_to_all | solution.py:244
  84.2 15.0 %collective-permute-start.7 = (bf16[1792,128]{1,0:T(8,128)(2,1)}, bf16[1792,128]{1,0:T(8,128)(2,1)S(1)}, u32[]{:S(2)}, u32[]{:S(2)}) collective-permute-start(bf16[1792,128]{1,0:T(8,128)(2,1)} %bitcast.15), channel_id=1, source_target_pairs={{0,16},{16,0},{32,48},{48,32},{64,80},{80,64},{96,112},{112,96},{1... | collective-permute-start | bytes 1376264 | tf_op jit(solution)/shard_map/ppermute | solution.py:11
  86.1 13.1 %collective-permute-start.6 = (bf16[128,384]{1,0:T(8,128)(2,1)S(1)}, bf16[128,384]{1,0:T(8,128)(2,1)S(1)}, u32[]{:S(2)}, u32[]{:S(2)}) collective-permute-start(bf16[128,384]{1,0:T(8,128)(2,1)S(1)} %get-tuple-element.44), channel_id=1, source_target_pairs={{0,16},{16,0},{32,48},{48,32},{64,80},{80,64},{96,112},{112,96},{1... | collective-permute-start | bytes 294920 | tf_op jit(solution)/shard_map/ppermute | solution.py:11
  99.2 21.8 %copy-start.3 = (bf16[256,1792]{1,0:T(8,128)(2,1)S(1)}, bf16[256,1792]{1,0:T(8,128)(2,1)}, u32[]{:S(2)}) copy-start(bf16[256,1792]{1,0:T(8,128)(2,1)} %copy-done.2) | copy-start | bytes 2752516
  99.2 27.3 %all-to-all-start.3 = ((bf16[32,8,112]{2,1,0:T(8,128)(2,1)}), bf16[32,8,112]{2,1,0:T(8,128)(2,1)S(1)}, u32[]{:S(2)}, u32[]{:S(2)}) async-start(bf16[32,8,112]{2,1,0:T(8,128)(2,1)} %bitcast.16), calls=%async_computation.3 | async-start | bytes 131072 | tf_op jit(solution)/shard_map/all_to_all | solution.py:176
  123.5 3.1 %copy-start.1 = (bf16[256,128]{1,0:T(8,128)(2,1)S(1)}, bf16[256,128]{1,0:T(8,128)(2,1)}, u32[]{:S(2)}) copy-start(bf16[256,128]{1,0:T(8,128)(2,1)} %get-tuple-element.47.refs_1_) | copy-start | bytes 196612

commit v5 on v4

--- a/solution.py
+++ b/solution.py
@@ -9,11 +9,6 @@
 def swapped(block, mask):
     count = lax.axis_size("node")
     return lax.ppermute(block, "node", [(at, at ^ mask) for at in range(count)])
-
-
-def swapped_parts(block, mask, axis):
-    parts = [swapped(part, mask) for part in jnp.split(block, 2, axis=axis)]
-    return jnp.concatenate(parts, axis=axis)
 
 
 def dot(lhs, rhs, lhs_dim, rhs_dim):
@@ -198,18 +193,21 @@
     pre = pre.reshape(node_count // 2, 2, capacity, 2 * hidden).transpose(1, 0, 2, 3)
     pre = pre.reshape(2, half, 2 * hidden)
     pre, away = by_core(core, pre[0], pre[1])
-    pre = pre + swapped_parts(away.astype(jnp.bfloat16), 1, 1).astype(jnp.float32)
-    arrived, pre = lax.optimization_barrier((arrived, pre))
+    away = away.astype(jnp.bfloat16)
+    arrived, pre, away = lax.optimization_barrier((arrived, pre, away))
 
     (copies,) = call(
         lambda *refs: spread_kernel(capacity, *refs),
         [bf16(local_count, 2 * piece, half)],
         arrived,
     )
-    copies, own_down, gate_up = lax.optimization_barrier((copies, down_weight_t, gate_up))
+    copies, own_down, gate_up, away = lax.optimization_barrier(
+        (copies, down_weight_t, gate_up, away)
+    )
     grads_in = lax.all_to_all(copies, "local", split_axis=0, concat_axis=0, tiled=True)
     other_down = swapped(own_down, 1)
     other_gate_up = swapped(gate_up, 1)
+    pre = pre + swapped(away, 1).astype(jnp.float32)
     other_down, pre = lax.optimization_barrier((other_down, pre))
     pre = pre + swapped(pre.astype(jnp.bfloat16), 2).astype(jnp.float32)
     by_piece = lambda block: block.reshape(local_count, piece, block.shape[1])

time: 128 us -> 127 us (level)
  starting transfers between devices: 86.6 us -> 84.9 us
    ppermute x8 -> x7, starting transfers between devices: 19.7 us -> 15.7 us  [swapped(): return lax.ppermute(block, 'node', [(at, at ^ mask) for at in range(count)])]
    all_to_all x1, waiting for transfers between devices: 6.22 us -> 2.33 us  [per_device(): lax.all_to_all(copies, 'local', split_axis=0, concat_axis=0, tiled=True)]
    all_to_all x2, waiting for transfers between devices: 2.06 us -> 5.32 us  [across_chips(): lax.all_to_all(block, 'node', split_axis=0, concat_axis=0, tiled=True, ax...]
    ppermute x8 -> x7, waiting for transfers between devices: 3.86 us -> 4.97 us  [swapped(): return lax.ppermute(block, 'node', [(at, at ^ mask) for at in range(count)])]
  transfers between devices with their start and end apart: 12 -> 11, of which waited for: 6 -> 6; matrix products, arithmetic and copies ran while one was open for 8% -> 8% of each run, Pallas kernels for 1% -> 1%
where the time goes in v5:
time: 127 us
  starting transfers between devices  84.9 us (67%)
  waiting for transfers between devices  22.4 us (18%)
  Pallas kernels  6.83 us (5%)
  matrix products  5.76 us (5%)
  local copies, waits for them, and re-layouts  3.44 us (3%)
  other arithmetic  2.28 us (2%)
    all_to_all x2, starting transfers between devices, across_chips(): lax.all_to_all(block, 'node', split_axis=0, concat_axis=0, tiled=True, ax...  57.1 us
    ppermute x7, starting transfers between devices, swapped(): return lax.ppermute(block, 'node', [(at, at ^ mask) for at in range(count)])  15.7 us
    all_to_all x1, waiting for transfers between devices, per_device(): lax.all_to_all(partial_value, 'local', split_axis=0, concat_axis=0, tiled...  9.82 us
    all_to_all x1, starting transfers between devices, per_device(): lax.all_to_all(copies, 'local', split_axis=0, concat_axis=0, tiled=True)  7.21 us
    pallas_call x6, Pallas kernels, call(): pl.pallas_call(kernel, out_shape=outs, in_specs=[pl.BlockSpec(memory_spac...  6.83 us
    dot_general x6, matrix products, dot(): lax.dot_general(lhs, rhs, (((lhs_dim,), (rhs_dim,)), ((), ())), preferred...  5.76 us
    all_to_all x2, waiting for transfers between devices, across_chips(): lax.all_to_all(block, 'node', split_axis=0, concat_axis=0, tiled=True, ax...  5.32 us
    ppermute x7, waiting for transfers between devices, swapped(): return lax.ppermute(block, 'node', [(at, at ^ mask) for at in range(count)])  4.97 us
  transfers between devices with their start and end apart: 11, of which 6 were waited for; matrix products, arithmetic and copies ran while one was open for 8% of the time, Pallas kernels for 1%

profile of v5, /device:TPU:32, one launch (start us, length us, event | category | flops | bytes accessed | tf_op | source)
XLA Modules:
  0.0 126.6 jit_solution(3926622268446492475)
XLA Ops:
  0.6 1.9 %shard_map.120 = (bf16[256,112]{1,0:T(8,128)(2,1)}, bf16[256,128]{1,0:T(8,128)(2,1)}) custom-call(s32[8,128]{1,0:T(8,128)} %bitcast.47, s32[8,128]{1,0:T(8,128)} %bitcast.48, s32[8,128]{1,0:T(8,128)} %bitcast.49, f32[8,128]{1,0:T(8,128)} %bitcast.50, bf16[4,112,128]{2,1,0:T(8,128)(2,1)} %bitcast.44), custom_call_target="tpu_custom_call" | custom-call | bytes 253952 | tf_op jit(solution)/shard_map/pallas_call | solution.py:24
  2.6 34.5 %all-to-all-start = ((bf16[32,8,112]{2,1,0:T(8,128)(2,1)}), bf16[32,8,112]{2,1,0:T(8,128)(2,1)S(1)}, u32[]{:S(2)}, u32[]{:S(2)}) async-start(bf16[32,8,112]{2,1,0:T(8,128)(2,1)} %bitcast.46), calls=%async_computation | async-start | bytes 131072 | tf_op jit(solution)/shard_map/all_to_all | solution.py:171
  37.1 0.0 copy-start.4
  37.1 1.7 %reshape.73 = bf16[256,1792]{1,0:T(8,128)(2,1)S(1)} reshape(bf16[64,4,1792]{2,1,0:T(4,128)(2,1)} %param.14) | data formatting | bytes 1835008 | tf_op jit(solution)/shard_map/reshape | solution.py:187
  38.8 0.0 copy-start.2
  38.9 0.0 copy-done.4
  38.9 0.0 copy-start.5
  38.9 0.1 constant_dynamic-update-slice_fusion.1
  39.0 1.3 copy-done.5
  40.2 0.1 constant_dynamic-update-slice_fusion
  40.3 0.0 copy-done.2
  40.3 0.4 fusion.7
  40.8 0.1 reshape.74
  41.0 3.3 %all-to-all-done = bf16[32,8,112]{2,1,0:T(8,128)(2,1)S(1)} async-done(((bf16[32,8,112]{2,1,0:T(8,128)(2,1)}), bf16[32,8,112]{2,1,0:T(8,128)(2,1)S(1)}, u32[]{:S(2)}, u32[]{:S(2)}) %all-to-all-start) | async-done | bytes 57376 | tf_op jit(solution)/shard_map/all_to_all | solution.py:171
  44.3 1.2 shard_map.121
  45.5 0.0 copy-start
  45.5 7.2 %all-to-all-start.1 = ((bf16[16,224,128]{2,1,0:T(8,128)(2,1)}), bf16[16,224,128]{2,1,0:T(8,128)(2,1)}, u32[]{:S(2)}, u32[]{:S(2)}) async-start(bf16[16,224,128]{2,1,0:T(8,128)(2,1)} %shard_map.121), calls=%async_computation.1 | async-start | bytes 1835008 | tf_op jit(solution)/shard_map/all_to_all | solution.py:207
  52.8 0.0 copy-done
  52.8 1.9 %collective-permute-start = (bf16[1792,128]{1,0:T(8,128)(2,1)S(1)}, bf16[1792,128]{1,0:T(8,128)(2,1)S(1)}, u32[]{:S(2)}, u32[]{:S(2)}) collective-permute-start(bf16[1792,128]{1,0:T(8,128)(2,1)S(1)} %copy-done), channel_id=1, source_target_pairs={{0,16},{16,0},{32,48},{48,32},{64,80},{80,64},{96,112},{112,96},{1... | collective-permute-start | bytes 1376264 | tf_op jit(solution)/shard_map/ppermute | solution.py:11
  54.7 2.4 %collective-permute-start.1 = (bf16[128,256]{1,0:T(8,128)(2,1)S(1)}, bf16[128,256]{1,0:T(8,128)(2,1)S(1)}, u32[]{:S(2)}, u32[]{:S(2)}) collective-permute-start(bf16[128,256]{1,0:T(8,128)(2,1)S(1)} %convert_element_type.28), channel_id=1, source_target_pairs={{0,16},{16,0},{32,48},{48,32},{64,80},{80,64},{96,112},{112,96},{1... | collective-permute-start | bytes 196616 | tf_op jit(solution)/shard_map/ppermute | solution.py:11
  57.1 1.9 %collective-permute-start.4 = (bf16[1792,256]{1,0:T(8,128)(2,1)S(1)}, bf16[1792,256]{1,0:T(8,128)(2,1)S(1)}, u32[]{:S(2)}, u32[]{:S(2)}) collective-permute-start(bf16[1792,256]{1,0:T(8,128)(2,1)S(1)} %constant_dynamic-update-slice_fusion), channel_id=1, source_target_pairs={{0,16},{16,0},{32,48},{48,32},{64,80},{80,64},{96,112},{112,96},{1... | collective-permute-start | bytes 2752520 | tf_op jit(solution)/shard_map/ppermute | solution.py:11
  59.0 0.0 collective-permute-done.1
  59.1 0.0 collective-permute-done
  59.1 2.4 %collective-permute-start.2 = (bf16[128,256]{1,0:T(8,128)(2,1)S(1)}, bf16[128,256]{1,0:T(8,128)(2,1)S(1)}, u32[]{:S(2)}, u32[]{:S(2)}) collective-permute-start(bf16[128,256]{1,0:T(8,128)(2,1)S(1)} %convert_element_type.30), channel_id=1, source_target_pairs={{0,32},{16,48},{32,0},{48,16},{64,96},{80,112},{96,64},{112,80},{1... | collective-permute-start | bytes 196616 | tf_op jit(solution)/shard_map/ppermute | solution.py:11
  61.6 0.1 shard_map.122
  61.6 3.8 %collective-permute-done.2 = bf16[128,256]{1,0:T(8,128)(2,1)S(1)} collective-permute-done((bf16[128,256]{1,0:T(8,128)(2,1)S(1)}, bf16[128,256]{1,0:T(8,128)(2,1)S(1)}, u32[]{:S(2)}, u32[]{:S(2)}) %collective-permute-start.2) | collective-permute-done | bytes 65568 | tf_op jit(solution)/shard_map/ppermute | solution.py:11
  65.5 2.3 %all-to-all-done.1 = bf16[16,224,128]{2,1,0:T(8,128)(2,1)} async-done(((bf16[16,224,128]{2,1,0:T(8,128)(2,1)}), bf16[16,224,128]{2,1,0:T(8,128)(2,1)}, u32[]{:S(2)}, u32[]{:S(2)}) %all-to-all-start.1) | async-done | bytes 917536 | tf_op jit(solution)/shard_map/all_to_all | solution.py:207
  67.8 1.6 %fusion.6 = (bf16[128,128]{1,0:T(8,128)(2,1)S(1)}, f32[128,128]{1,0:T(8,128)S(1)}) fusion(bf16[16,224,128]{2,1,0:T(8,128)(2,1)} %all-to-all-done.1, bf16[16,224,128]{2,1,0:T(8,128)(2,1)S(1)} %shard_map.122), kind=kOutput, calls=%fused_computation.22 | convolution fusion | flops 117456896 | bytes 1933312 | tf_op jit(solution)/shard_map/dot_general | solution.py:15
  69.5 2.7 %collective-permute-start.3 = (bf16[128,128]{1,0:T(8,128)(2,1)S(1)}, bf16[128,128]{1,0:T(8,128)(2,1)S(1)}, u32[]{:S(2)}, u32[]{:S(2)}) collective-permute-start(bf16[128,128]{1,0:T(8,128)(2,1)S(1)} %get-tuple-element.58), channel_id=1, source_target_pairs={{0,32},{16,48},{32,0},{48,16},{64,96},{80,112},{96,64},{112,80},{1... | collective-permute-start | bytes 98312 | tf_op jit(solution)/shard_map/ppermute | solution.py:11
  72.2 2.0 %broadcast_select_fusion = (bf16[16,1,112,128]{3,2,1,0:T(8,128)(2,1)S(1)}, bf16[16,1,112,128]{3,2,1,0:T(8,128)(2,1)}) fusion(pred[]{:T(512)S(6)} %eq.4, bf16[16,2,112,128]{3,2,1,0:T(8,128)(2,1)} %bitcast.14), kind=kLoop, calls=%fused_computation.5 | loop fusion | flops 458752 | bytes 1835009 | tf_op jit(solution)/shard_map/jit(_where)/select_n | solution.py:141
  74.2 1.1 collective-permute-done.3.other
  75.3 0.0 collective-permute-done.4
  75.3 1.7 %shard_map.123 = (bf16[128,384]{1,0:T(8,128)(2,1)S(1)}, bf16[16,224,128]{2,1,0:T(8,128)(2,1)}) custom-call(s32[1]{0:T(128)} %bitcast.core, f32[128,256]{1,0:T(8,128)S(1)} %convert_add_fusion.pre, f32[128,128]{1,0:T(8,128)S(1)} %get-tuple-element.59.part, bf16[128,128]{1,0:T(8,128)(2,1)S(1)} %collective-permute-done.3.other, ...), custom_call_target="tpu_custom_call" | custom-call | bytes 3080196 | tf_op jit(solution)/shard_map/pallas_call | solution.py:24
  77.0 4.9 %all-to-all-start.2 = ((bf16[16,224,128]{2,1,0:T(8,128)(2,1)}), bf16[16,224,128]{2,1,0:T(8,128)(2,1)S(1)}, u32[]{:S(2)}, u32[]{:S(2)}) async-start(bf16[16,224,128]{2,1,0:T(8,128)(2,1)} %get-tuple-element.47), calls=%async_computation.2 | async-start | bytes 1835008 | tf_op jit(solution)/shard_map/all_to_all | solution.py:242
  81.9 1.9 %collective-permute-start.6 = (bf16[1792,128]{1,0:T(8,128)(2,1)}, bf16[1792,128]{1,0:T(8,128)(2,1)S(1)}, u32[]{:S(2)}, u32[]{:S(2)}) collective-permute-start(bf16[1792,128]{1,0:T(8,128)(2,1)} %bitcast.15), channel_id=1, source_target_pairs={{0,16},{16,0},{32,48},{48,32},{64,80},{80,64},{96,112},{112,96},{1... | collective-permute-start | bytes 1376264 | tf_op jit(solution)/shard_map/ppermute | solution.py:11
  83.8 2.4 %collective-permute-start.5 = (bf16[128,384]{1,0:T(8,128)(2,1)S(1)}, bf16[128,384]{1,0:T(8,128)(2,1)S(1)}, u32[]{:S(2)}, u32[]{:S(2)}) collective-permute-start(bf16[128,384]{1,0:T(8,128)(2,1)S(1)} %get-tuple-element.48), channel_id=1, source_target_pairs={{0,16},{16,0},{32,48},{48,32},{64,80},{80,64},{96,112},{112,96},{1... | collective-permute-start | bytes 294920 | tf_op jit(solution)/shard_map/ppermute | solution.py:11
  86.2 0.3 fusion.4
  86.5 9.8 %all-to-all-done.2.refs_0_ = bf16[16,224,128]{2,1,0:T(8,128)(2,1)S(1)} async-done(((bf16[16,224,128]{2,1,0:T(8,128)(2,1)}), bf16[16,224,128]{2,1,0:T(8,128)(2,1)S(1)}, u32[]{:S(2)}, u32[]{:S(2)}) %all-to-all-start.2) | async-done | bytes 917536 | tf_op jit(solution)/shard_map/all_to_all | solution.py:242
  96.3 1.0 shard_map.124
  97.3 0.0 copy-start.3
  97.3 0.0 collective-permute-done.5
  97.3 0.0 collective-permute-done.6
  97.3 22.6 %all-to-all-start.3 = ((bf16[32,8,112]{2,1,0:T(8,128)(2,1)}), bf16[32,8,112]{2,1,0:T(8,128)(2,1)S(1)}, u32[]{:S(2)}, u32[]{:S(2)}) async-start(bf16[32,8,112]{2,1,0:T(8,128)(2,1)} %bitcast.16), calls=%async_computation.3 | async-start | bytes 131072 | tf_op jit(solution)/shard_map/all_to_all | solution.py:171
  119.9 0.1 pad_maximum_fusion
  120.1 0.1 reshape.82
  120.1 0.0 copy-done.3
  120.1 1.2 convolution_convert_fusion
  121.4 1.2 convolution_convert_fusion.1
  122.6 0.0 copy-start.1
  122.6 1.0 fusion
  123.6 2.0 %all-to-all-done.3 = bf16[32,8,112]{2,1,0:T(8,128)(2,1)S(1)} async-done(((bf16[32,8,112]{2,1,0:T(8,128)(2,1)}), bf16[32,8,112]{2,1,0:T(8,128)(2,1)S(1)}, u32[]{:S(2)}, u32[]{:S(2)}) %all-to-all-start.3) | async-done | bytes 57376 | tf_op jit(solution)/shard_map/all_to_all | solution.py:171
  125.7 0.0 copy-done.1
  125.7 0.9 shard_map.125
  (11 shorter events, 0.3 us)
Async XLA Ops:
  2.6 41.7 %all-to-all-start = ((bf16[32,8,112]{2,1,0:T(8,128)(2,1)}), bf16[32,8,112]{2,1,0:T(8,128)(2,1)S(1)}, u32[]{:S(2)}, u32[]{:S(2)}) async-start(bf16[32,8,112]{2,1,0:T(8,128)(2,1)} %bitcast.46), calls=%async_computation | async-start | bytes 131072 | tf_op jit(solution)/shard_map/all_to_all | solution.py:171
  37.1 1.7 %copy-start.4 = (bf16[1792,128]{1,0:T(8,128)(2,1)S(1)}, bf16[1792,128]{1,0:T(8,128)(2,1)}, u32[]{:S(2)}) copy-start(bf16[1792,128]{1,0:T(8,128)(2,1)} %param.15) | copy-start | bytes 1376260
  38.8 1.5 %copy-start.2 = (bf16[256,1792]{1,0:T(8,128)(2,1)}, bf16[256,1792]{1,0:T(8,128)(2,1)S(1)}, u32[]{:S(2)}) copy-start(bf16[256,1792]{1,0:T(8,128)(2,1)S(1)} %reshape.73) | copy-start | bytes 2752516
  38.9 1.4 %copy-start.5 = (bf16[1792,128]{1,0:T(8,128)(2,1)S(1)}, bf16[1792,128]{1,0:T(8,128)(2,1)}, u32[]{:S(2)}) copy-start(bf16[1792,128]{1,0:T(8,128)(2,1)} %param.16) | copy-start | bytes 1376260
  45.5 7.2 %copy-start = (bf16[1792,128]{1,0:T(8,128)(2,1)S(1)}, bf16[1792,128]{1,0:T(8,128)(2,1)}, u32[]{:S(2)}) copy-start(bf16[1792,128]{1,0:T(8,128)(2,1)} %param.17) | copy-start | bytes 1376260
  45.5 22.3 %all-to-all-start.1 = ((bf16[16,224,128]{2,1,0:T(8,128)(2,1)}), bf16[16,224,128]{2,1,0:T(8,128)(2,1)}, u32[]{:S(2)}, u32[]{:S(2)}) async-start(bf16[16,224,128]{2,1,0:T(8,128)(2,1)} %shard_map.121), calls=%async_computation.1 | async-start | bytes 1835008 | tf_op jit(solution)/shard_map/all_to_all | solution.py:207
  52.8 6.3 %collective-permute-start = (bf16[1792,128]{1,0:T(8,128)(2,1)S(1)}, bf16[1792,128]{1,0:T(8,128)(2,1)S(1)}, u32[]{:S(2)}, u32[]{:S(2)}) collective-permute-start(bf16[1792,128]{1,0:T(8,128)(2,1)S(1)} %copy-done), channel_id=1, source_target_pairs={{0,16},{16,0},{32,48},{48,32},{64,80},{80,64},{96,112},{112,96},{1... | collective-permute-start | bytes 1376264 | tf_op jit(solution)/shard_map/ppermute | solution.py:11
  54.7 4.3 %collective-permute-start.1 = (bf16[128,256]{1,0:T(8,128)(2,1)S(1)}, bf16[128,256]{1,0:T(8,128)(2,1)S(1)}, u32[]{:S(2)}, u32[]{:S(2)}) collective-permute-start(bf16[128,256]{1,0:T(8,128)(2,1)S(1)} %convert_element_type.28), channel_id=1, source_target_pairs={{0,16},{16,0},{32,48},{48,32},{64,80},{80,64},{96,112},{112,96},{1... | collective-permute-start | bytes 196616 | tf_op jit(solution)/shard_map/ppermute | solution.py:11
  57.1 18.2 %collective-permute-start.4 = (bf16[1792,256]{1,0:T(8,128)(2,1)S(1)}, bf16[1792,256]{1,0:T(8,128)(2,1)S(1)}, u32[]{:S(2)}, u32[]{:S(2)}) collective-permute-start(bf16[1792,256]{1,0:T(8,128)(2,1)S(1)} %constant_dynamic-update-slice_fusion), channel_id=1, source_target_pairs={{0,16},{16,0},{32,48},{48,32},{64,80},{80,64},{96,112},{112,96},{1... | collective-permute-start | bytes 2752520 | tf_op jit(solution)/shard_map/ppermute | solution.py:11
  59.1 6.4 %collective-permute-start.2 = (bf16[128,256]{1,0:T(8,128)(2,1)S(1)}, bf16[128,256]{1,0:T(8,128)(2,1)S(1)}, u32[]{:S(2)}, u32[]{:S(2)}) collective-permute-start(bf16[128,256]{1,0:T(8,128)(2,1)S(1)} %convert_element_type.30), channel_id=1, source_target_pairs={{0,32},{16,48},{32,0},{48,16},{64,96},{80,112},{96,64},{112,80},{1... | collective-permute-start | bytes 196616 | tf_op jit(solution)/shard_map/ppermute | solution.py:11
  69.5 5.8 %collective-permute-start.3 = (bf16[128,128]{1,0:T(8,128)(2,1)S(1)}, bf16[128,128]{1,0:T(8,128)(2,1)S(1)}, u32[]{:S(2)}, u32[]{:S(2)}) collective-permute-start(bf16[128,128]{1,0:T(8,128)(2,1)S(1)} %get-tuple-element.58), channel_id=1, source_target_pairs={{0,32},{16,48},{32,0},{48,16},{64,96},{80,112},{96,64},{112,80},{1... | collective-permute-start | bytes 98312 | tf_op jit(solution)/shard_map/ppermute | solution.py:11
  77.0 19.3 %all-to-all-start.2 = ((bf16[16,224,128]{2,1,0:T(8,128)(2,1)}), bf16[16,224,128]{2,1,0:T(8,128)(2,1)S(1)}, u32[]{:S(2)}, u32[]{:S(2)}) async-start(bf16[16,224,128]{2,1,0:T(8,128)(2,1)} %get-tuple-element.47), calls=%async_computation.2 | async-start | bytes 1835008 | tf_op jit(solution)/shard_map/all_to_all | solution.py:242
  81.9 15.4 %collective-permute-start.6 = (bf16[1792,128]{1,0:T(8,128)(2,1)}, bf16[1792,128]{1,0:T(8,128)(2,1)S(1)}, u32[]{:S(2)}, u32[]{:S(2)}) collective-permute-start(bf16[1792,128]{1,0:T(8,128)(2,1)} %bitcast.15), channel_id=1, source_target_pairs={{0,16},{16,0},{32,48},{48,32},{64,80},{80,64},{96,112},{112,96},{1... | collective-permute-start | bytes 1376264 | tf_op jit(solution)/shard_map/ppermute | solution.py:11
  83.8 13.5 %collective-permute-start.5 = (bf16[128,384]{1,0:T(8,128)(2,1)S(1)}, bf16[128,384]{1,0:T(8,128)(2,1)S(1)}, u32[]{:S(2)}, u32[]{:S(2)}) collective-permute-start(bf16[128,384]{1,0:T(8,128)(2,1)S(1)} %get-tuple-element.48), channel_id=1, source_target_pairs={{0,16},{16,0},{32,48},{48,32},{64,80},{80,64},{96,112},{112,96},{1... | collective-permute-start | bytes 294920 | tf_op jit(solution)/shard_map/ppermute | solution.py:11
  97.3 22.9 %copy-start.3 = (bf16[256,1792]{1,0:T(8,128)(2,1)S(1)}, bf16[256,1792]{1,0:T(8,128)(2,1)}, u32[]{:S(2)}) copy-start(bf16[256,1792]{1,0:T(8,128)(2,1)} %copy-done.2) | copy-start | bytes 2752516
  97.3 28.4 %all-to-all-start.3 = ((bf16[32,8,112]{2,1,0:T(8,128)(2,1)}), bf16[32,8,112]{2,1,0:T(8,128)(2,1)S(1)}, u32[]{:S(2)}, u32[]{:S(2)}) async-start(bf16[32,8,112]{2,1,0:T(8,128)(2,1)} %bitcast.16), calls=%async_computation.3 | async-start | bytes 131072 | tf_op jit(solution)/shard_map/all_to_all | solution.py:171
  122.6 3.1 %copy-start.1 = (bf16[256,128]{1,0:T(8,128)(2,1)S(1)}, bf16[256,128]{1,0:T(8,128)(2,1)}, u32[]{:S(2)}) copy-start(bf16[256,128]{1,0:T(8,128)(2,1)} %get-tuple-element.51.refs_1_) | copy-start | bytes 196612

commit v6 on v5

--- a/solution.py
+++ b/solution.py
@@ -96,11 +96,12 @@
         out[at, pl.ds(there, own.shape[1]), :] = other[at]
 
 
-def hidden_kernel(core, pre, part, other, gate_up, other_gate_up, acts, out):
+def hidden_kernel(core, pre, other_pre, part, other, gate_up, other_gate_up, acts, out):
     piece = gate_up.shape[1]
     hidden = part.shape[1]
-    pre_gate = pre[:, :hidden]
-    pre_up = pre[:, hidden:]
+    joined = pre[...] + other_pre[...].astype(jnp.float32)
+    pre_gate = joined[:, :hidden]
+    pre_up = joined[:, hidden:]
     grad_act = part[...] + other[...].astype(jnp.float32)
     gate_sig = jax.nn.sigmoid(pre_gate)
     silu_gate = pre_gate * gate_sig
@@ -209,7 +210,7 @@
     other_gate_up = swapped(gate_up, 1)
     pre = pre + swapped(away, 1).astype(jnp.float32)
     other_down, pre = lax.optimization_barrier((other_down, pre))
-    pre = pre + swapped(pre.astype(jnp.bfloat16), 2).astype(jnp.float32)
+    other_pre = swapped(pre.astype(jnp.bfloat16), 2)
     by_piece = lambda block: block.reshape(local_count, piece, block.shape[1])
     (down_pair,) = call(
         pair_kernel,
@@ -228,6 +229,7 @@
         [bf16(half, 3 * hidden), bf16(local_count, 2 * piece, half)],
         core.reshape(1),
         pre,
+        other_pre,
         part,
         other,
         by_piece(gate_up),

time: 127 us -> 125 us (0.984)
    all_to_all x1, waiting for transfers between devices: 2.33 us -> 4.99 us  [per_device(): lax.all_to_all(copies, 'local', split_axis=0, concat_axis=0, tiled=True)]
    ppermute x7, waiting for transfers between devices: 4.97 us -> 2.34 us  [swapped(): return lax.ppermute(block, 'node', [(at, at ^ mask) for at in range(count)])]
where the time goes in v6:
time: 125 us; the launch traced here: 124 us
  starting transfers between devices  83.7 us (67%)
  waiting for transfers between devices  21.6 us (17%)
  Pallas kernels  6.84 us (5%)
  matrix products  5.76 us (5%)
  local copies, waits for them, and re-layouts  3.44 us (3%)
  other arithmetic  2.26 us (2%)
    all_to_all x2, starting transfers between devices, across_chips(): lax.all_to_all(block, 'node', split_axis=0, concat_axis=0, tiled=True, ax...  57.1 us
    ppermute x7, starting transfers between devices, swapped(): return lax.ppermute(block, 'node', [(at, at ^ mask) for at in range(count)])  15.7 us
    all_to_all x1, waiting for transfers between devices, per_device(): lax.all_to_all(partial_value, 'local', split_axis=0, concat_axis=0, tiled...  9.03 us
    all_to_all x1, starting transfers between devices, per_device(): lax.all_to_all(copies, 'local', split_axis=0, concat_axis=0, tiled=True)  7.21 us
    pallas_call x6, Pallas kernels, call(): pl.pallas_call(kernel, out_shape=outs, in_specs=[pl.BlockSpec(memory_spac...  6.84 us
    dot_general x6, matrix products, dot(): lax.dot_general(lhs, rhs, (((lhs_dim,), (rhs_dim,)), ((), ())), preferred...  5.76 us
    all_to_all x2, waiting for transfers between devices, across_chips(): lax.all_to_all(block, 'node', split_axis=0, concat_axis=0, tiled=True, ax...  5.23 us
    all_to_all x1, waiting for transfers between devices, per_device(): lax.all_to_all(copies, 'local', split_axis=0, concat_axis=0, tiled=True)  4.99 us
  transfers between devices with their start and end apart: 11, of which 6 were waited for; matrix products, arithmetic and copies ran while one was open for 8% of the time, Pallas kernels for 1%

profile of v6, /device:TPU:32, one launch (start us, length us, event | category | flops | bytes accessed | tf_op | source)
XLA Modules:
  0.0 124.5 jit_solution(14675415269134694359)
XLA Ops:
  0.6 1.9 %shard_map.120 = (bf16[256,112]{1,0:T(8,128)(2,1)}, bf16[256,128]{1,0:T(8,128)(2,1)}) custom-call(s32[8,128]{1,0:T(8,128)} %bitcast.47, s32[8,128]{1,0:T(8,128)} %bitcast.48, s32[8,128]{1,0:T(8,128)} %bitcast.49, f32[8,128]{1,0:T(8,128)} %bitcast.50, bf16[4,112,128]{2,1,0:T(8,128)(2,1)} %bitcast.44), custom_call_target="tpu_custom_call" | custom-call | bytes 253952 | tf_op jit(solution)/shard_map/pallas_call | solution.py:24
  2.6 34.5 %all-to-all-start = ((bf16[32,8,112]{2,1,0:T(8,128)(2,1)}), bf16[32,8,112]{2,1,0:T(8,128)(2,1)S(1)}, u32[]{:S(2)}, u32[]{:S(2)}) async-start(bf16[32,8,112]{2,1,0:T(8,128)(2,1)} %bitcast.46), calls=%async_computation | async-start | bytes 131072 | tf_op jit(solution)/shard_map/all_to_all | solution.py:172
  37.1 0.0 copy-start.4
  37.1 1.7 %reshape.73 = bf16[256,1792]{1,0:T(8,128)(2,1)S(1)} reshape(bf16[64,4,1792]{2,1,0:T(4,128)(2,1)} %param.14) | data formatting | bytes 1835008 | tf_op jit(solution)/shard_map/reshape | solution.py:188
  38.8 0.0 copy-start.2
  38.9 0.0 copy-done.4
  38.9 0.0 copy-start.5
  38.9 0.1 constant_dynamic-update-slice_fusion.1
  39.0 1.3 %copy-done.5 = bf16[1792,128]{1,0:T(8,128)(2,1)S(1)} copy-done((bf16[1792,128]{1,0:T(8,128)(2,1)S(1)}, bf16[1792,128]{1,0:T(8,128)(2,1)}, u32[]{:S(2)}) %copy-start.5) | copy-done | bytes 458776
  40.2 0.1 constant_dynamic-update-slice_fusion
  40.3 0.0 copy-done.2
  40.3 0.4 fusion.7
  40.8 0.1 reshape.74
  41.0 3.3 %all-to-all-done = bf16[32,8,112]{2,1,0:T(8,128)(2,1)S(1)} async-done(((bf16[32,8,112]{2,1,0:T(8,128)(2,1)}), bf16[32,8,112]{2,1,0:T(8,128)(2,1)S(1)}, u32[]{:S(2)}, u32[]{:S(2)}) %all-to-all-start) | async-done | bytes 57376 | tf_op jit(solution)/shard_map/all_to_all | solution.py:172
  44.3 1.2 shard_map.121
  45.5 0.0 copy-start
  45.5 7.2 %all-to-all-start.1 = ((bf16[16,224,128]{2,1,0:T(8,128)(2,1)}), bf16[16,224,128]{2,1,0:T(8,128)(2,1)}, u32[]{:S(2)}, u32[]{:S(2)}) async-start(bf16[16,224,128]{2,1,0:T(8,128)(2,1)} %shard_map.121), calls=%async_computation.1 | async-start | bytes 1835008 | tf_op jit(solution)/shard_map/all_to_all | solution.py:208
  52.8 0.0 copy-done
  52.8 1.9 %collective-permute-start = (bf16[1792,128]{1,0:T(8,128)(2,1)S(1)}, bf16[1792,128]{1,0:T(8,128)(2,1)S(1)}, u32[]{:S(2)}, u32[]{:S(2)}) collective-permute-start(bf16[1792,128]{1,0:T(8,128)(2,1)S(1)} %copy-done), channel_id=1, source_target_pairs={{0,16},{16,0},{32,48},{48,32},{64,80},{80,64},{96,112},{112,96},{1... | collective-permute-start | bytes 1376264 | tf_op jit(solution)/shard_map/ppermute | solution.py:11
  54.7 2.4 %collective-permute-start.4 = (bf16[1792,256]{1,0:T(8,128)(2,1)S(1)}, bf16[1792,256]{1,0:T(8,128)(2,1)S(1)}, u32[]{:S(2)}, u32[]{:S(2)}) collective-permute-start(bf16[1792,256]{1,0:T(8,128)(2,1)S(1)} %constant_dynamic-update-slice_fusion), channel_id=1, source_target_pairs={{0,16},{16,0},{32,48},{48,32},{64,80},{80,64},{96,112},{112,96},{1... | collective-permute-start | bytes 2752520 | tf_op jit(solution)/shard_map/ppermute | solution.py:11
  57.1 1.9 %collective-permute-start.1 = (bf16[128,256]{1,0:T(8,128)(2,1)S(1)}, bf16[128,256]{1,0:T(8,128)(2,1)S(1)}, u32[]{:S(2)}, u32[]{:S(2)}) collective-permute-start(bf16[128,256]{1,0:T(8,128)(2,1)S(1)} %convert_element_type.25), channel_id=1, source_target_pairs={{0,16},{16,0},{32,48},{48,32},{64,80},{80,64},{96,112},{112,96},{1... | collective-permute-start | bytes 196616 | tf_op jit(solution)/shard_map/ppermute | solution.py:11
  59.0 1.2 collective-permute-done.1
  60.3 0.0 collective-permute-done
  60.3 2.4 %collective-permute-start.2 = (bf16[128,256]{1,0:T(8,128)(2,1)S(1)}, bf16[128,256]{1,0:T(8,128)(2,1)S(1)}, u32[]{:S(2)}, u32[]{:S(2)}) collective-permute-start(bf16[128,256]{1,0:T(8,128)(2,1)S(1)} %convert_element_type.27), channel_id=1, source_target_pairs={{0,32},{16,48},{32,0},{48,16},{64,96},{80,112},{96,64},{112,80},{1... | collective-permute-start | bytes 196616 | tf_op jit(solution)/shard_map/ppermute | solution.py:11
  62.8 0.1 shard_map.122
  62.8 5.0 %all-to-all-done.1 = bf16[16,224,128]{2,1,0:T(8,128)(2,1)} async-done(((bf16[16,224,128]{2,1,0:T(8,128)(2,1)}), bf16[16,224,128]{2,1,0:T(8,128)(2,1)}, u32[]{:S(2)}, u32[]{:S(2)}) %all-to-all-start.1) | async-done | bytes 917536 | tf_op jit(solution)/shard_map/all_to_all | solution.py:208
  67.8 1.6 %fusion.6 = (bf16[128,128]{1,0:T(8,128)(2,1)S(1)}, f32[128,128]{1,0:T(8,128)S(1)}) fusion(bf16[16,224,128]{2,1,0:T(8,128)(2,1)} %all-to-all-done.1, bf16[16,224,128]{2,1,0:T(8,128)(2,1)S(1)} %shard_map.122), kind=kOutput, calls=%fused_computation.21 | convolution fusion | flops 117456896 | bytes 1933312 | tf_op jit(solution)/shard_map/dot_general | solution.py:15
  69.5 2.7 %collective-permute-start.3 = (bf16[128,128]{1,0:T(8,128)(2,1)S(1)}, bf16[128,128]{1,0:T(8,128)(2,1)S(1)}, u32[]{:S(2)}, u32[]{:S(2)}) collective-permute-start(bf16[128,128]{1,0:T(8,128)(2,1)S(1)} %get-tuple-element.58), channel_id=1, source_target_pairs={{0,32},{16,48},{32,0},{48,16},{64,96},{80,112},{96,64},{112,80},{1... | collective-permute-start | bytes 98312 | tf_op jit(solution)/shard_map/ppermute | solution.py:11
  72.2 2.0 %broadcast_select_fusion = (bf16[16,1,112,128]{3,2,1,0:T(8,128)(2,1)S(1)}, bf16[16,1,112,128]{3,2,1,0:T(8,128)(2,1)}) fusion(pred[]{:T(512)S(6)} %eq.4, bf16[16,2,112,128]{3,2,1,0:T(8,128)(2,1)} %bitcast.14), kind=kLoop, calls=%fused_computation.5 | loop fusion | flops 458752 | bytes 1835009 | tf_op jit(solution)/shard_map/jit(_where)/select_n | solution.py:142
  74.2 0.0 collective-permute-done.2.other_pre
  74.2 1.1 collective-permute-done.3.other
  75.3 0.0 collective-permute-done.4
  75.3 1.7 %shard_map.123 = (bf16[128,384]{1,0:T(8,128)(2,1)S(1)}, bf16[16,224,128]{2,1,0:T(8,128)(2,1)}) custom-call(s32[1]{0:T(128)} %bitcast.core, f32[128,256]{1,0:T(8,128)S(1)} %convert_add_fusion.pre, bf16[128,256]{1,0:T(8,128)(2,1)S(1)} %collective-permute-done.2.other_pre, f32[128,128]{1,0:T(8,128)S(1)} %get-tuple-element.59.part, ...), custom_call_target="tpu_custom_call" | custom-call | bytes 3145732 | tf_op jit(solution)/shard_map/pallas_call | solution.py:24
  77.0 3.6 %all-to-all-start.2 = ((bf16[16,224,128]{2,1,0:T(8,128)(2,1)}), bf16[16,224,128]{2,1,0:T(8,128)(2,1)S(1)}, u32[]{:S(2)}, u32[]{:S(2)}) async-start(bf16[16,224,128]{2,1,0:T(8,128)(2,1)} %get-tuple-element.47), calls=%async_computation.2 | async-start | bytes 1835008 | tf_op jit(solution)/shard_map/all_to_all | solution.py:244
  80.7 1.9 %collective-permute-start.6 = (bf16[1792,128]{1,0:T(8,128)(2,1)}, bf16[1792,128]{1,0:T(8,128)(2,1)S(1)}, u32[]{:S(2)}, u32[]{:S(2)}) collective-permute-start(bf16[1792,128]{1,0:T(8,128)(2,1)} %bitcast.15), channel_id=1, source_target_pairs={{0,16},{16,0},{32,48},{48,32},{64,80},{80,64},{96,112},{112,96},{1... | collective-permute-start | bytes 1376264 | tf_op jit(solution)/shard_map/ppermute | solution.py:11
  82.6 2.4 %collective-permute-start.5 = (bf16[128,384]{1,0:T(8,128)(2,1)S(1)}, bf16[128,384]{1,0:T(8,128)(2,1)S(1)}, u32[]{:S(2)}, u32[]{:S(2)}) collective-permute-start(bf16[128,384]{1,0:T(8,128)(2,1)S(1)} %get-tuple-element.48), channel_id=1, source_target_pairs={{0,16},{16,0},{32,48},{48,32},{64,80},{80,64},{96,112},{112,96},{1... | collective-permute-start | bytes 294920 | tf_op jit(solution)/shard_map/ppermute | solution.py:11
  85.0 0.3 fusion.4
  85.3 9.0 %all-to-all-done.2.refs_0_ = bf16[16,224,128]{2,1,0:T(8,128)(2,1)S(1)} async-done(((bf16[16,224,128]{2,1,0:T(8,128)(2,1)}), bf16[16,224,128]{2,1,0:T(8,128)(2,1)S(1)}, u32[]{:S(2)}, u32[]{:S(2)}) %all-to-all-start.2) | async-done | bytes 917536 | tf_op jit(solution)/shard_map/all_to_all | solution.py:244
  94.3 1.0 shard_map.124
  95.2 0.0 copy-start.3
  95.2 0.0 collective-permute-done.5
  95.2 0.0 collective-permute-done.6
  95.2 22.6 %all-to-all-start.3 = ((bf16[32,8,112]{2,1,0:T(8,128)(2,1)}), bf16[32,8,112]{2,1,0:T(8,128)(2,1)S(1)}, u32[]{:S(2)}, u32[]{:S(2)}) async-start(bf16[32,8,112]{2,1,0:T(8,128)(2,1)} %bitcast.16), calls=%async_computation.3 | async-start | bytes 131072 | tf_op jit(solution)/shard_map/all_to_all | solution.py:172
  117.9 0.1 pad_maximum_fusion
  118.1 0.1 reshape.82
  118.1 0.0 copy-done.3
  118.1 1.2 convolution_convert_fusion
  119.3 1.2 convolution_convert_fusion.1
  120.6 0.0 copy-start.1
  120.6 1.0 fusion
  121.6 2.0 %all-to-all-done.3 = bf16[32,8,112]{2,1,0:T(8,128)(2,1)S(1)} async-done(((bf16[32,8,112]{2,1,0:T(8,128)(2,1)}), bf16[32,8,112]{2,1,0:T(8,128)(2,1)S(1)}, u32[]{:S(2)}, u32[]{:S(2)}) %all-to-all-start.3) | async-done | bytes 57376 | tf_op jit(solution)/shard_map/all_to_all | solution.py:172
  123.6 0.0 copy-done.1
  123.6 0.9 shard_map.125
  (10 shorter events, 0.3 us)
Async XLA Ops:
  2.6 41.7 %all-to-all-start = ((bf16[32,8,112]{2,1,0:T(8,128)(2,1)}), bf16[32,8,112]{2,1,0:T(8,128)(2,1)S(1)}, u32[]{:S(2)}, u32[]{:S(2)}) async-start(bf16[32,8,112]{2,1,0:T(8,128)(2,1)} %bitcast.46), calls=%async_computation | async-start | bytes 131072 | tf_op jit(solution)/shard_map/all_to_all | solution.py:172
  37.1 1.7 %copy-start.4 = (bf16[1792,128]{1,0:T(8,128)(2,1)S(1)}, bf16[1792,128]{1,0:T(8,128)(2,1)}, u32[]{:S(2)}) copy-start(bf16[1792,128]{1,0:T(8,128)(2,1)} %param.15) | copy-start | bytes 1376260
  38.8 1.5 %copy-start.2 = (bf16[256,1792]{1,0:T(8,128)(2,1)}, bf16[256,1792]{1,0:T(8,128)(2,1)S(1)}, u32[]{:S(2)}) copy-start(bf16[256,1792]{1,0:T(8,128)(2,1)S(1)} %reshape.73) | copy-start | bytes 2752516
  38.9 1.4 %copy-start.5 = (bf16[1792,128]{1,0:T(8,128)(2,1)S(1)}, bf16[1792,128]{1,0:T(8,128)(2,1)}, u32[]{:S(2)}) copy-start(bf16[1792,128]{1,0:T(8,128)(2,1)} %param.16) | copy-start | bytes 1376260
  45.5 7.2 %copy-start = (bf16[1792,128]{1,0:T(8,128)(2,1)S(1)}, bf16[1792,128]{1,0:T(8,128)(2,1)}, u32[]{:S(2)}) copy-start(bf16[1792,128]{1,0:T(8,128)(2,1)} %param.17) | copy-start | bytes 1376260
  45.5 22.3 %all-to-all-start.1 = ((bf16[16,224,128]{2,1,0:T(8,128)(2,1)}), bf16[16,224,128]{2,1,0:T(8,128)(2,1)}, u32[]{:S(2)}, u32[]{:S(2)}) async-start(bf16[16,224,128]{2,1,0:T(8,128)(2,1)} %shard_map.121), calls=%async_computation.1 | async-start | bytes 1835008 | tf_op jit(solution)/shard_map/all_to_all | solution.py:208
  52.8 7.5 %collective-permute-start = (bf16[1792,128]{1,0:T(8,128)(2,1)S(1)}, bf16[1792,128]{1,0:T(8,128)(2,1)S(1)}, u32[]{:S(2)}, u32[]{:S(2)}) collective-permute-start(bf16[1792,128]{1,0:T(8,128)(2,1)S(1)} %copy-done), channel_id=1, source_target_pairs={{0,16},{16,0},{32,48},{48,32},{64,80},{80,64},{96,112},{112,96},{1... | collective-permute-start | bytes 1376264 | tf_op jit(solution)/shard_map/ppermute | solution.py:11
  54.7 20.6 %collective-permute-start.4 = (bf16[1792,256]{1,0:T(8,128)(2,1)S(1)}, bf16[1792,256]{1,0:T(8,128)(2,1)S(1)}, u32[]{:S(2)}, u32[]{:S(2)}) collective-permute-start(bf16[1792,256]{1,0:T(8,128)(2,1)S(1)} %constant_dynamic-update-slice_fusion), channel_id=1, source_target_pairs={{0,16},{16,0},{32,48},{48,32},{64,80},{80,64},{96,112},{112,96},{1... | collective-permute-start | bytes 2752520 | tf_op jit(solution)/shard_map/ppermute | solution.py:11
  57.1 3.1 %collective-permute-start.1 = (bf16[128,256]{1,0:T(8,128)(2,1)S(1)}, bf16[128,256]{1,0:T(8,128)(2,1)S(1)}, u32[]{:S(2)}, u32[]{:S(2)}) collective-permute-start(bf16[128,256]{1,0:T(8,128)(2,1)S(1)} %convert_element_type.25), channel_id=1, source_target_pairs={{0,16},{16,0},{32,48},{48,32},{64,80},{80,64},{96,112},{112,96},{1... | collective-permute-start | bytes 196616 | tf_op jit(solution)/shard_map/ppermute | solution.py:11
  60.3 13.9 %collective-permute-start.2 = (bf16[128,256]{1,0:T(8,128)(2,1)S(1)}, bf16[128,256]{1,0:T(8,128)(2,1)S(1)}, u32[]{:S(2)}, u32[]{:S(2)}) collective-permute-start(bf16[128,256]{1,0:T(8,128)(2,1)S(1)} %convert_element_type.27), channel_id=1, source_target_pairs={{0,32},{16,48},{32,0},{48,16},{64,96},{80,112},{96,64},{112,80},{1... | collective-permute-start | bytes 196616 | tf_op jit(solution)/shard_map/ppermute | solution.py:11
  69.5 5.8 %collective-permute-start.3 = (bf16[128,128]{1,0:T(8,128)(2,1)S(1)}, bf16[128,128]{1,0:T(8,128)(2,1)S(1)}, u32[]{:S(2)}, u32[]{:S(2)}) collective-permute-start(bf16[128,128]{1,0:T(8,128)(2,1)S(1)} %get-tuple-element.58), channel_id=1, source_target_pairs={{0,32},{16,48},{32,0},{48,16},{64,96},{80,112},{96,64},{112,80},{1... | collective-permute-start | bytes 98312 | tf_op jit(solution)/shard_map/ppermute | solution.py:11
  77.0 17.3 %all-to-all-start.2 = ((bf16[16,224,128]{2,1,0:T(8,128)(2,1)}), bf16[16,224,128]{2,1,0:T(8,128)(2,1)S(1)}, u32[]{:S(2)}, u32[]{:S(2)}) async-start(bf16[16,224,128]{2,1,0:T(8,128)(2,1)} %get-tuple-element.47), calls=%async_computation.2 | async-start | bytes 1835008 | tf_op jit(solution)/shard_map/all_to_all | solution.py:244
  80.7 14.6 %collective-permute-start.6 = (bf16[1792,128]{1,0:T(8,128)(2,1)}, bf16[1792,128]{1,0:T(8,128)(2,1)S(1)}, u32[]{:S(2)}, u32[]{:S(2)}) collective-permute-start(bf16[1792,128]{1,0:T(8,128)(2,1)} %bitcast.15), channel_id=1, source_target_pairs={{0,16},{16,0},{32,48},{48,32},{64,80},{80,64},{96,112},{112,96},{1... | collective-permute-start | bytes 1376264 | tf_op jit(solution)/shard_map/ppermute | solution.py:11
  82.6 12.7 %collective-permute-start.5 = (bf16[128,384]{1,0:T(8,128)(2,1)S(1)}, bf16[128,384]{1,0:T(8,128)(2,1)S(1)}, u32[]{:S(2)}, u32[]{:S(2)}) collective-permute-start(bf16[128,384]{1,0:T(8,128)(2,1)S(1)} %get-tuple-element.48), channel_id=1, source_target_pairs={{0,16},{16,0},{32,48},{48,32},{64,80},{80,64},{96,112},{112,96},{1... | collective-permute-start | bytes 294920 | tf_op jit(solution)/shard_map/ppermute | solution.py:11
  95.2 22.9 %copy-start.3 = (bf16[256,1792]{1,0:T(8,128)(2,1)S(1)}, bf16[256,1792]{1,0:T(8,128)(2,1)}, u32[]{:S(2)}) copy-start(bf16[256,1792]{1,0:T(8,128)(2,1)} %copy-done.2) | copy-start | bytes 2752516
  95.2 28.3 %all-to-all-start.3 = ((bf16[32,8,112]{2,1,0:T(8,128)(2,1)}), bf16[32,8,112]{2,1,0:T(8,128)(2,1)S(1)}, u32[]{:S(2)}, u32[]{:S(2)}) async-start(bf16[32,8,112]{2,1,0:T(8,128)(2,1)} %bitcast.16), calls=%async_computation.3 | async-start | bytes 131072 | tf_op jit(solution)/shard_map/all_to_all | solution.py:172
  120.6 3.0 %copy-start.1 = (bf16[256,128]{1,0:T(8,128)(2,1)S(1)}, bf16[256,128]{1,0:T(8,128)(2,1)}, u32[]{:S(2)}) copy-start(bf16[256,128]{1,0:T(8,128)(2,1)} %get-tuple-element.51.refs_1_) | copy-start | bytes 196612

commit v7 on v6

--- a/solution.py
+++ b/solution.py
@@ -94,6 +94,14 @@
     for at in range(out.shape[0]):
         out[at, pl.ds(here, own.shape[1]), :] = own[at]
         out[at, pl.ds(there, own.shape[1]), :] = other[at]
+
+
+def project_kernel(grads, weights, part, rounded):
+    total = jnp.zeros(part.shape, jnp.float32)
+    for at in range(grads.shape[0]):
+        total = total + dot(grads[at], weights[at], 0, 0)
+    part[...] = total
+    rounded[...] = total.astype(jnp.bfloat16)
 
 
 def hidden_kernel(core, pre, other_pre, part, other, gate_up, other_gate_up, acts, out):
@@ -219,11 +227,13 @@
         by_piece(own_down),
         by_piece(other_down),
     )
-    grads_in, down_pair = lax.optimization_barrier((grads_in, down_pair))
-    part = dot(
-        grads_in.reshape(2 * quarter, half), down_pair.reshape(2 * quarter, hidden), 0, 0
-    )
-    other = swapped(part.astype(jnp.bfloat16), 2)
+    part, rounded = call(
+        project_kernel,
+        [jax.ShapeDtypeStruct((half, hidden), jnp.float32), bf16(half, hidden)],
+        grads_in,
+        down_pair,
+    )
+    other = swapped(rounded, 2)
     acts, partial_value = call(
         hidden_kernel,
         [bf16(half, 3 * hidden), bf16(local_count, 2 * piece, half)],

time: 125 us -> 125 us (level)
  Pallas kernels: 6.84 us -> 8.5 us
  matrix products: 5.76 us -> 4.15 us
    pallas_call x6 -> x7, Pallas kernels: 6.84 us -> 8.5 us  [call(): pl.pallas_call(kernel, out_shape=outs, in_specs=[pl.BlockSpec(memory_spac...]
    dot_general x6 -> x5, matrix products: 5.76 us -> 4.15 us  [dot(): lax.dot_general(lhs, rhs, (((lhs_dim,), (rhs_dim,)), ((), ())), preferred...]
  transfers between devices with their start and end apart: 11 -> 11, of which waited for: 6 -> 6; matrix products, arithmetic and copies ran while one was open for 8% -> 6% of each run, Pallas kernels for 1% -> 1%
where the time goes in v7:
time: 125 us; the launch traced here: 124 us
  starting transfers between devices  84 us (67%)
  waiting for transfers between devices  22.2 us (18%)
  Pallas kernels  8.5 us (7%)
  matrix products  4.15 us (3%)
  local copies, waits for them, and re-layouts  3.45 us (3%)
  other arithmetic  1.25 us (1%)
    all_to_all x2, starting transfers between devices, across_chips(): lax.all_to_all(block, 'node', split_axis=0, concat_axis=0, tiled=True, ax...  57.3 us
    ppermute x7, starting transfers between devices, swapped(): return lax.ppermute(block, 'node', [(at, at ^ mask) for at in range(count)])  15.7 us
    all_to_all x1, waiting for transfers between devices, per_device(): lax.all_to_all(partial_value, 'local', split_axis=0, concat_axis=0, tiled...  8.62 us
    pallas_call x7, Pallas kernels, call(): pl.pallas_call(kernel, out_shape=outs, in_specs=[pl.BlockSpec(memory_spac...  8.5 us
    all_to_all x1, starting transfers between devices, per_device(): lax.all_to_all(copies, 'local', split_axis=0, concat_axis=0, tiled=True)  7.17 us
    all_to_all x2, waiting for transfers between devices, across_chips(): lax.all_to_all(block, 'node', split_axis=0, concat_axis=0, tiled=True, ax...  5.32 us
    all_to_all x1, waiting for transfers between devices, per_device(): lax.all_to_all(copies, 'local', split_axis=0, concat_axis=0, tiled=True)  4.93 us
    dot_general x5, matrix products, dot(): lax.dot_general(lhs, rhs, (((lhs_dim,), (rhs_dim,)), ((), ())), preferred...  4.15 us
  transfers between devices with their start and end apart: 11, of which 6 were waited for; matrix products, arithmetic and copies ran while one was open for 6% of the time, Pallas kernels for 1%

profile of v7, /device:TPU:32, one launch (start us, length us, event | category | flops | bytes accessed | tf_op | source)
XLA Modules:
  0.0 124.5 jit_solution(15229738300638137488)
XLA Ops:
  0.6 1.9 %shard_map.120 = (bf16[256,112]{1,0:T(8,128)(2,1)}, bf16[256,128]{1,0:T(8,128)(2,1)}) custom-call(s32[8,128]{1,0:T(8,128)} %bitcast.43, s32[8,128]{1,0:T(8,128)} %bitcast.44, s32[8,128]{1,0:T(8,128)} %bitcast.45, f32[8,128]{1,0:T(8,128)} %bitcast.46, bf16[4,112,128]{2,1,0:T(8,128)(2,1)} %bitcast.40), custom_call_target="tpu_custom_call" | custom-call | bytes 253952 | tf_op jit(solution)/shard_map/pallas_call | solution.py:24
  2.6 34.5 %all-to-all-start = ((bf16[32,8,112]{2,1,0:T(8,128)(2,1)}), bf16[32,8,112]{2,1,0:T(8,128)(2,1)S(1)}, u32[]{:S(2)}, u32[]{:S(2)}) async-start(bf16[32,8,112]{2,1,0:T(8,128)(2,1)} %bitcast.42), calls=%async_computation | async-start | bytes 131072 | tf_op jit(solution)/shard_map/all_to_all | solution.py:180
  37.1 0.0 copy-start.5
  37.1 1.7 %reshape.71 = bf16[256,1792]{1,0:T(8,128)(2,1)S(1)} reshape(bf16[64,4,1792]{2,1,0:T(4,128)(2,1)} %param.14) | data formatting | bytes 1835008 | tf_op jit(solution)/shard_map/reshape | solution.py:196
  38.8 0.0 copy-start.2
  38.9 0.0 copy-done.5
  38.9 0.0 copy-start.6
  38.9 0.1 constant_dynamic-update-slice_fusion.1
  39.0 1.3 %copy-done.6 = bf16[1792,128]{1,0:T(8,128)(2,1)S(1)} copy-done((bf16[1792,128]{1,0:T(8,128)(2,1)S(1)}, bf16[1792,128]{1,0:T(8,128)(2,1)}, u32[]{:S(2)}) %copy-start.6) | copy-done | bytes 458776
  40.2 0.1 constant_dynamic-update-slice_fusion
  40.3 0.0 copy-done.2
  40.3 0.4 fusion.6
  40.8 0.1 reshape.72
  41.0 3.3 %all-to-all-done = bf16[32,8,112]{2,1,0:T(8,128)(2,1)S(1)} async-done(((bf16[32,8,112]{2,1,0:T(8,128)(2,1)}), bf16[32,8,112]{2,1,0:T(8,128)(2,1)S(1)}, u32[]{:S(2)}, u32[]{:S(2)}) %all-to-all-start) | async-done | bytes 57376 | tf_op jit(solution)/shard_map/all_to_all | solution.py:180
  44.3 1.2 shard_map.121
  45.5 0.0 copy-start
  45.5 7.2 %all-to-all-start.1 = ((bf16[16,224,128]{2,1,0:T(8,128)(2,1)}), bf16[16,224,128]{2,1,0:T(8,128)(2,1)S(1)}, u32[]{:S(2)}, u32[]{:S(2)}) async-start(bf16[16,224,128]{2,1,0:T(8,128)(2,1)} %shard_map.121), calls=%async_computation.1 | async-start | bytes 1835008 | tf_op jit(solution)/shard_map/all_to_all | solution.py:216
  52.7 1.9 %collective-permute-start.4 = (bf16[1792,256]{1,0:T(8,128)(2,1)S(1)}, bf16[1792,256]{1,0:T(8,128)(2,1)}, u32[]{:S(2)}, u32[]{:S(2)}) collective-permute-start(bf16[1792,256]{1,0:T(8,128)(2,1)S(1)} %constant_dynamic-update-slice_fusion), channel_id=1, source_target_pairs={{0,16},{16,0},{32,48},{48,32},{64,80},{80,64},{96,112},{112,96},{1... | collective-permute-start | bytes 2752520 | tf_op jit(solution)/shard_map/ppermute | solution.py:11
  54.7 0.0 copy-done
  54.7 2.4 %collective-permute-start = (bf16[1792,128]{1,0:T(8,128)(2,1)S(1)}, bf16[1792,128]{1,0:T(8,128)(2,1)S(1)}, u32[]{:S(2)}, u32[]{:S(2)}) collective-permute-start(bf16[1792,128]{1,0:T(8,128)(2,1)S(1)} %copy-done), channel_id=1, source_target_pairs={{0,16},{16,0},{32,48},{48,32},{64,80},{80,64},{96,112},{112,96},{1... | collective-permute-start | bytes 1376264 | tf_op jit(solution)/shard_map/ppermute | solution.py:11
  57.1 1.9 %collective-permute-start.1 = (bf16[128,256]{1,0:T(8,128)(2,1)S(1)}, bf16[128,256]{1,0:T(8,128)(2,1)S(1)}, u32[]{:S(2)}, u32[]{:S(2)}) collective-permute-start(bf16[128,256]{1,0:T(8,128)(2,1)S(1)} %convert_element_type.22), channel_id=1, source_target_pairs={{0,16},{16,0},{32,48},{48,32},{64,80},{80,64},{96,112},{112,96},{1... | collective-permute-start | bytes 196616 | tf_op jit(solution)/shard_map/ppermute | solution.py:11
  59.0 1.2 collective-permute-done.1
  60.2 0.0 collective-permute-done
  60.3 2.4 %collective-permute-start.2 = (bf16[128,256]{1,0:T(8,128)(2,1)S(1)}, bf16[128,256]{1,0:T(8,128)(2,1)S(1)}, u32[]{:S(2)}, u32[]{:S(2)}) collective-permute-start(bf16[128,256]{1,0:T(8,128)(2,1)S(1)} %convert_element_type.24), channel_id=1, source_target_pairs={{0,32},{16,48},{32,0},{48,16},{64,96},{80,112},{96,64},{112,80},{1... | collective-permute-start | bytes 196616 | tf_op jit(solution)/shard_map/ppermute | solution.py:11
  62.7 0.1 shard_map.122.weights
  62.8 4.9 %all-to-all-done.1.grads = bf16[16,224,128]{2,1,0:T(8,128)(2,1)S(1)} async-done(((bf16[16,224,128]{2,1,0:T(8,128)(2,1)}), bf16[16,224,128]{2,1,0:T(8,128)(2,1)S(1)}, u32[]{:S(2)}, u32[]{:S(2)}) %all-to-all-start.1) | async-done | bytes 917536 | tf_op jit(solution)/shard_map/all_to_all | solution.py:216
  67.7 0.5 shard_map.123
  68.2 2.7 %collective-permute-start.3 = (bf16[128,128]{1,0:T(8,128)(2,1)S(1)}, bf16[128,128]{1,0:T(8,128)(2,1)S(1)}, u32[]{:S(2)}, u32[]{:S(2)}) collective-permute-start(bf16[128,128]{1,0:T(8,128)(2,1)S(1)} %get-tuple-element.43), channel_id=1, source_target_pairs={{0,32},{16,48},{32,0},{48,16},{64,96},{80,112},{96,64},{112,80},{1... | collective-permute-start | bytes 98312 | tf_op jit(solution)/shard_map/ppermute | solution.py:11
  70.9 1.0 broadcast_select_fusion
  71.9 0.0 collective-permute-done.2.other_pre
  71.9 2.1 %collective-permute-done.3.other = bf16[128,128]{1,0:T(8,128)(2,1)S(1)} collective-permute-done((bf16[128,128]{1,0:T(8,128)(2,1)S(1)}, bf16[128,128]{1,0:T(8,128)(2,1)S(1)}, u32[]{:S(2)}, u32[]{:S(2)}) %collective-permute-start.3) | collective-permute-done | bytes 32800 | tf_op jit(solution)/shard_map/ppermute | solution.py:11
  74.0 0.0 collective-permute-done.4
  74.0 2.9 %shard_map.124 = (bf16[128,384]{1,0:T(8,128)(2,1)S(1)}, bf16[16,224,128]{2,1,0:T(8,128)(2,1)}) custom-call(s32[1]{0:T(128)} %bitcast.core, f32[128,256]{1,0:T(8,128)S(1)} %convert_add_fusion.pre, bf16[128,256]{1,0:T(8,128)(2,1)S(1)} %collective-permute-done.2.other_pre, f32[128,128]{1,0:T(8,128)S(1)} %get-tuple-element.42.part, ...), custom_call_target="tpu_custom_call" | custom-call | bytes 3145732 | tf_op jit(solution)/shard_map/pallas_call | solution.py:24
  76.9 0.0 copy-start.4
  76.9 3.8 %all-to-all-start.2 = ((bf16[16,224,128]{2,1,0:T(8,128)(2,1)}), bf16[16,224,128]{2,1,0:T(8,128)(2,1)S(1)}, u32[]{:S(2)}, u32[]{:S(2)}) async-start(bf16[16,224,128]{2,1,0:T(8,128)(2,1)} %get-tuple-element.47), calls=%async_computation.2 | async-start | bytes 1835008 | tf_op jit(solution)/shard_map/all_to_all | solution.py:254
  80.7 1.9 %collective-permute-start.6 = (bf16[1792,128]{1,0:T(8,128)(2,1)}, bf16[1792,128]{1,0:T(8,128)(2,1)S(1)}, u32[]{:S(2)}, u32[]{:S(2)}) collective-permute-start(bf16[1792,128]{1,0:T(8,128)(2,1)} %bitcast.14), channel_id=1, source_target_pairs={{0,16},{16,0},{32,48},{48,32},{64,80},{80,64},{96,112},{112,96},{1... | collective-permute-start | bytes 1376264 | tf_op jit(solution)/shard_map/ppermute | solution.py:11
  82.6 2.4 %collective-permute-start.5 = (bf16[128,384]{1,0:T(8,128)(2,1)S(1)}, bf16[128,384]{1,0:T(8,128)(2,1)S(1)}, u32[]{:S(2)}, u32[]{:S(2)}) collective-permute-start(bf16[128,384]{1,0:T(8,128)(2,1)S(1)} %get-tuple-element.48), channel_id=1, source_target_pairs={{0,16},{16,0},{32,48},{48,32},{64,80},{80,64},{96,112},{112,96},{1... | collective-permute-start | bytes 294920 | tf_op jit(solution)/shard_map/ppermute | solution.py:11
  85.1 0.0 copy-done.4
  85.1 0.3 fusion.4
  85.3 8.6 %all-to-all-done.2.refs_0_ = bf16[16,224,128]{2,1,0:T(8,128)(2,1)S(1)} async-done(((bf16[16,224,128]{2,1,0:T(8,128)(2,1)}), bf16[16,224,128]{2,1,0:T(8,128)(2,1)S(1)}, u32[]{:S(2)}, u32[]{:S(2)}) %all-to-all-start.2) | async-done | bytes 917536 | tf_op jit(solution)/shard_map/all_to_all | solution.py:254
  94.0 1.0 shard_map.125
  94.9 0.0 copy-start.3
  94.9 0.0 collective-permute-done.5
  94.9 0.0 collective-permute-done.6
  94.9 22.8 %all-to-all-start.3 = ((bf16[32,8,112]{2,1,0:T(8,128)(2,1)}), bf16[32,8,112]{2,1,0:T(8,128)(2,1)S(1)}, u32[]{:S(2)}, u32[]{:S(2)}) async-start(bf16[32,8,112]{2,1,0:T(8,128)(2,1)} %bitcast.15), calls=%async_computation.3 | async-start | bytes 131072 | tf_op jit(solution)/shard_map/all_to_all | solution.py:180
  117.8 0.1 pad_maximum_fusion
  117.9 0.1 reshape.80
  118.0 0.0 copy-done.3
  118.0 1.2 convolution_convert_fusion
  119.2 1.2 convolution_convert_fusion.1
  120.5 0.0 copy-start.1
  120.5 1.0 fusion
  121.5 2.0 %all-to-all-done.3 = bf16[32,8,112]{2,1,0:T(8,128)(2,1)S(1)} async-done(((bf16[32,8,112]{2,1,0:T(8,128)(2,1)}), bf16[32,8,112]{2,1,0:T(8,128)(2,1)S(1)}, u32[]{:S(2)}, u32[]{:S(2)}) %all-to-all-start.3) | async-done | bytes 57376 | tf_op jit(solution)/shard_map/all_to_all | solution.py:180
  123.5 0.0 copy-done.1
  123.5 0.9 shard_map.126
  (10 shorter events, 0.3 us)
Async XLA Ops:
  2.6 41.7 %all-to-all-start = ((bf16[32,8,112]{2,1,0:T(8,128)(2,1)}), bf16[32,8,112]{2,1,0:T(8,128)(2,1)S(1)}, u32[]{:S(2)}, u32[]{:S(2)}) async-start(bf16[32,8,112]{2,1,0:T(8,128)(2,1)} %bitcast.42), calls=%async_computation | async-start | bytes 131072 | tf_op jit(solution)/shard_map/all_to_all | solution.py:180
  37.1 1.7 %copy-start.5 = (bf16[1792,128]{1,0:T(8,128)(2,1)S(1)}, bf16[1792,128]{1,0:T(8,128)(2,1)}, u32[]{:S(2)}) copy-start(bf16[1792,128]{1,0:T(8,128)(2,1)} %param.15) | copy-start | bytes 1376260
  38.8 1.5 %copy-start.2 = (bf16[256,1792]{1,0:T(8,128)(2,1)}, bf16[256,1792]{1,0:T(8,128)(2,1)S(1)}, u32[]{:S(2)}) copy-start(bf16[256,1792]{1,0:T(8,128)(2,1)S(1)} %reshape.71) | copy-start | bytes 2752516
  38.9 1.4 %copy-start.6 = (bf16[1792,128]{1,0:T(8,128)(2,1)S(1)}, bf16[1792,128]{1,0:T(8,128)(2,1)}, u32[]{:S(2)}) copy-start(bf16[1792,128]{1,0:T(8,128)(2,1)} %param.16) | copy-start | bytes 1376260
  45.5 9.1 %copy-start = (bf16[1792,128]{1,0:T(8,128)(2,1)S(1)}, bf16[1792,128]{1,0:T(8,128)(2,1)}, u32[]{:S(2)}) copy-start(bf16[1792,128]{1,0:T(8,128)(2,1)} %param.17) | copy-start | bytes 1376260
  45.5 22.2 %all-to-all-start.1 = ((bf16[16,224,128]{2,1,0:T(8,128)(2,1)}), bf16[16,224,128]{2,1,0:T(8,128)(2,1)S(1)}, u32[]{:S(2)}, u32[]{:S(2)}) async-start(bf16[16,224,128]{2,1,0:T(8,128)(2,1)} %shard_map.121), calls=%async_computation.1 | async-start | bytes 1835008 | tf_op jit(solution)/shard_map/all_to_all | solution.py:216
  52.7 21.3 %collective-permute-start.4 = (bf16[1792,256]{1,0:T(8,128)(2,1)S(1)}, bf16[1792,256]{1,0:T(8,128)(2,1)}, u32[]{:S(2)}, u32[]{:S(2)}) collective-permute-start(bf16[1792,256]{1,0:T(8,128)(2,1)S(1)} %constant_dynamic-update-slice_fusion), channel_id=1, source_target_pairs={{0,16},{16,0},{32,48},{48,32},{64,80},{80,64},{96,112},{112,96},{1... | collective-permute-start | bytes 2752520 | tf_op jit(solution)/shard_map/ppermute | solution.py:11
  54.7 5.6 %collective-permute-start = (bf16[1792,128]{1,0:T(8,128)(2,1)S(1)}, bf16[1792,128]{1,0:T(8,128)(2,1)S(1)}, u32[]{:S(2)}, u32[]{:S(2)}) collective-permute-start(bf16[1792,128]{1,0:T(8,128)(2,1)S(1)} %copy-done), channel_id=1, source_target_pairs={{0,16},{16,0},{32,48},{48,32},{64,80},{80,64},{96,112},{112,96},{1... | collective-permute-start | bytes 1376264 | tf_op jit(solution)/shard_map/ppermute | solution.py:11
  57.1 3.1 %collective-permute-start.1 = (bf16[128,256]{1,0:T(8,128)(2,1)S(1)}, bf16[128,256]{1,0:T(8,128)(2,1)S(1)}, u32[]{:S(2)}, u32[]{:S(2)}) collective-permute-start(bf16[128,256]{1,0:T(8,128)(2,1)S(1)} %convert_element_type.22), channel_id=1, source_target_pairs={{0,16},{16,0},{32,48},{48,32},{64,80},{80,64},{96,112},{112,96},{1... | collective-permute-start | bytes 196616 | tf_op jit(solution)/shard_map/ppermute | solution.py:11
  60.3 11.7 %collective-permute-start.2 = (bf16[128,256]{1,0:T(8,128)(2,1)S(1)}, bf16[128,256]{1,0:T(8,128)(2,1)S(1)}, u32[]{:S(2)}, u32[]{:S(2)}) collective-permute-start(bf16[128,256]{1,0:T(8,128)(2,1)S(1)} %convert_element_type.24), channel_id=1, source_target_pairs={{0,32},{16,48},{32,0},{48,16},{64,96},{80,112},{96,64},{112,80},{1... | collective-permute-start | bytes 196616 | tf_op jit(solution)/shard_map/ppermute | solution.py:11
  68.2 5.8 %collective-permute-start.3 = (bf16[128,128]{1,0:T(8,128)(2,1)S(1)}, bf16[128,128]{1,0:T(8,128)(2,1)S(1)}, u32[]{:S(2)}, u32[]{:S(2)}) collective-permute-start(bf16[128,128]{1,0:T(8,128)(2,1)S(1)} %get-tuple-element.43), channel_id=1, source_target_pairs={{0,32},{16,48},{32,0},{48,16},{64,96},{80,112},{96,64},{112,80},{1... | collective-permute-start | bytes 98312 | tf_op jit(solution)/shard_map/ppermute | solution.py:11
  76.9 8.1 %copy-start.4 = (bf16[16,1,112,128]{3,2,1,0:T(8,128)(2,1)S(1)}, bf16[16,1,112,128]{3,2,1,0:T(8,128)(2,1)}, u32[]{:S(2)}) copy-start(bf16[16,1,112,128]{3,2,1,0:T(8,128)(2,1)} %get-tuple-element.54) | copy-start | bytes 1376260
  76.9 17.0 %all-to-all-start.2 = ((bf16[16,224,128]{2,1,0:T(8,128)(2,1)}), bf16[16,224,128]{2,1,0:T(8,128)(2,1)S(1)}, u32[]{:S(2)}, u32[]{:S(2)}) async-start(bf16[16,224,128]{2,1,0:T(8,128)(2,1)} %get-tuple-element.47), calls=%async_computation.2 | async-start | bytes 1835008 | tf_op jit(solution)/shard_map/all_to_all | solution.py:254
  80.7 14.2 %collective-permute-start.6 = (bf16[1792,128]{1,0:T(8,128)(2,1)}, bf16[1792,128]{1,0:T(8,128)(2,1)S(1)}, u32[]{:S(2)}, u32[]{:S(2)}) collective-permute-start(bf16[1792,128]{1,0:T(8,128)(2,1)} %bitcast.14), channel_id=1, source_target_pairs={{0,16},{16,0},{32,48},{48,32},{64,80},{80,64},{96,112},{112,96},{1... | collective-permute-start | bytes 1376264 | tf_op jit(solution)/shard_map/ppermute | solution.py:11
  82.6 12.3 %collective-permute-start.5 = (bf16[128,384]{1,0:T(8,128)(2,1)S(1)}, bf16[128,384]{1,0:T(8,128)(2,1)S(1)}, u32[]{:S(2)}, u32[]{:S(2)}) collective-permute-start(bf16[128,384]{1,0:T(8,128)(2,1)S(1)} %get-tuple-element.48), channel_id=1, source_target_pairs={{0,16},{16,0},{32,48},{48,32},{64,80},{80,64},{96,112},{112,96},{1... | collective-permute-start | bytes 294920 | tf_op jit(solution)/shard_map/ppermute | solution.py:11
  94.9 23.1 %copy-start.3 = (bf16[256,1792]{1,0:T(8,128)(2,1)S(1)}, bf16[256,1792]{1,0:T(8,128)(2,1)}, u32[]{:S(2)}) copy-start(bf16[256,1792]{1,0:T(8,128)(2,1)} %copy-done.2) | copy-start | bytes 2752516
  94.9 28.6 %all-to-all-start.3 = ((bf16[32,8,112]{2,1,0:T(8,128)(2,1)}), bf16[32,8,112]{2,1,0:T(8,128)(2,1)S(1)}, u32[]{:S(2)}, u32[]{:S(2)}) async-start(bf16[32,8,112]{2,1,0:T(8,128)(2,1)} %bitcast.15), calls=%async_computation.3 | async-start | bytes 131072 | tf_op jit(solution)/shard_map/all_to_all | solution.py:180
  120.5 3.1 %copy-start.1 = (bf16[256,128]{1,0:T(8,128)(2,1)S(1)}, bf16[256,128]{1,0:T(8,128)(2,1)}, u32[]{:S(2)}) copy-start(bf16[256,128]{1,0:T(8,128)(2,1)} %get-tuple-element.51.refs_1_) | copy-start | bytes 196612

commit v8 on v7

--- a/solution.py
+++ b/solution.py
@@ -89,17 +89,12 @@
     return pl.multiple_of(core[0] * piece, 16), pl.multiple_of((1 - core[0]) * piece, 16)
 
 
-def pair_kernel(core, own, other, out):
-    here, there = starts(core, own.shape[1])
-    for at in range(out.shape[0]):
-        out[at, pl.ds(here, own.shape[1]), :] = own[at]
-        out[at, pl.ds(there, own.shape[1]), :] = other[at]
-
-
-def project_kernel(grads, weights, part, rounded):
+def project_kernel(core, grads, own, other, part, rounded):
+    piece = own.shape[1]
     total = jnp.zeros(part.shape, jnp.float32)
-    for at in range(grads.shape[0]):
-        total = total + dot(grads[at], weights[at], 0, 0)
+    for start, weights in zip(starts(core, piece), (own, other)):
+        for at in range(grads.shape[0]):
+            total = total + dot(grads[at, pl.ds(start, piece), :], weights[at], 0, 0)
     part[...] = total
     rounded[...] = total.astype(jnp.bfloat16)
 
@@ -220,18 +215,13 @@
     other_down, pre = lax.optimization_barrier((other_down, pre))
     other_pre = swapped(pre.astype(jnp.bfloat16), 2)
     by_piece = lambda block: block.reshape(local_count, piece, block.shape[1])
-    (down_pair,) = call(
-        pair_kernel,
-        [bf16(local_count, 2 * piece, hidden)],
-        core.reshape(1),
-        by_piece(own_down),
-        by_piece(other_down),
-    )
     part, rounded = call(
         project_kernel,
         [jax.ShapeDtypeStruct((half, hidden), jnp.float32), bf16(half, hidden)],
+        core.reshape(1),
         grads_in,
-        down_pair,
+        by_piece(down_weight_t),
+        by_piece(other_down),
     )
     other = swapped(rounded, 2)
     acts, partial_value = call(

time: 125 us -> 126 us (level)
  local copies, waits for them, and re-layouts: 3.45 us -> 5.23 us
  Pallas kernels: 8.5 us -> 7.21 us
    unnamed x15 -> x21, local copies, waits for them, and re-layouts: 1.36 us -> 3.14 us
    pallas_call x7 -> x6, Pallas kernels: 8.5 us -> 7.21 us  [call(): pl.pallas_call(kernel, out_shape=outs, in_specs=[pl.BlockSpec(memory_spac...]
where the time goes in v8:
time: 126 us; the launch traced here: 125 us
  starting transfers between devices  84 us (67%)
  waiting for transfers between devices  22.2 us (18%)
  Pallas kernels  7.21 us (6%)
  local copies, waits for them, and re-layouts  5.23 us (4%)
  matrix products  4.15 us (3%)
    all_to_all x2, starting transfers between devices, across_chips(): lax.all_to_all(block, 'node', split_axis=0, concat_axis=0, tiled=True, ax...  57.3 us
    ppermute x7, starting transfers between devices, swapped(): return lax.ppermute(block, 'node', [(at, at ^ mask) for at in range(count)])  15.7 us
    all_to_all x1, waiting for transfers between devices, per_device(): lax.all_to_all(partial_value, 'local', split_axis=0, concat_axis=0, tiled...  9.29 us
    pallas_call x6, Pallas kernels, call(): pl.pallas_call(kernel, out_shape=outs, in_specs=[pl.BlockSpec(memory_spac...  7.21 us
    all_to_all x1, starting transfers between devices, per_device(): lax.all_to_all(copies, 'local', split_axis=0, concat_axis=0, tiled=True)  7.17 us
    all_to_all x2, waiting for transfers between devices, across_chips(): lax.all_to_all(block, 'node', split_axis=0, concat_axis=0, tiled=True, ax...  5.31 us
    all_to_all x1, waiting for transfers between devices, per_device(): lax.all_to_all(copies, 'local', split_axis=0, concat_axis=0, tiled=True)  4.25 us
    dot_general x5, matrix products, dot(): lax.dot_general(lhs, rhs, (((lhs_dim,), (rhs_dim,)), ((), ())), preferred...  4.15 us
  transfers between devices with their start and end apart: 11, of which 6 were waited for; matrix products, arithmetic and copies ran while one was open for 6% of the time, Pallas kernels for 1%

profile of v8, /device:TPU:32, one launch (start us, length us, event | category | flops | bytes accessed | tf_op | source)
XLA Modules:
  0.0 124.9 jit_solution(5078948650831591150)
XLA Ops:
  0.6 1.9 %shard_map.120 = (bf16[256,112]{1,0:T(8,128)(2,1)}, bf16[256,128]{1,0:T(8,128)(2,1)}) custom-call(s32[8,128]{1,0:T(8,128)} %bitcast.45, s32[8,128]{1,0:T(8,128)} %bitcast.46, s32[8,128]{1,0:T(8,128)} %bitcast.47, f32[8,128]{1,0:T(8,128)} %bitcast.48, bf16[4,112,128]{2,1,0:T(8,128)(2,1)} %bitcast.42), custom_call_target="tpu_custom_call" | custom-call | bytes 253952 | tf_op jit(solution)/shard_map/pallas_call | solution.py:24
  2.6 34.5 %all-to-all-start = ((bf16[32,8,112]{2,1,0:T(8,128)(2,1)}), bf16[32,8,112]{2,1,0:T(8,128)(2,1)S(1)}, u32[]{:S(2)}, u32[]{:S(2)}) async-start(bf16[32,8,112]{2,1,0:T(8,128)(2,1)} %bitcast.44), calls=%async_computation | async-start | bytes 131072 | tf_op jit(solution)/shard_map/all_to_all | solution.py:175
  37.1 0.0 copy-start.7
  37.1 1.7 %reshape.71 = bf16[256,1792]{1,0:T(8,128)(2,1)S(1)} reshape(bf16[64,4,1792]{2,1,0:T(4,128)(2,1)} %param.14) | data formatting | bytes 1835008 | tf_op jit(solution)/shard_map/reshape | solution.py:191
  38.8 0.0 copy-start.4
  38.9 0.0 copy-done.7
  38.9 0.0 copy-start.8
  38.9 0.1 constant_dynamic-update-slice_fusion.1
  39.0 1.3 %copy-done.8 = bf16[1792,128]{1,0:T(8,128)(2,1)S(1)} copy-done((bf16[1792,128]{1,0:T(8,128)(2,1)S(1)}, bf16[1792,128]{1,0:T(8,128)(2,1)}, u32[]{:S(2)}) %copy-start.8) | copy-done | bytes 458776
  40.2 0.1 constant_dynamic-update-slice_fusion
  40.3 0.0 copy-done.4
  40.3 0.4 fusion.6
  40.8 0.1 reshape.72
  41.0 3.3 %all-to-all-done = bf16[32,8,112]{2,1,0:T(8,128)(2,1)S(1)} async-done(((bf16[32,8,112]{2,1,0:T(8,128)(2,1)}), bf16[32,8,112]{2,1,0:T(8,128)(2,1)S(1)}, u32[]{:S(2)}, u32[]{:S(2)}) %all-to-all-start) | async-done | bytes 57376 | tf_op jit(solution)/shard_map/all_to_all | solution.py:175
  44.3 1.2 shard_map.121
  45.5 0.0 copy-start
  45.5 7.2 %all-to-all-start.1 = ((bf16[16,224,128]{2,1,0:T(8,128)(2,1)}), bf16[16,224,128]{2,1,0:T(8,128)(2,1)S(1)}, u32[]{:S(2)}, u32[]{:S(2)}) async-start(bf16[16,224,128]{2,1,0:T(8,128)(2,1)} %shard_map.121), calls=%async_computation.1 | async-start | bytes 1835008 | tf_op jit(solution)/shard_map/all_to_all | solution.py:211
  52.7 1.9 %collective-permute-start.4 = (bf16[1792,256]{1,0:T(8,128)(2,1)S(1)}, bf16[1792,256]{1,0:T(8,128)(2,1)S(1)}, u32[]{:S(2)}, u32[]{:S(2)}) collective-permute-start(bf16[1792,256]{1,0:T(8,128)(2,1)S(1)} %constant_dynamic-update-slice_fusion), channel_id=1, source_target_pairs={{0,16},{16,0},{32,48},{48,32},{64,80},{80,64},{96,112},{112,96},{1... | collective-permute-start | bytes 2752520 | tf_op jit(solution)/shard_map/ppermute | solution.py:11
  54.6 0.0 copy-done
  54.6 2.4 %collective-permute-start = (bf16[1792,128]{1,0:T(8,128)(2,1)S(1)}, bf16[1792,128]{1,0:T(8,128)(2,1)S(1)}, u32[]{:S(2)}, u32[]{:S(2)}) collective-permute-start(bf16[1792,128]{1,0:T(8,128)(2,1)S(1)} %copy-done), channel_id=1, source_target_pairs={{0,16},{16,0},{32,48},{48,32},{64,80},{80,64},{96,112},{112,96},{1... | collective-permute-start | bytes 1376264 | tf_op jit(solution)/shard_map/ppermute | solution.py:11
  57.1 1.9 %collective-permute-start.1 = (bf16[128,256]{1,0:T(8,128)(2,1)S(1)}, bf16[128,256]{1,0:T(8,128)(2,1)S(1)}, u32[]{:S(2)}, u32[]{:S(2)}) collective-permute-start(bf16[128,256]{1,0:T(8,128)(2,1)S(1)} %convert_element_type.22), channel_id=1, source_target_pairs={{0,16},{16,0},{32,48},{48,32},{64,80},{80,64},{96,112},{112,96},{1... | collective-permute-start | bytes 196616 | tf_op jit(solution)/shard_map/ppermute | solution.py:11
  59.0 1.2 collective-permute-done.1
  60.2 0.0 collective-permute-done
  60.2 0.0 copy-start.1
  60.2 0.8 copy-done.1
  61.0 2.4 %collective-permute-start.2 = (bf16[128,256]{1,0:T(8,128)(2,1)S(1)}, bf16[128,256]{1,0:T(8,128)(2,1)S(1)}, u32[]{:S(2)}, u32[]{:S(2)}) collective-permute-start(bf16[128,256]{1,0:T(8,128)(2,1)S(1)} %convert_element_type.24), channel_id=1, source_target_pairs={{0,32},{16,48},{32,0},{48,16},{64,96},{80,112},{96,64},{112,80},{1... | collective-permute-start | bytes 196616 | tf_op jit(solution)/shard_map/ppermute | solution.py:11
  63.5 4.2 %all-to-all-done.1.grads = bf16[16,224,128]{2,1,0:T(8,128)(2,1)S(1)} async-done(((bf16[16,224,128]{2,1,0:T(8,128)(2,1)}), bf16[16,224,128]{2,1,0:T(8,128)(2,1)S(1)}, u32[]{:S(2)}, u32[]{:S(2)}) %all-to-all-start.1) | async-done | bytes 917536 | tf_op jit(solution)/shard_map/all_to_all | solution.py:211
  67.7 0.0 copy-start.2
  67.7 1.0 copy-done.2
  68.7 0.5 shard_map.122
  69.2 2.7 %collective-permute-start.3 = (bf16[128,128]{1,0:T(8,128)(2,1)S(1)}, bf16[128,128]{1,0:T(8,128)(2,1)S(1)}, u32[]{:S(2)}, u32[]{:S(2)}) collective-permute-start(bf16[128,128]{1,0:T(8,128)(2,1)S(1)} %get-tuple-element.43), channel_id=1, source_target_pairs={{0,32},{16,48},{32,0},{48,16},{64,96},{80,112},{96,64},{112,80},{1... | collective-permute-start | bytes 98312 | tf_op jit(solution)/shard_map/ppermute | solution.py:11
  71.9 1.0 broadcast_select_fusion
  72.9 0.0 collective-permute-done.2.other_pre
  72.9 2.1 %collective-permute-done.3.other = bf16[128,128]{1,0:T(8,128)(2,1)S(1)} collective-permute-done((bf16[128,128]{1,0:T(8,128)(2,1)S(1)}, bf16[128,128]{1,0:T(8,128)(2,1)S(1)}, u32[]{:S(2)}, u32[]{:S(2)}) %collective-permute-start.3) | collective-permute-done | bytes 32800 | tf_op jit(solution)/shard_map/ppermute | solution.py:11
  75.1 0.0 collective-permute-done.4
  75.1 1.7 %shard_map.123 = (bf16[128,384]{1,0:T(8,128)(2,1)S(1)}, bf16[16,224,128]{2,1,0:T(8,128)(2,1)}) custom-call(s32[1]{0:T(128)} %bitcast.core, f32[128,256]{1,0:T(8,128)S(1)} %convert_add_fusion.pre, bf16[128,256]{1,0:T(8,128)(2,1)S(1)} %collective-permute-done.2.other_pre, f32[128,128]{1,0:T(8,128)S(1)} %get-tuple-element.42.part, ...), custom_call_target="tpu_custom_call" | custom-call | bytes 3145732 | tf_op jit(solution)/shard_map/pallas_call | solution.py:24
  76.8 0.0 copy-start.9
  76.8 0.0 copy-start.6
  76.8 3.8 %all-to-all-start.2 = ((bf16[16,224,128]{2,1,0:T(8,128)(2,1)}), bf16[16,224,128]{2,1,0:T(8,128)(2,1)S(1)}, u32[]{:S(2)}, u32[]{:S(2)}) async-start(bf16[16,224,128]{2,1,0:T(8,128)(2,1)} %get-tuple-element.47), calls=%async_computation.2 | async-start | bytes 1835008 | tf_op jit(solution)/shard_map/all_to_all | solution.py:244
  80.5 0.0 copy-done.9
  80.5 1.9 %collective-permute-start.6 = (bf16[1792,128]{1,0:T(8,128)(2,1)S(1)}, bf16[1792,128]{1,0:T(8,128)(2,1)S(1)}, u32[]{:S(2)}, u32[]{:S(2)}) collective-permute-start(bf16[1792,128]{1,0:T(8,128)(2,1)S(1)} %bitcast.39), channel_id=1, source_target_pairs={{0,16},{16,0},{32,48},{48,32},{64,80},{80,64},{96,112},{112,96},{1... | collective-permute-start | bytes 1376264 | tf_op jit(solution)/shard_map/ppermute | solution.py:11
  82.5 2.4 %collective-permute-start.5 = (bf16[128,384]{1,0:T(8,128)(2,1)S(1)}, bf16[128,384]{1,0:T(8,128)(2,1)S(1)}, u32[]{:S(2)}, u32[]{:S(2)}) collective-permute-start(bf16[128,384]{1,0:T(8,128)(2,1)S(1)} %get-tuple-element.48), channel_id=1, source_target_pairs={{0,16},{16,0},{32,48},{48,32},{64,80},{80,64},{96,112},{112,96},{1... | collective-permute-start | bytes 294920 | tf_op jit(solution)/shard_map/ppermute | solution.py:11
  84.9 0.0 copy-done.6
  84.9 0.3 fusion.4
  85.2 9.3 %all-to-all-done.2.refs_0_ = bf16[16,224,128]{2,1,0:T(8,128)(2,1)S(1)} async-done(((bf16[16,224,128]{2,1,0:T(8,128)(2,1)}), bf16[16,224,128]{2,1,0:T(8,128)(2,1)S(1)}, u32[]{:S(2)}, u32[]{:S(2)}) %all-to-all-start.2) | async-done | bytes 917536 | tf_op jit(solution)/shard_map/all_to_all | solution.py:244
  94.5 1.0 shard_map.124
  95.4 0.0 copy-start.5
  95.4 0.0 collective-permute-done.5
  95.4 0.0 collective-permute-done.6
  95.4 22.8 %all-to-all-start.3 = ((bf16[32,8,112]{2,1,0:T(8,128)(2,1)}), bf16[32,8,112]{2,1,0:T(8,128)(2,1)S(1)}, u32[]{:S(2)}, u32[]{:S(2)}) async-start(bf16[32,8,112]{2,1,0:T(8,128)(2,1)} %bitcast.15), calls=%async_computation.3 | async-start | bytes 131072 | tf_op jit(solution)/shard_map/all_to_all | solution.py:175
  118.3 0.1 pad_maximum_fusion
  118.4 0.1 reshape.80
  118.5 0.0 copy-done.5
  118.5 1.2 convolution_convert_fusion
  119.7 1.2 convolution_convert_fusion.1
  121.0 0.0 copy-start.3
  121.0 1.0 fusion
  122.0 2.0 %all-to-all-done.3 = bf16[32,8,112]{2,1,0:T(8,128)(2,1)S(1)} async-done(((bf16[32,8,112]{2,1,0:T(8,128)(2,1)}), bf16[32,8,112]{2,1,0:T(8,128)(2,1)S(1)}, u32[]{:S(2)}, u32[]{:S(2)}) %all-to-all-start.3) | async-done | bytes 57376 | tf_op jit(solution)/shard_map/all_to_all | solution.py:175
  124.0 0.0 copy-done.3
  124.0 0.9 shard_map.125
  (10 shorter events, 0.3 us)
Async XLA Ops:
  2.6 41.7 %all-to-all-start = ((bf16[32,8,112]{2,1,0:T(8,128)(2,1)}), bf16[32,8,112]{2,1,0:T(8,128)(2,1)S(1)}, u32[]{:S(2)}, u32[]{:S(2)}) async-start(bf16[32,8,112]{2,1,0:T(8,128)(2,1)} %bitcast.44), calls=%async_computation | async-start | bytes 131072 | tf_op jit(solution)/shard_map/all_to_all | solution.py:175
  37.1 1.7 %copy-start.7 = (bf16[1792,128]{1,0:T(8,128)(2,1)S(1)}, bf16[1792,128]{1,0:T(8,128)(2,1)}, u32[]{:S(2)}) copy-start(bf16[1792,128]{1,0:T(8,128)(2,1)} %param.15) | copy-start | bytes 1376260
  38.8 1.5 %copy-start.4 = (bf16[256,1792]{1,0:T(8,128)(2,1)}, bf16[256,1792]{1,0:T(8,128)(2,1)S(1)}, u32[]{:S(2)}) copy-start(bf16[256,1792]{1,0:T(8,128)(2,1)S(1)} %reshape.71) | copy-start | bytes 2752516
  38.9 1.4 %copy-start.8 = (bf16[1792,128]{1,0:T(8,128)(2,1)S(1)}, bf16[1792,128]{1,0:T(8,128)(2,1)}, u32[]{:S(2)}) copy-start(bf16[1792,128]{1,0:T(8,128)(2,1)} %param.16) | copy-start | bytes 1376260
  45.5 9.1 %copy-start = (bf16[1792,128]{1,0:T(8,128)(2,1)S(1)}, bf16[1792,128]{1,0:T(8,128)(2,1)}, u32[]{:S(2)}) copy-start(bf16[1792,128]{1,0:T(8,128)(2,1)} %param.17) | copy-start | bytes 1376260
  45.5 22.2 %all-to-all-start.1 = ((bf16[16,224,128]{2,1,0:T(8,128)(2,1)}), bf16[16,224,128]{2,1,0:T(8,128)(2,1)S(1)}, u32[]{:S(2)}, u32[]{:S(2)}) async-start(bf16[16,224,128]{2,1,0:T(8,128)(2,1)} %shard_map.121), calls=%async_computation.1 | async-start | bytes 1835008 | tf_op jit(solution)/shard_map/all_to_all | solution.py:211
  52.7 22.4 %collective-permute-start.4 = (bf16[1792,256]{1,0:T(8,128)(2,1)S(1)}, bf16[1792,256]{1,0:T(8,128)(2,1)S(1)}, u32[]{:S(2)}, u32[]{:S(2)}) collective-permute-start(bf16[1792,256]{1,0:T(8,128)(2,1)S(1)} %constant_dynamic-update-slice_fusion), channel_id=1, source_target_pairs={{0,16},{16,0},{32,48},{48,32},{64,80},{80,64},{96,112},{112,96},{1... | collective-permute-start | bytes 2752520 | tf_op jit(solution)/shard_map/ppermute | solution.py:11
  54.6 5.6 %collective-permute-start = (bf16[1792,128]{1,0:T(8,128)(2,1)S(1)}, bf16[1792,128]{1,0:T(8,128)(2,1)S(1)}, u32[]{:S(2)}, u32[]{:S(2)}) collective-permute-start(bf16[1792,128]{1,0:T(8,128)(2,1)S(1)} %copy-done), channel_id=1, source_target_pairs={{0,16},{16,0},{32,48},{48,32},{64,80},{80,64},{96,112},{112,96},{1... | collective-permute-start | bytes 1376264 | tf_op jit(solution)/shard_map/ppermute | solution.py:11
  57.1 3.1 %collective-permute-start.1 = (bf16[128,256]{1,0:T(8,128)(2,1)S(1)}, bf16[128,256]{1,0:T(8,128)(2,1)S(1)}, u32[]{:S(2)}, u32[]{:S(2)}) collective-permute-start(bf16[128,256]{1,0:T(8,128)(2,1)S(1)} %convert_element_type.22), channel_id=1, source_target_pairs={{0,16},{16,0},{32,48},{48,32},{64,80},{80,64},{96,112},{112,96},{1... | collective-permute-start | bytes 196616 | tf_op jit(solution)/shard_map/ppermute | solution.py:11
  60.2 0.8 copy-start.1
  61.0 11.9 %collective-permute-start.2 = (bf16[128,256]{1,0:T(8,128)(2,1)S(1)}, bf16[128,256]{1,0:T(8,128)(2,1)S(1)}, u32[]{:S(2)}, u32[]{:S(2)}) collective-permute-start(bf16[128,256]{1,0:T(8,128)(2,1)S(1)} %convert_element_type.24), channel_id=1, source_target_pairs={{0,32},{16,48},{32,0},{48,16},{64,96},{80,112},{96,64},{112,80},{1... | collective-permute-start | bytes 196616 | tf_op jit(solution)/shard_map/ppermute | solution.py:11
  67.7 1.0 copy-start.2
  69.2 5.8 %collective-permute-start.3 = (bf16[128,128]{1,0:T(8,128)(2,1)S(1)}, bf16[128,128]{1,0:T(8,128)(2,1)S(1)}, u32[]{:S(2)}, u32[]{:S(2)}) collective-permute-start(bf16[128,128]{1,0:T(8,128)(2,1)S(1)} %get-tuple-element.43), channel_id=1, source_target_pairs={{0,32},{16,48},{32,0},{48,16},{64,96},{80,112},{96,64},{112,80},{1... | collective-permute-start | bytes 98312 | tf_op jit(solution)/shard_map/ppermute | solution.py:11
  76.8 3.8 %copy-start.9 = (bf16[16,1,112,128]{3,2,1,0:T(8,128)(2,1)S(1)}, bf16[16,1,112,128]{3,2,1,0:T(8,128)(2,1)}, u32[]{:S(2)}) copy-start(bf16[16,1,112,128]{3,2,1,0:T(8,128)(2,1)} %get-tuple-element.55) | copy-start | bytes 1376260
  76.8 8.1 %copy-start.6 = (bf16[16,1,112,128]{3,2,1,0:T(8,128)(2,1)S(1)}, bf16[16,1,112,128]{3,2,1,0:T(8,128)(2,1)}, u32[]{:S(2)}) copy-start(bf16[16,1,112,128]{3,2,1,0:T(8,128)(2,1)} %get-tuple-element.54) | copy-start | bytes 1376260
  76.8 17.7 %all-to-all-start.2 = ((bf16[16,224,128]{2,1,0:T(8,128)(2,1)}), bf16[16,224,128]{2,1,0:T(8,128)(2,1)S(1)}, u32[]{:S(2)}, u32[]{:S(2)}) async-start(bf16[16,224,128]{2,1,0:T(8,128)(2,1)} %get-tuple-element.47), calls=%async_computation.2 | async-start | bytes 1835008 | tf_op jit(solution)/shard_map/all_to_all | solution.py:244
  80.5 14.9 %collective-permute-start.6 = (bf16[1792,128]{1,0:T(8,128)(2,1)S(1)}, bf16[1792,128]{1,0:T(8,128)(2,1)S(1)}, u32[]{:S(2)}, u32[]{:S(2)}) collective-permute-start(bf16[1792,128]{1,0:T(8,128)(2,1)S(1)} %bitcast.39), channel_id=1, source_target_pairs={{0,16},{16,0},{32,48},{48,32},{64,80},{80,64},{96,112},{112,96},{1... | collective-permute-start | bytes 1376264 | tf_op jit(solution)/shard_map/ppermute | solution.py:11
  82.5 12.9 %collective-permute-start.5 = (bf16[128,384]{1,0:T(8,128)(2,1)S(1)}, bf16[128,384]{1,0:T(8,128)(2,1)S(1)}, u32[]{:S(2)}, u32[]{:S(2)}) collective-permute-start(bf16[128,384]{1,0:T(8,128)(2,1)S(1)} %get-tuple-element.48), channel_id=1, source_target_pairs={{0,16},{16,0},{32,48},{48,32},{64,80},{80,64},{96,112},{112,96},{1... | collective-permute-start | bytes 294920 | tf_op jit(solution)/shard_map/ppermute | solution.py:11
  95.4 23.1 %copy-start.5 = (bf16[256,1792]{1,0:T(8,128)(2,1)S(1)}, bf16[256,1792]{1,0:T(8,128)(2,1)}, u32[]{:S(2)}) copy-start(bf16[256,1792]{1,0:T(8,128)(2,1)} %copy-done.4) | copy-start | bytes 2752516
  95.4 28.6 %all-to-all-start.3 = ((bf16[32,8,112]{2,1,0:T(8,128)(2,1)}), bf16[32,8,112]{2,1,0:T(8,128)(2,1)S(1)}, u32[]{:S(2)}, u32[]{:S(2)}) async-start(bf16[32,8,112]{2,1,0:T(8,128)(2,1)} %bitcast.15), calls=%async_computation.3 | async-start | bytes 131072 | tf_op jit(solution)/shard_map/all_to_all | solution.py:175
  121.0 3.1 %copy-start.3 = (bf16[256,128]{1,0:T(8,128)(2,1)S(1)}, bf16[256,128]{1,0:T(8,128)(2,1)}, u32[]{:S(2)}) copy-start(bf16[256,128]{1,0:T(8,128)(2,1)} %get-tuple-element.51.refs_1_) | copy-start | bytes 196612
